TPU v7x, 32 devices: a whole 2x2x4 slice. The times are simulated.
32 devices in a mesh: section: 2 (over x), seq: 4 (over z), mp: 4 (over y, core).
Axes of the slice: x: 2, y: 2, z: 4, core: 2. Of those that a mesh axis runs over, the one named last changes fastest.
Arguments:
- inputs: bfloat16 [6, 768, 2048], P(None, 'mp', 'seq'), may hold values from -6 to 6
- cotangent: bfloat16 [6, 768, 2048], P(None, 'mp', 'seq'), may hold values from -6 to 6
- labels: int32 [6, 2048], P(None, 'seq'), may hold values from 0 to 767
- scored: int32 [6, 2048], P(None, 'seq'), may hold values 0 or 1
- expand_weight: bfloat16 [2, 3072, 768], P('section', 'mp'), may hold values from -0.21875 to 0.21875
- expand_bias: float32 [2, 3072], P('section', 'mp'), may hold values from -3 to 3
- reduce_weight: bfloat16 [2, 768, 3072], P('section', None, 'mp'), may hold values from -0.1875 to 0.1875
- reduce_bias: float32 [2, 768], P('section', 'mp'), may hold values from -2 to 2
- first_gain: float32 [2, 768], P('section', 'mp'), may hold values from 0.5 to 1.5
- first_shift: float32 [2, 768], P('section', 'mp'), may hold values from -2 to 2
- second_gain: float32 [2, 768], P('section', 'mp'), may hold values from 0.5 to 1.5
- second_shift: float32 [2, 768], P('section', 'mp'), may hold values from -2 to 2
Outputs:
- outputs: float32 [2, 6, 768, 2048], P('section', None, 'mp', 'seq')
- input_grads: float32 [2, 6, 768, 2048], P('section', None, 'mp', 'seq')
- expand_weight_grad: float32 [2, 3072, 768], P('section', 'mp')
- expand_bias_grad: float32 [2, 3072], P('section', 'mp')
- reduce_weight_grad: float32 [2, 768, 3072], P('section', None, 'mp')
- reduce_bias_grad: float32 [2, 768], P('section', 'mp')
- first_gain_grad: float32 [2, 768], P('section', 'mp')
- first_shift_grad: float32 [2, 768], P('section', 'mp')
- second_gain_grad: float32 [2, 768], P('section', 'mp')
- second_shift_grad: float32 [2, 768], P('section', 'mp')
- accuracy: float32 [], replicated
All inputs are finite; a program needn't handle non-finite values. No bound on the sum of `scored` on one device may be relied on, other than what follows from the above.
Results may differ from a plain program's by a relative error of at most 0.02.
Values may be sent and summed in bfloat16 or wider, within the bound.
No kernel may reach another device: no remote copies, remote signals or barrier semaphores. Data moves between devices by JAX's collectives and lax.ppermute only.
A program may use at most 256 MiB of HBM per device.

v0:
```python
import math

import jax
import jax.numpy as jnp
from jax import lax
from jax.sharding import PartitionSpec as P

EPSILON = 1e-05


def shifted(array, axis, by):
    size = lax.axis_size(axis)
    pairs = [(i, i + by) for i in range(size) if 0 <= i + by < size]
    return lax.ppermute(array, axis, pairs)


def trig_block(row_ids, column_ids, points):
    phases = row_ids[:, None] * column_ids[None, :] % points
    angles = phases.astype(jnp.float32) * (2.0 * math.pi / points)
    return (jnp.cos(angles).astype(jnp.bfloat16), jnp.sin(angles).astype(jnp.bfloat16))


def row_totals(first_rows, second_rows):
    return lax.psum((first_rows, second_rows), "mp")


def norm_forward(values, scaling, offsets, width):
    row_total, square = row_totals(jnp.sum(values, axis=0), jnp.sum(values * values, axis=0))
    average = row_total / width
    spread = jnp.maximum(square / width - average * average, 0.0)
    inverse = lax.rsqrt(spread + EPSILON)
    standard = (values - average[None, :]) * inverse[None, :]
    return (standard * scaling[:, None] + offsets[:, None], standard, inverse)


def norm_backward(upstream, standard, inverse, scaling, width):
    weighted = upstream * scaling[:, None]
    plain_sum, cross_sum = row_totals(
        jnp.sum(weighted, axis=0), jnp.sum(weighted * standard, axis=0)
    )
    grad_values = inverse[None, :] * (
        weighted - plain_sum[None, :] / width - standard * (cross_sum[None, :] / width)
    )
    return (grad_values, jnp.sum(upstream * standard, axis=1), jnp.sum(upstream, axis=1))


def gelu_slope(values):
    cumulative = 0.5 * (1.0 + lax.erf(values * (1.0 / math.sqrt(2.0))))
    density = jnp.exp(-0.5 * values * values) * (1.0 / math.sqrt(2.0 * math.pi))
    return cumulative + values * density


def contract_first(left, right):
    return lax.dot_general(
        left, right, (((0,), (0,)), ((), ())), preferred_element_type=jnp.float32
    )


def contract_last(left, right):
    return lax.dot_general(
        left, right, (((1,), (1,)), ((), ())), preferred_element_type=jnp.float32
    )


def shards(
    inputs,
    cotangent,
    labels,
    scored,
    expand_weight,
    expand_bias,
    reduce_weight,
    reduce_bias,
    first_gain,
    first_shift,
    second_gain,
    second_shift,
):
    batches = inputs.shape[0]
    feature_count = inputs.shape[1]
    token_count = inputs.shape[2]
    width = feature_count * lax.axis_size("mp")
    length = token_count * lax.axis_size("seq")
    factor = 1.0 / math.sqrt(length * width)
    mp_index = lax.axis_index("mp")
    seq_index = lax.axis_index("seq")
    is_first = lax.axis_index("section") == 0
    token_ids = seq_index * token_count + jnp.arange(token_count, dtype=jnp.int32)
    token_cos, token_sin = trig_block(jnp.arange(length, dtype=jnp.int32), token_ids, length)
    all_features = jnp.arange(width, dtype=jnp.int32)
    feature_ids = mp_index * feature_count + jnp.arange(feature_count, dtype=jnp.int32)
    feature_cos, feature_sin = trig_block(feature_ids, all_features, width)
    expand_mat = expand_weight[0]
    expand_vec = expand_bias[0]
    reduce_mat = reduce_weight[0]
    reduce_vec = reduce_bias[0]
    gain_first = first_gain[0]
    shift_first = first_shift[0]
    gain_second = second_gain[0]
    shift_second = second_shift[0]
    empty_rows = jnp.zeros((feature_count, token_count), jnp.float32)

    def gather_rows(values):
        return lax.all_gather(values, "mp", axis=0, tiled=True)

    received = jnp.zeros((feature_count, token_count), jnp.bfloat16)
    forward_results = []
    saved_state = []
    for period in range(batches + 1):
        source = jnp.where(is_first, inputs[min(period, batches - 1)], received)
        gather_pieces = lax.all_gather(source, "mp", axis=0, tiled=True)
        feature_cos_mixed = jnp.dot(feature_cos, gather_pieces, preferred_element_type=jnp.float32)
        feature_sin_mixed = jnp.dot(feature_sin, gather_pieces, preferred_element_type=jnp.float32)
        layer_cos_mixed = feature_cos_mixed.astype(jnp.bfloat16)
        layer_sin_mixed = feature_sin_mixed.astype(jnp.bfloat16)
        token_mixed = jnp.dot(
            lax.all_gather(layer_cos_mixed, "seq", axis=1, tiled=True),
            token_cos,
            preferred_element_type=jnp.float32,
        ) - jnp.dot(
            lax.all_gather(layer_sin_mixed, "seq", axis=1, tiled=True),
            token_sin,
            preferred_element_type=jnp.float32,
        )
        layer_token_mixed = token_mixed * factor
        normed, layer_standard_one, layer_inverse_one = norm_forward(
            source.astype(jnp.float32) + layer_token_mixed, gain_first, shift_first, width
        )
        layer_normed_full = gather_rows(normed.astype(jnp.bfloat16))
        layer_hidden_pre = (
            jnp.dot(expand_mat, layer_normed_full, preferred_element_type=jnp.float32)
            + expand_vec[:, None]
        )
        layer_active = jax.nn.gelu(layer_hidden_pre, approximate=False).astype(jnp.bfloat16)
        branch = lax.psum_scatter(
            jnp.dot(reduce_mat, layer_active, preferred_element_type=jnp.float32).astype(
                jnp.bfloat16
            ),
            "mp",
            scatter_dimension=0,
            tiled=True,
        ).astype(jnp.float32)
        result, layer_standard_two, layer_inverse_two = norm_forward(
            normed + branch + reduce_vec[:, None], gain_second, shift_second, width
        )
        result, kept = (
            result,
            (
                layer_normed_full,
                layer_hidden_pre,
                layer_active,
                layer_standard_one,
                layer_inverse_one,
                layer_standard_two,
                layer_inverse_two,
            ),
        )
        forward_results.append(result)
        saved_state.append(kept)
        if period < batches:
            received = shifted(result.astype(jnp.bfloat16), "section", 1)
    all_results = jnp.stack(forward_results)
    own_outputs = jnp.where(is_first, all_results[:batches], all_results[1:])
    exponent = jnp.exp(own_outputs)
    local_labels = labels - mp_index * feature_count
    matches = jnp.arange(feature_count, dtype=jnp.int32)[None, :, None] == local_labels[:, None, :]
    total_exp, label_exp = row_totals(
        jnp.sum(exponent, axis=1), jnp.sum(jnp.where(matches, exponent, 0.0), axis=1)
    )
    local_count = jnp.sum(label_exp / total_exp * scored.astype(jnp.float32))
    accuracy = lax.psum(local_count, ("section", "seq"))
    received = jnp.zeros((feature_count, token_count), jnp.bfloat16)
    back_results = []
    totals = None
    for period in range(batches + 1):
        if period < batches:
            seed_grad = cotangent[batches - 1 - period].astype(jnp.float32)
        else:
            seed_grad = jnp.zeros((feature_count, token_count), jnp.float32)
        upstream = jnp.where(is_first, received.astype(jnp.float32), seed_grad)
        normed_full, hidden_pre, active, standard_one, inverse_one, standard_two, inverse_two = (
            saved_state[batches - period]
        )
        grad_second, gain_second_grad, shift_second_grad = norm_backward(
            upstream, standard_two, inverse_two, gain_second, width
        )
        branch_full = gather_rows(grad_second.astype(jnp.bfloat16))
        grad_active = contract_first(reduce_mat, branch_full)
        reduce_mat_grad = contract_last(branch_full, active)
        grad_pre = (grad_active * gelu_slope(hidden_pre)).astype(jnp.bfloat16)
        expand_mat_grad = contract_last(grad_pre, normed_full)
        grad_normed = grad_second + lax.psum_scatter(
            contract_first(expand_mat, grad_pre).astype(jnp.bfloat16),
            "mp",
            scatter_dimension=0,
            tiled=True,
        ).astype(jnp.float32)
        grad_first, gain_first_grad, shift_first_grad = norm_backward(
            grad_normed, standard_one, inverse_one, gain_first, width
        )
        back_pieces = lax.all_gather(grad_first.astype(jnp.bfloat16), "seq", axis=1, tiled=True)
        token_grad_cos = jnp.dot(back_pieces, token_cos, preferred_element_type=jnp.float32)
        token_grad_sin = (empty_rows, empty_rows)[1] - jnp.dot(
            back_pieces, token_sin, preferred_element_type=jnp.float32
        )
        layer_grad_cos = (token_grad_cos * factor).astype(jnp.bfloat16)
        layer_grad_sin = (token_grad_sin * factor).astype(jnp.bfloat16)
        grad_source = grad_first + (
            jnp.dot(
                feature_cos,
                lax.all_gather(layer_grad_cos, "mp", axis=0, tiled=True),
                preferred_element_type=jnp.float32,
            )
            + jnp.dot(
                feature_sin,
                lax.all_gather(layer_grad_sin, "mp", axis=0, tiled=True),
                preferred_element_type=jnp.float32,
            )
        )
        grads = (
            expand_mat_grad,
            jnp.sum(grad_pre.astype(jnp.float32), axis=1),
            reduce_mat_grad,
            jnp.sum(grad_second, axis=1),
            gain_first_grad,
            shift_first_grad,
            gain_second_grad,
            shift_second_grad,
        )
        grad_source, grads = (grad_source, grads)
        back_results.append(grad_source)
        totals = grads if totals is None else jax.tree.map(jnp.add, totals, grads)
        if period < batches:
            received = shifted(grad_source.astype(jnp.bfloat16), "section", -1)
    all_grads = jnp.stack(back_results)
    own_grads = jnp.where(is_first, all_grads[1:][::-1], all_grads[:batches][::-1])
    summed = (
        lax.psum(totals[0].astype(jnp.bfloat16), "seq").astype(jnp.float32),
        lax.psum(totals[1].astype(jnp.bfloat16), "seq").astype(jnp.float32),
        lax.psum(totals[2].astype(jnp.bfloat16), "seq").astype(jnp.float32),
        lax.psum(totals[3].astype(jnp.bfloat16), "seq").astype(jnp.float32),
        lax.psum(totals[4].astype(jnp.bfloat16), "seq").astype(jnp.float32),
        lax.psum(totals[5].astype(jnp.bfloat16), "seq").astype(jnp.float32),
        lax.psum(totals[6].astype(jnp.bfloat16), "seq").astype(jnp.float32),
        lax.psum(totals[7].astype(jnp.bfloat16), "seq").astype(jnp.float32),
    )
    return (
        own_outputs[None],
        own_grads[None],
        summed[0][None],
        summed[1][None],
        summed[2][None],
        summed[3][None],
        summed[4][None],
        summed[5][None],
        summed[6][None],
        summed[7][None],
        accuracy,
    )


def solution(mesh):
    placed = (
        P(None, "mp", "seq"),
        P(None, "mp", "seq"),
        P(None, "seq"),
        P(None, "seq"),
        P("section", "mp", None),
        P("section", "mp"),
        P("section", None, "mp"),
        P("section", "mp"),
        P("section", "mp"),
        P("section", "mp"),
        P("section", "mp"),
        P("section", "mp"),
    )
    return jax.shard_map(
        shards,
        mesh=mesh,
        in_specs=placed,
        out_specs=(
            P("section", None, "mp", "seq"),
            P("section", None, "mp", "seq"),
            P("section", "mp", None),
            P("section", "mp"),
            P("section", None, "mp"),
            P("section", "mp"),
            P("section", "mp"),
            P("section", "mp"),
            P("section", "mp"),
            P("section", "mp"),
            P(),
        ),
        check_vma=False,
    )
```

profile of v0, /device:TPU:0, one launch (start us, length us, event | category | flops | bytes accessed | tf_op | source)
XLA Modules:
  0.0 2043.4 jit_solution(5949460970578623905)
XLA Ops:
  24.0 19.8 all_gather.169
  116.1 22.4 %reduce-scatter.15.cloned.1.call-done = bf16[192,512]{1,0:T(8,128)(2,1)} async-done(((bf16[768,512]{1,0:T(8,128)(2,1)}), bf16[192,512]{1,0:T(8,128)(2,1)}) %reduce-scatter.15.cloned.1.call-update) | async-done | bytes 196624 | tf_op jit(solution)/shard_map/reduce_scatter | solution.py:135
  166.9 19.5 all_gather.173
  258.9 22.9 %reduce-scatter.17.cloned.1.call-done = bf16[192,512]{1,0:T(8,128)(2,1)} async-done(((bf16[768,512]{1,0:T(8,128)(2,1)}), bf16[192,512]{1,0:T(8,128)(2,1)}) %reduce-scatter.17.cloned.1.call-update) | async-done | bytes 196624 | tf_op jit(solution)/shard_map/reduce_scatter | solution.py:135
  310.6 19.5 all_gather.177
  402.4 23.1 %reduce-scatter.19.cloned.1.call-done = bf16[192,512]{1,0:T(8,128)(2,1)} async-done(((bf16[768,512]{1,0:T(8,128)(2,1)}), bf16[192,512]{1,0:T(8,128)(2,1)}) %reduce-scatter.19.cloned.1.call-update) | async-done | bytes 196624 | tf_op jit(solution)/shard_map/reduce_scatter | solution.py:135
  453.6 19.5 all_gather.181
  488.8 18.6 all_gather.182
  546.0 23.2 %reduce-scatter.21.cloned.1.call-done = bf16[192,512]{1,0:T(8,128)(2,1)} async-done(((bf16[768,512]{1,0:T(8,128)(2,1)}), bf16[192,512]{1,0:T(8,128)(2,1)}) %reduce-scatter.21.cloned.1.call-update) | async-done | bytes 196624 | tf_op jit(solution)/shard_map/reduce_scatter | solution.py:135
  599.2 19.5 all_gather.185
  690.2 22.9 %reduce-scatter.23.cloned.1.call-done = bf16[192,512]{1,0:T(8,128)(2,1)} async-done(((bf16[768,512]{1,0:T(8,128)(2,1)}), bf16[192,512]{1,0:T(8,128)(2,1)}) %reduce-scatter.23.cloned.1.call-update) | async-done | bytes 196624 | tf_op jit(solution)/shard_map/reduce_scatter | solution.py:135
  743.4 19.5 all_gather.189
  835.1 23.1 %reduce-scatter.25.cloned.1.call-done = bf16[192,512]{1,0:T(8,128)(2,1)} async-done(((bf16[768,512]{1,0:T(8,128)(2,1)}), bf16[192,512]{1,0:T(8,128)(2,1)}) %reduce-scatter.25.cloned.1.call-update) | async-done | bytes 196624 | tf_op jit(solution)/shard_map/reduce_scatter | solution.py:135
  888.5 19.5 all_gather.193
  983.6 23.1 %reduce-scatter.27.cloned.1.call-done = bf16[192,512]{1,0:T(8,128)(2,1)} async-done(((bf16[768,512]{1,0:T(8,128)(2,1)}), bf16[192,512]{1,0:T(8,128)(2,1)}) %reduce-scatter.27.cloned.1.call-update) | async-done | bytes 196624 | tf_op jit(solution)/shard_map/reduce_scatter | solution.py:135
  1041.2 23.9 %reduce-scatter.29.cloned.1.call-done = bf16[192,512]{1,0:T(8,128)(2,1)} async-done(((bf16[768,512]{1,0:T(8,128)(2,1)}), bf16[192,512]{1,0:T(8,128)(2,1)}) %reduce-scatter.29.cloned.1.call-update) | async-done | bytes 196624 | tf_op jit(solution)/shard_map/reduce_scatter | solution.py:192
  1076.2 19.8 all_gather.197
  1217.5 19.8 all_gather.201
  1358.7 19.8 all_gather.205
  1500.4 19.9 all_gather.209
  1637.5 19.8 all_gather.213
  1774.6 19.8 all_gather.217
  1913.3 22.9 %psum.535 = f32[]{:T(128)} all-reduce(f32[]{:T(128)} %multiply_reduce_fusion.48), channel_id=1, replica_groups=mesh['section'=2,'seq'=4,'mp'=4] {'section','seq'}, use_global_device_ids=true, to_apply=%region_181.182 | all-reduce | flops 1 | bytes 8 | tf_op jit(solution)/shard_map/psum | solution.py:171
  1949.8 25.7 %all_gather.221 = bf16[192,2048]{1,0:T(8,128)(2,1)S(1)} all-gather(bf16[192,512]{1,0:T(8,128)(2,1)S(1)} %fusion.544), channel_id=1, replica_groups=mesh['section'=2,'seq'=4,'mp'=4] {'seq'}, dimensions={1}, use_global_device_ids=true | all-gather | bytes 983040 | tf_op jit(solution)/shard_map/all_gather | solution.py:201
  (908 shorter events, 1519.2 us)
Async XLA Ops:
  7.2 131.3 %reduce-scatter.15.cloned.1.call-start = ((), (), s32[]{:S(2)}) async-start(), calls=%async_computation.14 | async-start | bytes 983040 | tf_op jit(solution)/shard_map/reduce_scatter | solution.py:135
  116.1 165.7 %reduce-scatter.17.cloned.1.call-start = ((), (), s32[]{:S(2)}) async-start(), calls=%async_computation.15 | async-start | bytes 983040 | tf_op jit(solution)/shard_map/reduce_scatter | solution.py:135
  145.8 7.5 collective-permute-start
  258.4 167.1 %reduce-scatter.19.cloned.1.call-start = ((), (), s32[]{:S(2)}) async-start(), calls=%async_computation.16 | async-start | bytes 983040 | tf_op jit(solution)/shard_map/reduce_scatter | solution.py:135
  288.9 7.5 collective-permute-start.1
  402.1 167.1 %reduce-scatter.21.cloned.1.call-start = ((), (), s32[]{:S(2)}) async-start(), calls=%async_computation.17 | async-start | bytes 983040 | tf_op jit(solution)/shard_map/reduce_scatter | solution.py:135
  545.8 167.3 %reduce-scatter.23.cloned.1.call-start = ((), (), s32[]{:S(2)}) async-start(), calls=%async_computation.18 | async-start | bytes 983040 | tf_op jit(solution)/shard_map/reduce_scatter | solution.py:135
  689.8 168.5 %reduce-scatter.25.cloned.1.call-start = ((), (), s32[]{:S(2)}) async-start(), calls=%async_computation.19 | async-start | bytes 983040 | tf_op jit(solution)/shard_map/reduce_scatter | solution.py:135
  720.8 7.5 collective-permute-start.4
  834.9 171.8 %reduce-scatter.27.cloned.1.call-start = ((), (), s32[]{:S(2)}) async-start(), calls=%async_computation.20 | async-start | bytes 983040 | tf_op jit(solution)/shard_map/reduce_scatter | solution.py:135
  983.3 81.7 %reduce-scatter.29.cloned.1.call-start = ((), (), s32[]{:S(2)}) async-start(), calls=%async_computation.21 | async-start | bytes 983040 | tf_op jit(solution)/shard_map/reduce_scatter | solution.py:192
  1041.2 167.0 %reduce-scatter.31.cloned.1.call-start = ((), (), s32[]{:S(2)}) async-start(), calls=%async_computation.22 | async-start | bytes 983040 | tf_op jit(solution)/shard_map/reduce_scatter | solution.py:192
  1151.7 9.0 collective-permute-start.6
  1186.4 160.6 %reduce-scatter.33.cloned.1.call-start = ((), (), s32[]{:S(2)}) async-start(), calls=%async_computation.23 | async-start | bytes 983040 | tf_op jit(solution)/shard_map/reduce_scatter | solution.py:192
  1293.3 9.2 collective-permute-start.7
  1325.4 165.7 %reduce-scatter.35.cloned.1.call-start = ((), (), s32[]{:S(2)}) async-start(), calls=%async_computation.24 | async-start | bytes 983040 | tf_op jit(solution)/shard_map/reduce_scatter | solution.py:192
  1434.5 9.0 collective-permute-start.8
  1469.3 159.7 %reduce-scatter.37.cloned.1.call-start = ((), (), s32[]{:S(2)}) async-start(), calls=%async_computation.25 | async-start | bytes 983040 | tf_op jit(solution)/shard_map/reduce_scatter | solution.py:192
  1576.1 9.2 collective-permute-start.9
  1607.4 160.1 %reduce-scatter.39.cloned.1.call-start = ((), (), s32[]{:S(2)}) async-start(), calls=%async_computation.26 | async-start | bytes 983040 | tf_op jit(solution)/shard_map/reduce_scatter | solution.py:192
  1713.4 9.1 collective-permute-start.10
  1745.8 154.6 %reduce-scatter.41.cloned.1.call-start = ((), (), s32[]{:S(2)}) async-start(), calls=%async_computation.27 | async-start | bytes 983040 | tf_op jit(solution)/shard_map/reduce_scatter | solution.py:192
  1849.7 9.2 collective-permute-start.11
  1878.7 153.4 %all-reduce.32.cloned.1.call-start = ((), (), s32[]{:S(2)}) async-start(), calls=%async_computation.28 | async-start | bytes 4718592 | tf_op jit(solution)/shard_map/psum | solution.py:238
  (270 other events, 4314.6 us)
Sparse Core Ops, SparseCore 0:
  116.2 22.2 reduce-scatter.14
  258.6 23.2 reduce-scatter.16
  402.2 23.2 reduce-scatter.18
  545.9 23.2 reduce-scatter.20
  689.9 23.1 reduce-scatter.22
  835.0 23.2 reduce-scatter.24
  983.5 23.2 reduce-scatter.26
  1041.3 23.7 reduce-scatter.28
  1186.5 21.5 reduce-scatter.30
  1325.5 21.5 reduce-scatter.32
  1469.4 21.5 reduce-scatter.34
  1607.5 21.5 reduce-scatter.36
  1745.9 21.5 reduce-scatter.38
  1878.9 21.5 reduce-scatter.40
  1913.5 109.5 all-reduce.31
where the time goes:
time: 2050 us; the launch traced here: 2040 us
  blocking collectives  907 us (44%)
  matrix products  649 us (32%)
  waiting for transfers between devices  314 us (15%)
  other arithmetic  101 us (5%)
  starting transfers between devices  31.7 us (2%)
  local copies, waits for them, and re-layouts  24.3 us (1%)
    psum x28, blocking collectives, row_totals(): return lax.psum((first_rows, second_rows), 'mp')  170 us
    reduce_scatter x7, waiting for transfers between devices, shards(): lax.psum_scatter(jnp.dot(reduce_mat, layer_active, preferred_element_type...  161 us
    all_gather x7, blocking collectives, shards(): lax.all_gather(grad_first.astype(jnp.bfloat16), 'seq', axis=1, tiled=True)  145 us
    all_gather x7, blocking collectives, shards(): lax.all_gather(layer_cos_mixed, 'seq', axis=1, tiled=True)  137 us
    all_gather x7, blocking collectives, shards(): lax.all_gather(layer_sin_mixed, 'seq', axis=1, tiled=True)  129 us
    all_gather x14, blocking collectives, gather_rows(): return lax.all_gather(values, 'mp', axis=0, tiled=True)  117 us
    dot_general x7, matrix products, shards(): jnp.dot(back_pieces, token_cos, preferred_element_type=jnp.float32)  114 us
    dot_general x7, matrix products, shards(): jnp.dot(back_pieces, token_sin, preferred_element_type=jnp.float32)  112 us
  transfers between devices with their start and end apart: 27, of which 26 were waited for; matrix products, arithmetic and copies ran while one was open for 5% of the time, Pallas kernels for 0%

commit v1 on v0

v1 whole, which is shorter than its diff:
```python
import math

import jax
import jax.numpy as jnp
import ml_dtypes
import numpy as np
from jax import lax
from jax.experimental import pallas as pl
from jax.experimental.pallas import tpu as pltpu
from jax.sharding import PartitionSpec as P

EPSILON = 1e-05
BF = jnp.bfloat16
F32 = jnp.float32
MIB = 1 << 20


def trig(rows, columns, points):
    phases = (rows.astype(np.int64)[:, None] * columns.astype(np.int64)[None, :]) % points
    angles = phases.astype(np.float64) * (2.0 * math.pi / points)
    return np.cos(angles), np.sin(angles)


def low_table(table):
    return table.astype(np.float32).astype(ml_dtypes.bfloat16)


def feature_tables(width, group):
    pairs = width // group // 2
    ids = np.arange(width // 2)
    cos, sin = trig(ids, np.arange(width), width)
    sin[0] = trig(np.array([width // 2]), np.arange(width), width)[0][0]
    packed = np.stack([cos.reshape(group, pairs, width), sin.reshape(group, pairs, width)], 1)
    unpack = np.zeros((width, width), np.float32)
    for k in range(width // 2):
        place = (k // pairs) * 2 * pairs + k % pairs
        if k == 0:
            unpack[0, place] = 1.0
            unpack[width // 2, place + pairs] = 1.0
        else:
            unpack[k, place] = 1.0
            unpack[k, place + pairs] = -1.0
            unpack[width - k, place] = 1.0
            unpack[width - k, place + pairs] = 1.0
    return low_table(packed.reshape(width, width)), low_table(unpack)


def params(limit=24):
    return pltpu.CompilerParams(vmem_limit_bytes=limit * MIB)


def mm(left, right):
    return jnp.dot(left, right, preferred_element_type=F32)


def mm_nt(left, right):
    return lax.dot_general(left, right, (((1,), (1,)), ((), ())), preferred_element_type=F32)


def token_kernel(count, tokens, d_ref, m_ref, c_ref, s_ref, o_ref, x_ref):
    group, rows = d_ref.shape[0], d_ref.shape[1]

    @pl.when(pl.program_id(0) == 0)
    def _():
        for m in range(count):
            for g in range(group):
                x_ref[m * rows : (m + 1) * rows, g * tokens : (g + 1) * tokens] = d_ref[
                    g, :, m * tokens : (m + 1) * tokens
                ]

    values = x_ref[...]
    mixed = jnp.where(m_ref[...] > 0.0, mm(values, c_ref[...]), mm(values, s_ref[...])).astype(BF)
    for g in range(o_ref.shape[0]):
        for m in range(count):
            o_ref[g, :, m * tokens : (m + 1) * tokens] = mixed[
                m * rows : (m + 1) * rows, g * tokens : (g + 1) * tokens
            ]


def token_transform(data, mask, cos, sin, count):
    group, rows, columns = data.shape
    length = cos.shape[0]
    tokens = columns // count
    dests = max(1, min(group, 512 // tokens))
    block = dests * tokens
    whole = lambda i: (0, 0)
    return pl.pallas_call(
        lambda *refs: token_kernel(count, tokens, *refs),
        grid=(length // block,),
        in_specs=[
            pl.BlockSpec(data.shape, lambda i: (0, 0, 0)),
            pl.BlockSpec(mask.shape, whole),
            pl.BlockSpec((length, block), lambda i: (0, i)),
            pl.BlockSpec((length, block), lambda i: (0, i)),
        ],
        out_specs=pl.BlockSpec((dests, rows, columns), lambda i: (i, 0, 0)),
        out_shape=jax.ShapeDtypeStruct(data.shape, BF),
        scratch_shapes=[pltpu.VMEM((count * rows, length), BF)],
        compiler_params=params(40),
        cost_estimate=pl.CostEstimate(
            flops=4 * count * rows * length * length,
            bytes_accessed=4 * length * length,
            transcendentals=0,
        ),
    )(data, mask, cos, sin)


def gelu_parts(x):
    e = jnp.exp(-0.5 * x * x)
    t = 1.0 / (1.0 + (0.3275911 / math.sqrt(2.0)) * jnp.abs(x))
    poly = t * (
        0.5 * 0.254829592
        + t
        * (
            0.5 * -0.284496736
            + t * (0.5 * 1.421413741 + t * (0.5 * -1.453152027 + t * (0.5 * 1.061405429)))
        )
    )
    tail = poly * e
    return jnp.where(x >= 0.0, 1.0 - tail, tail), e * (1.0 / math.sqrt(2.0 * math.pi))


def blocks(size, step):
    step = step if size % step == 0 else size
    return [(i, step) for i in range(0, size, step)]


def ffn_kernel(a_ref, b_ref, w1_ref, bias_ref, w2_ref, oa_ref, ob_ref, act_ref, slope_ref):
    columns = a_ref.shape[1]
    x = jnp.concatenate([a_ref[...], b_ref[...]], axis=1)
    for start, size in blocks(w1_ref.shape[0], 256):
        hidden = mm(w1_ref[start : start + size], x) + bias_ref[start : start + size]
        cdf, density = gelu_parts(hidden)
        act_ref[start : start + size] = (hidden * cdf).astype(BF)
        slope_ref[start : start + size] = (cdf + hidden * density).astype(BF)
    for start, size in blocks(w2_ref.shape[0], 256):
        part = mm(w2_ref[start : start + size], act_ref[...]).astype(BF)
        oa_ref[start : start + size] = part[:, :columns]
        ob_ref[start : start + size] = part[:, columns:]


def ffn(first, second, w1, bias, w2):
    width, columns = first.shape
    units = w1.shape[0]
    half = jax.ShapeDtypeStruct((width, columns), BF)
    full = jax.ShapeDtypeStruct((units, 2 * columns), BF)
    return pl.pallas_call(
        ffn_kernel,
        out_shape=(half, half, full, full),
        compiler_params=params(32),
        cost_estimate=pl.CostEstimate(
            flops=8 * width * units * columns, bytes_accessed=8 << 20, transcendentals=0
        ),
    )(first, second, w1, bias, w2)


def ffn_back_kernel(a_ref, b_ref, w2t_ref, slope_ref, w1t_ref, oa_ref, ob_ref, gp_ref, gb_ref):
    columns = a_ref.shape[1]
    g = jnp.concatenate([a_ref[...], b_ref[...]], axis=1)
    for start, size in blocks(w2t_ref.shape[0], 256):
        grad = mm(w2t_ref[start : start + size], g) * slope_ref[start : start + size].astype(F32)
        low = grad.astype(BF)
        gp_ref[start : start + size] = low
        gb_ref[start : start + size] = jnp.sum(low.astype(F32), axis=1, keepdims=True)
    for start, size in blocks(w1t_ref.shape[0], 256):
        part = mm(w1t_ref[start : start + size], gp_ref[...]).astype(BF)
        oa_ref[start : start + size] = part[:, :columns]
        ob_ref[start : start + size] = part[:, columns:]


def ffn_back(first, second, w2t, slope, w1t):
    width, columns = first.shape
    units = w2t.shape[0]
    half = jax.ShapeDtypeStruct((width, columns), BF)
    return pl.pallas_call(
        ffn_back_kernel,
        out_shape=(
            half,
            half,
            jax.ShapeDtypeStruct((units, 2 * columns), BF),
            jax.ShapeDtypeStruct((units, 1), F32),
        ),
        compiler_params=params(32),
        cost_estimate=pl.CostEstimate(
            flops=8 * width * units * columns, bytes_accessed=8 << 20, transcendentals=0
        ),
    )(first, second, w2t, slope, w1t)


def weight_kernel(count, *refs):
    x_refs, pre_refs = refs[: 2 * count], refs[2 * count : 3 * count]
    g_refs, act_refs = refs[3 * count : 5 * count], refs[5 * count : 6 * count]
    one_ref, two_ref = refs[-2:]

    def joined(pieces):
        return jnp.concatenate([piece[...] for piece in pieces], axis=1)

    g, act = joined(g_refs), joined(act_refs)
    for start, size in blocks(g.shape[0], 256):
        two_ref[start : start + size] = mm_nt(g[start : start + size], act).astype(BF)
    pre, x = joined(pre_refs), joined(x_refs)
    for start, size in blocks(pre.shape[0], 256):
        one_ref[start : start + size] = mm_nt(pre[start : start + size], x).astype(BF)


def weight_grads(xs, pres, gs, acts):
    units, width = pres[0].shape[0], xs[0].shape[0]
    tokens = sum(p.shape[1] for p in pres)
    return pl.pallas_call(
        lambda *refs: weight_kernel(len(pres), *refs),
        out_shape=(
            jax.ShapeDtypeStruct((units, width), BF),
            jax.ShapeDtypeStruct((width, units), BF),
        ),
        compiler_params=params(40),
        cost_estimate=pl.CostEstimate(
            flops=4 * width * units * tokens, bytes_accessed=8 << 20, transcendentals=0
        ),
    )(*xs, *pres, *gs, *acts)


def pencil_kernel(count, tokens, section_ref, x_ref, o_ref):
    for d in range(o_ref.shape[0]):
        for m in range(count):
            o_ref[d, :, m * tokens : (m + 1) * tokens] = x_ref[
                0, m, :, d * tokens : (d + 1) * tokens
            ]


def pencil_parts(local, section, sections, mps):
    batches, features, token_count = local.shape
    count, tokens = batches // sections, token_count // mps
    local = local.reshape(sections, count, features, token_count)
    out = jax.ShapeDtypeStruct((mps, features, count * tokens), local.dtype)
    return pl.pallas_call(
        lambda *refs: pencil_kernel(count, tokens, *refs),
        grid_spec=pltpu.PrefetchScalarGridSpec(
            num_scalar_prefetch=1,
            grid=(1,),
            in_specs=[
                pl.BlockSpec((1, count, features, token_count), lambda i, s: (s[0], 0, 0, 0))
            ],
            out_specs=pl.BlockSpec(out.shape, lambda i, s: (0, 0, 0)),
        ),
        out_shape=out,
        compiler_params=params(16),
    )(section.reshape(1), local)


def block_kernel(count, tokens, x_ref, o_ref):
    for d in range(x_ref.shape[1]):
        for m in range(count):
            o_ref[0, m, :, d * tokens : (d + 1) * tokens] = x_ref[
                0, d, :, m * tokens : (m + 1) * tokens
            ].astype(F32)


def block_parts(got, sections, count):
    parts, features, columns = got.shape
    mps, tokens = parts // sections, columns // count
    got = got.reshape(sections, mps, features, columns)
    out = jax.ShapeDtypeStruct((sections, count, features, mps * tokens), F32)
    whole = lambda i: (i, 0, 0, 0)
    return pl.pallas_call(
        lambda *refs: block_kernel(count, tokens, *refs),
        grid=(sections,),
        in_specs=[pl.BlockSpec((1, mps, features, columns), whole)],
        out_specs=pl.BlockSpec((1,) + out.shape[1:], whole),
        out_shape=out,
        compiler_params=params(16),
    )(got).reshape(1, sections * count, features, mps * tokens)


def norm_forward(values, scaling, offsets):
    average = jnp.mean(values, axis=0, keepdims=True)
    centered = values - average
    spread = jnp.mean(centered * centered, axis=0, keepdims=True)
    inverse = lax.rsqrt(spread + EPSILON)
    standard = centered * inverse
    return standard * scaling + offsets, standard, inverse


def norm_backward(upstream, standard, inverse, scaling):
    weighted = upstream * scaling
    grad = inverse * (
        weighted
        - jnp.mean(weighted, axis=0, keepdims=True)
        - standard * jnp.mean(weighted * standard, axis=0, keepdims=True)
    )
    return grad, jnp.sum(upstream * standard, axis=1), jnp.sum(upstream, axis=1)


def shards(
    inputs,
    cotangent,
    labels,
    scored,
    expand_weight,
    expand_bias,
    reduce_weight,
    reduce_bias,
    first_gain,
    first_shift,
    second_gain,
    second_shift,
):
    batches, feature_count, token_count = inputs.shape
    sections, seqs, mps = (lax.axis_size(axis) for axis in ("section", "seq", "mp"))
    group = seqs * mps
    width = feature_count * mps
    length = token_count * seqs
    units = expand_weight.shape[1]
    count = batches // sections
    tokens = token_count // mps
    columns = count * tokens
    factor = 1.0 / math.sqrt(length * width)
    section = lax.axis_index("section")
    seq_index = lax.axis_index("seq")
    mp_index = lax.axis_index("mp")
    is_first = section == 0
    ring = (("seq", "mp"),)[0]

    packed_np, unpack_np = feature_tables(width, group)
    packed, unpack = jnp.asarray(packed_np), jnp.asarray(unpack_np)
    ids = np.arange(length)
    cos_np, sin_np = trig(ids, ids, length)
    token_cos, token_sin = jnp.asarray(low_table(cos_np)), jnp.asarray(low_table(sin_np))
    rows = width // group
    row_ids = jnp.arange(count * rows, dtype=jnp.int32) % rows
    device = seq_index * mps + mp_index
    mask = (row_ids < rows // 2) | ((row_ids == rows // 2) & (device == 0))
    mask = mask.astype(F32)[:, None]

    swap = [(i, (i + 1) % sections) for i in range(sections)]
    own_one, own_two = expand_weight[0], reduce_weight[0]
    other_one = lax.ppermute(own_one, "section", swap)
    other_two = lax.ppermute(own_two, "section", swap)
    w1 = [jnp.where(is_first, own_one, other_one), jnp.where(is_first, other_one, own_one)]
    w2 = [jnp.where(is_first, own_two, other_two), jnp.where(is_first, other_two, own_two)]
    core_swap = [(i, i ^ 1) for i in range(mps)]
    sides = mps // 2

    def side_shift(array, by):
        pairs = [(i, (i // 2 + by) % sides * 2 + i % 2) for i in range(mps)]
        return lax.ppermute(array, "mp", pairs)

    small = jnp.concatenate(
        [
            expand_bias[0],
            reduce_bias[0],
            first_gain[0],
            first_shift[0],
            second_gain[0],
            second_shift[0],
        ]
    )
    other = lax.ppermute(small, "section", swap)
    small = jnp.where(is_first, jnp.stack([small, other]), jnp.stack([other, small]))
    biases, vectors = small[:, :units], small[:, units:].reshape(sections, 5, 1, feature_count)
    sibling = lax.ppermute(vectors, "mp", core_swap)
    core = mp_index % 2
    chip = jnp.concatenate(
        [jnp.where(core == 0, vectors, sibling), jnp.where(core == 0, sibling, vectors)], axis=2
    )
    chips = jnp.stack([side_shift(chip, -j) if j else chip for j in range(sides)], axis=2)
    order = [(i - mp_index // 2) % sides for i in range(sides)]
    vectors = jnp.stack(
        [lax.dynamic_index_in_dim(chips, i, 2, keepdims=False) for i in order], axis=2
    ).reshape(sections, 5, width, 1)

    def to_pencils(local):
        own = pencil_parts(local, section, sections, mps)
        return lax.all_to_all(own, "mp", 0, 0, tiled=True).reshape(width, columns)

    def to_blocks(layers):
        sent = jnp.stack(layers).reshape(sections * mps, feature_count, columns)
        got = lax.all_to_all(sent, ("section", "mp"), 0, 0, tiled=True)
        return block_parts(got, sections, count)

    def fourier(low):
        sent = mm(packed, low).astype(BF).reshape(group, rows, columns)
        got = lax.all_to_all(sent, ring, 0, 0, tiled=True)
        mixed = token_transform(got, mask, token_cos, token_sin, count)
        got = lax.all_to_all(mixed, ring, 0, 0, tiled=True).reshape(width, columns)
        return mm(unpack, got) * factor

    def gathered(own):
        firsts = [own] + [side_shift(own, j) for j in range(1, sides)]
        return [(first, lax.ppermute(first, "mp", core_swap)) for first in firsts]

    def reduced(parts):
        total = None
        for j in reversed(range(sides)):
            keep, give = parts[j]
            chip = keep.astype(F32) + lax.ppermute(give, "mp", core_swap).astype(F32)
            if j > 0:
                chip = side_shift(chip.astype(BF), -j).astype(F32)
            total = chip if total is None else total + chip
        return total

    def counts(out, local_labels, local_scored):
        exponent = jnp.exp(out)
        matches = jnp.arange(width, dtype=jnp.int32)[:, None] == local_labels[None, :]
        label_exp = jnp.sum(jnp.where(matches, exponent, 0.0), axis=0)
        return jnp.sum(label_exp / jnp.sum(exponent, axis=0) * local_scored)

    def own_tokens(ints):
        own = lax.dynamic_slice(ints, (section * count, mp_index * tokens), (count, tokens))
        return own.reshape(columns)

    local_labels, local_scored = own_tokens(labels), own_tokens(scored).astype(F32)

    low = to_pencils(inputs)
    saved, outs, hits = [], [], jnp.zeros((), F32)
    for layer in range(2):
        reduce_vec, gain1, shift1, gain2, shift2 = (vectors[layer, i] for i in range(5))
        bias = biases[layer][:, None]
        normed, unit1, inv1 = norm_forward(low.astype(F32) + fourier(low), gain1, shift1)
        xs = gathered(normed.astype(BF))
        runs = [ffn(a, b, w1[layer], bias, w2[layer]) for a, b in xs]
        branch = reduced([run[:2] for run in runs])
        out, unit2, inv2 = norm_forward(normed + branch + reduce_vec, gain2, shift2)
        low = out.astype(BF)
        outs.append(low)
        hits = hits + counts(out, local_labels, local_scored)
        saved.append((unit1, inv1, xs, runs, unit2, inv2))
    outputs = to_blocks(outs)

    up = to_pencils(cotangent)
    grads_in, weights_out, smalls = [None, None], [None, None], []
    for layer in (1, 0):
        _, gain1, _, gain2, _ = (vectors[layer, i] for i in range(5))
        unit1, inv1, xs, runs, unit2, inv2 = saved[layer]
        grad_second, gain2_grad, shift2_grad = norm_backward(up.astype(F32), unit2, inv2, gain2)
        gs = gathered(grad_second.astype(BF))
        w2t, w1t = w2[layer].T, w1[layer].T
        backs = [ffn_back(a, b, w2t, run[3], w1t) for (a, b), run in zip(gs, runs)]
        branch = reduced([back[:2] for back in backs])
        weights_out[layer] = weight_grads(
            [x for pair in xs for x in pair],
            [back[2] for back in backs],
            [g for pair in gs for g in pair],
            [run[2] for run in runs],
        )
        branch, weights_out[layer] = lax.optimization_barrier((branch, weights_out[layer]))
        grad_normed = grad_second + branch
        bias_grad = sum(back[3] for back in backs)[:, 0]
        grad_first, gain1_grad, shift1_grad = norm_backward(grad_normed, unit1, inv1, gain1)
        grad_source = grad_first + fourier(grad_first.astype(BF))
        up = grad_source.astype(BF)
        grads_in[layer] = up
        smalls = [
            (bias_grad, jnp.sum(grad_second, axis=1), gain1_grad, shift1_grad, gain2_grad, shift2_grad)
        ] + smalls
    input_grads = to_blocks(grads_in)

    def scattered(layer):
        return [
            lax.psum_scatter(w, "seq", scatter_dimension=0, tiled=True) for w in weights_out[layer]
        ]

    late, early = scattered(1), scattered(0)
    weight_sums = []
    for first, second in zip(early, late):
        got = lax.ppermute(jnp.where(is_first, second, first), "section", swap)
        total = (jnp.where(is_first, first, second).astype(F32) + got.astype(F32)).astype(BF)
        weight_sums.append(lax.all_gather(total, "seq", axis=0, tiled=True).astype(F32))

    def summed(array, axis):
        size, step = lax.axis_size(axis), 1
        while step < size:
            array = array + lax.ppermute(array, axis, [(i, i ^ step) for i in range(size)])
            step *= 2
        return array

    def padded(flat):
        return jnp.pad(flat, (0, -flat.shape[0] % 1024)).reshape(-1, 128)

    per = 5 * width
    flat = [v for layer in smalls for v in layer[1:]] + [hits[None]]
    flat = summed(padded(jnp.concatenate(flat)), "mp")
    bias_rows = padded(jnp.concatenate([layer[0] for layer in smalls]))
    flat = jnp.concatenate([flat, bias_rows])
    flat = summed(summed(flat, "seq"), "section")
    bias_sum = flat[-bias_rows.shape[0] :].reshape(-1)[: 2 * units].reshape(2, units)
    bias_sum = lax.dynamic_index_in_dim(bias_sum, section, 0, keepdims=False)
    flat = flat[: -bias_rows.shape[0]].reshape(-1)
    accuracy = flat[2 * per]
    features = flat[: 2 * per].reshape(2, 5, mps, feature_count)
    features = lax.dynamic_index_in_dim(features, section, 0, keepdims=False)
    features = lax.dynamic_index_in_dim(features, mp_index, 1, keepdims=False)

    return (
        outputs,
        input_grads,
        weight_sums[0][None],
        bias_sum[None],
        weight_sums[1][None],
        features[0][None],
        features[1][None],
        features[2][None],
        features[3][None],
        features[4][None],
        accuracy,
    )


def solution(mesh):
    placed = (
        P(None, "mp", "seq"),
        P(None, "mp", "seq"),
        P(None, "seq"),
        P(None, "seq"),
        P("section", "mp", None),
        P("section", "mp"),
        P("section", None, "mp"),
        P("section", "mp"),
        P("section", "mp"),
        P("section", "mp"),
        P("section", "mp"),
        P("section", "mp"),
    )
    return jax.shard_map(
        shards,
        mesh=mesh,
        in_specs=placed,
        out_specs=(
            P("section", None, "mp", "seq"),
            P("section", None, "mp", "seq"),
            P("section", "mp", None),
            P("section", "mp"),
            P("section", None, "mp"),
            P("section", "mp"),
            P("section", "mp"),
            P("section", "mp"),
            P("section", "mp"),
            P("section", "mp"),
            P(),
        ),
        check_vma=False,
    )
```

time: 2050 us -> 625 us (0.30)
  blocking collectives: 907 us -> 97 us
  matrix products: 649 us -> 11.8 us
  waiting for transfers between devices: 314 us -> 226 us
  Pallas kernels: 0 us -> 72.4 us
  local copies, waits for them, and re-layouts: 24.3 us -> 84.5 us
  other arithmetic: 101 us -> 49.8 us
  starting transfers between devices: 31.7 us -> 57.7 us
    all_gather x56 -> x0, blocking collectives: 705 us -> none  [the longest x7 145 us: shards(): lax.all_gather(grad_first.astype(jnp.bfloat16), 'seq', axis=1, tiled=True)]
    dot_general x98 -> x8, matrix products: 649 us -> 11.8 us  [mm(): return jnp.dot(left, right, preferred_element_type=F32)]
    reduce_scatter x14 -> x4, waiting for transfers between devices: 252 us -> 48.1 us  [scattered(): lax.psum_scatter(w, 'seq', scatter_dimension=0, tiled=True)]
    psum x30 -> x0, blocking collectives: 202 us -> none  [the longest x28 170 us: row_totals(): return lax.psum((first_rows, second_rows), 'mp')]
    all_to_all x0 -> x5, blocking collectives: none -> 97 us  [the longest x2 42.7 us: fourier(): got = lax.all_to_all(sent, ring, 0, 0, tiled=True)]
    ppermute x12 -> x36, waiting for transfers between devices: 61.1 us -> 143 us  [the longest x9 97.9 us: side_shift(): return lax.ppermute(array, 'mp', pairs)]
    pallas_call x0 -> x18, Pallas kernels: none -> 72.4 us  [the longest x4 26.9 us: token_transform(): pl.pallas_call(lambda *refs: token_kernel(count, tokens, *refs), grid=(le...]
    unnamed x535 -> x308, local copies, waits for them, and re-layouts: 24.3 us -> 56.7 us
  transfers between devices with their start and end apart: 27 -> 49, of which waited for: 26 -> 23; matrix products, arithmetic and copies ran while one was open for 5% -> 12% of each run, Pallas kernels for 0% -> 8%
where the time goes in v1:
time: 625 us; the launch traced here: 616 us
  waiting for transfers between devices  226 us (36%)
  blocking collectives  97 us (16%)
  local copies, waits for them, and re-layouts  84.5 us (14%)
  Pallas kernels  72.4 us (12%)
  starting transfers between devices  57.7 us (9%)
  other arithmetic  49.8 us (8%)
  between operations  17.3 us (3%)
  matrix products  11.8 us (2%)
    ppermute x9, waiting for transfers between devices, side_shift(): return lax.ppermute(array, 'mp', pairs)  97.9 us
    unnamed x308, local copies, waits for them, and re-layouts  56.7 us
    reduce_scatter x4, waiting for transfers between devices, scattered(): lax.psum_scatter(w, 'seq', scatter_dimension=0, tiled=True)  48.1 us
    all_to_all x2, blocking collectives, fourier(): got = lax.all_to_all(sent, ring, 0, 0, tiled=True)  42.7 us
    all_to_all x2, blocking collectives, fourier(): got = lax.all_to_all(mixed, ring, 0, 0, tiled=True).reshape(width, columns)  40.6 us
    pallas_call x4, Pallas kernels, token_transform(): pl.pallas_call(lambda *refs: token_kernel(count, tokens, *refs), grid=(le...  26.9 us
    ppermute x1, waiting for transfers between devices, shards(): other_two = lax.ppermute(own_two, 'section', swap)  21.9 us
    pallas_call x4, Pallas kernels, ffn(): pl.pallas_call(ffn_kernel, out_shape=(half, half, full, full), compiler_p...  19.2 us
  transfers between devices with their start and end apart: 49, of which 23 were waited for; matrix products, arithmetic and copies ran while one was open for 12% of the time, Pallas kernels for 8%

profile of v1, /device:TPU:0, one launch (start us, length us, event | category | flops | bytes accessed | tf_op | source)
XLA Modules:
  0.0 616.4 jit_solution(13082929724673635532)
XLA Ops:
  8.6 13.7 %all_to_all.60 = bf16[4,192,384]{2,1,0:T(8,128)(2,1)S(1)} all-to-all(bf16[4,192,384]{2,1,0:T(8,128)(2,1)S(1)} %shard_map.239), channel_id=1, replica_groups=mesh['section'=2,'seq'=4,'mp'=4] {'mp'}, dimensions={0} | all-to-all | bytes 1179648 | tf_op jit(solution)/shard_map/all_to_all | solution.py:373
  29.9 15.5 %all-to-all-done.1.refs_0_ = bf16[16,48,384]{2,1,0:T(8,128)(2,1)S(1)} async-done(((bf16[16,48,384]{2,1,0:T(8,128)(2,1)}), bf16[16,48,384]{2,1,0:T(8,128)(2,1)S(1)}, u32[]{:S(2)}, u32[]{:S(2)}) %all-to-all-start.1) | async-done | bytes 589856 | tf_op jit(solution)/shard_map/all_to_all | solution.py:382
  48.8 7.0 %shard_map.240 = bf16[16,48,384]{2,1,0:T(8,128)(2,1)} custom-call(bf16[16,48,384]{2,1,0:T(8,128)(2,1)S(1)} %all-to-all-done.1.refs_0_, f32[144,1]{1,0:T(8,128)S(1)} %fusion.41.refs_1_, bf16[2048,2048]{1,0:T(8,128)(2,1)S(1)} %copy-done.2, bf16[2048,2048]{1,0:T(8,128)(2,1)} %constant.146.clone.refs_3_), custom_call_target="tpu_custom_call" | custom-call | flops 2415919104 | bytes 16777216 | tf_op jit(solution)/shard_map/pallas_call | solution.py:87
  82.1 14.6 %collective-permute-done.3.a_ref.refs_2_ = bf16[768,384]{1,0:T(8,128)(2,1)} collective-permute-done((bf16[768,384]{1,0:T(8,128)(2,1)S(1)}, bf16[768,384]{1,0:T(8,128)(2,1)}, u32[]{:S(2)}, u32[]{:S(2)}) %collective-permute-start.3) | collective-permute-done | bytes 589856 | tf_op jit(solution)/shard_map/ppermute | solution.py:345
  100.7 21.9 %collective-permute-done.6 = bf16[768,768]{0,1:T(8,128)(2,1)} collective-permute-done((bf16[768,768]{0,1:T(8,128)(2,1)S(1)}, bf16[768,768]{0,1:T(8,128)(2,1)}, u32[]{:S(2)}, u32[]{:S(2)}) %collective-permute-start.6) | collective-permute-done | bytes 1179680 | tf_op jit(solution)/shard_map/ppermute | solution.py:337
  146.2 14.0 %collective-permute-done.8 = bf16[768,384]{1,0:T(8,128)(2,1)S(1)} collective-permute-done((bf16[768,384]{1,0:T(8,128)(2,1)S(1)}, bf16[768,384]{1,0:T(8,128)(2,1)S(1)}, u32[]{:S(2)}, u32[]{:S(2)}) %collective-permute-start.8) | collective-permute-done | bytes 589856 | tf_op jit(solution)/shard_map/ppermute | solution.py:345
  166.2 22.1 %all_to_all.61.refs_0_ = bf16[16,48,384]{2,1,0:T(8,128)(2,1)S(1)} all-to-all(bf16[16,48,384]{2,1,0:T(8,128)(2,1)} %bitcast.170), channel_id=1, replica_groups=mesh['section'=2,'seq'=4,'mp'=4] {'seq','mp'}, dimensions={0} | all-to-all | bytes 1179648 | tf_op jit(solution)/shard_map/all_to_all | solution.py:382
  198.1 20.4 %all_to_all.62 = bf16[16,48,384]{2,1,0:T(8,128)(2,1)S(1)} all-to-all(bf16[16,48,384]{2,1,0:T(8,128)(2,1)S(1)} %shard_map.243), channel_id=1, replica_groups=mesh['section'=2,'seq'=4,'mp'=4] {'seq','mp'}, dimensions={0} | all-to-all | bytes 1179648 | tf_op jit(solution)/shard_map/all_to_all | solution.py:384
  221.9 14.8 %collective-permute-done.11.a_ref.refs_2_ = bf16[768,384]{1,0:T(8,128)(2,1)} collective-permute-done((bf16[768,384]{1,0:T(8,128)(2,1)S(1)}, bf16[768,384]{1,0:T(8,128)(2,1)}, u32[]{:S(2)}, u32[]{:S(2)}) %collective-permute-start.11) | collective-permute-done | bytes 589856 | tf_op jit(solution)/shard_map/ppermute | solution.py:345
  279.7 10.6 %collective-permute-done.14 = bf16[768,384]{1,0:T(8,128)(2,1)} collective-permute-done((bf16[768,384]{1,0:T(8,128)(2,1)}, bf16[768,384]{1,0:T(8,128)(2,1)}, u32[]{:S(2)}, u32[]{:S(2)}) %collective-permute-start.14) | collective-permute-done | bytes 589856 | tf_op jit(solution)/shard_map/ppermute | solution.py:345
  299.8 13.2 %collective-permute-done.17.a_ref.refs_8_ = bf16[768,384]{1,0:T(8,128)(2,1)S(1)} collective-permute-done((bf16[768,384]{1,0:T(8,128)(2,1)S(1)}, bf16[768,384]{1,0:T(8,128)(2,1)S(1)}, u32[]{:S(2)}, u32[]{:S(2)}) %collective-permute-start.17) | collective-permute-done | bytes 589856 | tf_op jit(solution)/shard_map/ppermute | solution.py:345
  321.4 6.7 %shard_map.250 = (bf16[768,768]{1,0:T(8,128)(2,1)}, bf16[768,768]{1,0:T(8,128)(2,1)S(1)}) custom-call(bf16[768,384]{1,0:T(8,128)(2,1)S(1)} %copy-done.26, bf16[768,384]{1,0:T(8,128)(2,1)} %collective-permute-done.15.b_ref.refs_1_, bf16[768,384]{1,0:T(8,128)(2,1)} %collective-permute-done.11.a_ref.refs_2_, ...), custom_call_target="tpu_custom_call" | custom-call | flops 3623878656 | bytes 8388608 | tf_op jit(solution)/shard_map/pallas_call | solution.py:209
  328.1 7.3 %collective-permute-done.20 = bf16[768,384]{1,0:T(8,128)(2,1)S(1)} collective-permute-done((bf16[768,384]{1,0:T(8,128)(2,1)S(1)}, bf16[768,384]{1,0:T(8,128)(2,1)S(1)}, u32[]{:S(2)}, u32[]{:S(2)}) %collective-permute-start.20) | collective-permute-done | bytes 589856 | tf_op jit(solution)/shard_map/ppermute | solution.py:345
  344.9 20.7 %all_to_all.63.refs_0_ = bf16[16,48,384]{2,1,0:T(8,128)(2,1)S(1)} all-to-all(bf16[16,48,384]{2,1,0:T(8,128)(2,1)S(1)} %bitcast.171), channel_id=1, replica_groups=mesh['section'=2,'seq'=4,'mp'=4] {'seq','mp'}, dimensions={0} | all-to-all | bytes 1179648 | tf_op jit(solution)/shard_map/all_to_all | solution.py:382
  369.0 6.5 %shard_map.251 = bf16[16,48,384]{2,1,0:T(8,128)(2,1)S(1)} custom-call(bf16[16,48,384]{2,1,0:T(8,128)(2,1)S(1)} %all_to_all.63.refs_0_, f32[144,1]{1,0:T(8,128)S(1)} %copy-done.10, bf16[2048,2048]{1,0:T(8,128)(2,1)S(1)} %copy-done.4, bf16[2048,2048]{1,0:T(8,128)(2,1)} %constant.146.clone.refs_3_), custom_call_target="tpu_custom_call" | custom-call | flops 2415919104 | bytes 16777216 | tf_op jit(solution)/shard_map/pallas_call | solution.py:87
  375.5 20.2 %all_to_all.64 = bf16[16,48,384]{2,1,0:T(8,128)(2,1)S(1)} all-to-all(bf16[16,48,384]{2,1,0:T(8,128)(2,1)S(1)} %shard_map.251), channel_id=1, replica_groups=mesh['section'=2,'seq'=4,'mp'=4] {'seq','mp'}, dimensions={0} | all-to-all | bytes 1179648 | tf_op jit(solution)/shard_map/all_to_all | solution.py:384
  399.3 14.8 %collective-permute-done.23.a_ref.refs_8_ = bf16[768,384]{1,0:T(8,128)(2,1)} collective-permute-done((bf16[768,384]{1,0:T(8,128)(2,1)S(1)}, bf16[768,384]{1,0:T(8,128)(2,1)}, u32[]{:S(2)}, u32[]{:S(2)}) %collective-permute-start.23) | collective-permute-done | bytes 589856 | tf_op jit(solution)/shard_map/ppermute | solution.py:345
  425.0 6.5 %shard_map.254 = (bf16[768,768]{1,0:T(8,128)(2,1)}, bf16[768,768]{1,0:T(8,128)(2,1)}) custom-call(bf16[768,384]{1,0:T(8,128)(2,1)S(1)} %copy-done.23, bf16[768,384]{1,0:T(8,128)(2,1)S(1)} %copy-done.39, bf16[768,384]{1,0:T(8,128)(2,1)} %collective-permute-done.3.a_ref.refs_2_, bf16[768,384]{1,0:T(8,128)(2,1)} %collective-permute-done.4.b_ref.refs_3_, ...), custom_call_target="tpu_custom_call" | custom-call | flops 3623878656 | bytes 8388608 | tf_op jit(solution)/shard_map/pallas_call | solution.py:209
  431.5 8.5 %collective-permute-done.26 = bf16[768,384]{1,0:T(8,128)(2,1)S(1)} collective-permute-done((bf16[768,384]{1,0:T(8,128)(2,1)S(1)}, bf16[768,384]{1,0:T(8,128)(2,1)S(1)}, u32[]{:S(2)}, u32[]{:S(2)}) %collective-permute-start.26) | collective-permute-done | bytes 589856 | tf_op jit(solution)/shard_map/ppermute | solution.py:345
  458.2 23.5 %reduce-scatter.9.cloned.1.call-done = bf16[192,768]{1,0:T(8,128)(2,1)} async-done(((bf16[768,768]{1,0:T(8,128)(2,1)}), bf16[192,768]{1,0:T(8,128)(2,1)}) %reduce-scatter.9.cloned.1.call-update) | async-done | bytes 294928 | tf_op jit(solution)/shard_map/reduce_scatter | solution.py:459
  495.6 7.0 %shard_map.255 = bf16[16,48,384]{2,1,0:T(8,128)(2,1)} custom-call(bf16[16,48,384]{2,1,0:T(8,128)(2,1)S(1)} %all-to-all-done.9.refs_0_, f32[144,1]{1,0:T(8,128)S(1)} %copy-done.10, bf16[2048,2048]{1,0:T(8,128)(2,1)S(1)} %copy-done.5, bf16[2048,2048]{1,0:T(8,128)(2,1)} %constant.146.clone.refs_3_), custom_call_target="tpu_custom_call" | custom-call | flops 2415919104 | bytes 16777216 | tf_op jit(solution)/shard_map/pallas_call | solution.py:87
  520.2 24.6 %reduce-scatter.5.cloned.1.call-done = bf16[192,768]{1,0:T(8,128)(2,1)} async-done(((bf16[768,768]{1,0:T(8,128)(2,1)}), bf16[192,768]{1,0:T(8,128)(2,1)}) %reduce-scatter.5.cloned.1.call-update) | async-done | bytes 294928 | tf_op jit(solution)/shard_map/reduce_scatter | solution.py:459
  561.5 6.5 %all-to-all-done.5 = bf16[8,192,384]{2,1,0:T(8,128)(2,1)S(1)} async-done(((bf16[8,192,384]{2,1,0:T(8,128)(2,1)}), bf16[8,192,384]{2,1,0:T(8,128)(2,1)S(1)}, u32[]{:S(2)}, u32[]{:S(2)}) %all-to-all-start.5) | async-done | bytes 1179680 | tf_op jit(solution)/shard_map/all_to_all | solution.py:377
  594.8 11.7 %all-gather.3.cloned.1.call-done = bf16[768,768]{1,0:T(8,128)(2,1)} async-done(((bf16[192,768]{1,0:T(8,128)(2,1)}), bf16[768,768]{1,0:T(8,128)(2,1)}) %all-gather.3.cloned.1.call-update) | async-done | bytes 1179664 | tf_op jit(solution)/shard_map/all_gather | solution.py:467
  (516 shorter events, 266.8 us)
Async XLA Ops:
  24.9 20.5 %all-to-all-start.1 = ((bf16[16,48,384]{2,1,0:T(8,128)(2,1)}), bf16[16,48,384]{2,1,0:T(8,128)(2,1)S(1)}, u32[]{:S(2)}, u32[]{:S(2)}) async-start(bf16[16,48,384]{2,1,0:T(8,128)(2,1)} %bitcast.4), calls=%async_computation.1 | async-start | bytes 1179648 | tf_op jit(solution)/shard_map/all_to_all | solution.py:382
  55.8 21.8 %all-to-all-start.2 = ((bf16[16,48,384]{2,1,0:T(8,128)(2,1)}), bf16[16,48,384]{2,1,0:T(8,128)(2,1)}, u32[]{:S(2)}, u32[]{:S(2)}) async-start(bf16[16,48,384]{2,1,0:T(8,128)(2,1)} %shard_map.240), calls=%async_computation.2 | async-start | bytes 1179648 | tf_op jit(solution)/shard_map/all_to_all | solution.py:384
  69.3 30.3 %collective-permute-start.5 = (bf16[768,768]{0,1:T(8,128)(2,1)S(1)}, bf16[768,768]{0,1:T(8,128)(2,1)S(1)}, u32[]{:S(2)}, u32[]{:S(2)}) collective-permute-start(bf16[768,768]{0,1:T(8,128)(2,1)S(1)} %bitcast.166), channel_id=1, source_target_pairs={{0,16},{16,0},{1,17},{17,1},{2,18},{18,2},{3,19},{19,3},{4,20},{20... | collective-permute-start | bytes 3538952 | tf_op jit(solution)/shard_map/ppermute | solution.py:336
  72.5 50.1 %collective-permute-start.6 = (bf16[768,768]{0,1:T(8,128)(2,1)S(1)}, bf16[768,768]{0,1:T(8,128)(2,1)}, u32[]{:S(2)}, u32[]{:S(2)}) collective-permute-start(bf16[768,768]{0,1:T(8,128)(2,1)S(1)} %bitcast.167), channel_id=1, source_target_pairs={{0,16},{16,0},{1,17},{17,1},{2,18},{18,2},{3,19},{19,3},{4,20},{20... | collective-permute-start | bytes 3538952 | tf_op jit(solution)/shard_map/ppermute | solution.py:337
  96.6 33.0 %collective-permute-start.4 = (bf16[768,384]{1,0:T(8,128)(2,1)}, bf16[768,384]{1,0:T(8,128)(2,1)}, u32[]{:S(2)}, u32[]{:S(2)}) collective-permute-start(bf16[768,384]{1,0:T(8,128)(2,1)} %collective-permute-done.3.a_ref.refs_2_), channel_id=1, source_target_pairs={{0,1},{1,0},{2,3},{3,2},{4,5},{5,4},{6,7},{7,6},{8,9},{9,8},{10,11... | collective-permute-start | bytes 1769480 | tf_op jit(solution)/shard_map/ppermute | solution.py:389
  144.4 15.8 %collective-permute-start.8 = (bf16[768,384]{1,0:T(8,128)(2,1)S(1)}, bf16[768,384]{1,0:T(8,128)(2,1)S(1)}, u32[]{:S(2)}, u32[]{:S(2)}) collective-permute-start(bf16[768,384]{1,0:T(8,128)(2,1)S(1)} %add_convert_fusion.3), channel_id=1, source_target_pairs={{0,2},{1,3},{2,0},{3,1},{4,6},{5,7},{6,4},{7,5},{8,10},{9,11},{10,... | collective-permute-start | bytes 1769480 | tf_op jit(solution)/shard_map/ppermute | solution.py:345
  221.3 15.5 %collective-permute-start.11 = (bf16[768,384]{1,0:T(8,128)(2,1)S(1)}, bf16[768,384]{1,0:T(8,128)(2,1)}, u32[]{:S(2)}, u32[]{:S(2)}) collective-permute-start(bf16[768,384]{1,0:T(8,128)(2,1)S(1)} %fusion.30.a_ref.refs_0_), channel_id=1, source_target_pairs={{0,2},{1,3},{2,0},{3,1},{4,6},{5,7},{6,4},{7,5},{8,10},{9,11},{10,... | collective-permute-start | bytes 1769480 | tf_op jit(solution)/shard_map/ppermute | solution.py:345
  242.2 17.7 %collective-permute-start.15 = (bf16[768,384]{1,0:T(8,128)(2,1)}, bf16[768,384]{1,0:T(8,128)(2,1)}, u32[]{:S(2)}, u32[]{:S(2)}) collective-permute-start(bf16[768,384]{1,0:T(8,128)(2,1)} %copy-done.24), channel_id=1, source_target_pairs={{0,1},{1,0},{2,3},{3,2},{4,5},{5,4},{6,7},{7,6},{8,9},{9,8},{10,11... | collective-permute-start | bytes 1769480 | tf_op jit(solution)/shard_map/ppermute | solution.py:389
  254.7 17.5 %collective-permute-start.13 = (bf16[768,384]{1,0:T(8,128)(2,1)}, bf16[768,384]{1,0:T(8,128)(2,1)}, u32[]{:S(2)}, u32[]{:S(2)}) collective-permute-start(bf16[768,384]{1,0:T(8,128)(2,1)} %get-tuple-element.58), channel_id=1, source_target_pairs={{0,1},{1,0},{2,3},{3,2},{4,5},{5,4},{6,7},{7,6},{8,9},{9,8},{10,11... | collective-permute-start | bytes 1769480 | tf_op jit(solution)/shard_map/ppermute | solution.py:395
  255.7 21.9 %all-to-all-start.6 = ((bf16[4,192,384]{2,1,0:T(8,128)(2,1)}), bf16[4,192,384]{2,1,0:T(8,128)(2,1)}, u32[]{:S(2)}, u32[]{:S(2)}) async-start(bf16[4,192,384]{2,1,0:T(8,128)(2,1)} %copy-done.7), calls=%async_computation.6 | async-start | bytes 1179648 | tf_op jit(solution)/shard_map/all_to_all | solution.py:373
  259.9 198.4 %reduce-scatter.11.cloned.1.call-start = ((), (), s32[]{:S(2)}) async-start(), calls=%async_computation.20 | async-start | bytes 1474560 | tf_op jit(solution)/shard_map/reduce_scatter | solution.py:459
  274.3 16.0 %collective-permute-start.14 = (bf16[768,384]{1,0:T(8,128)(2,1)}, bf16[768,384]{1,0:T(8,128)(2,1)}, u32[]{:S(2)}, u32[]{:S(2)}) collective-permute-start(bf16[768,384]{1,0:T(8,128)(2,1)} %add_convert_fusion.2), channel_id=1, source_target_pairs={{0,2},{1,3},{2,0},{3,1},{4,6},{5,7},{6,4},{7,5},{8,10},{9,11},{10,... | collective-permute-start | bytes 1769480 | tf_op jit(solution)/shard_map/ppermute | solution.py:345
  414.2 67.5 %reduce-scatter.9.cloned.1.call-start = ((), (), s32[]{:S(2)}) async-start(), calls=%async_computation.19 | async-start | bytes 1474560 | tf_op jit(solution)/shard_map/reduce_scatter | solution.py:459
  424.4 15.7 %collective-permute-start.26 = (bf16[768,384]{1,0:T(8,128)(2,1)S(1)}, bf16[768,384]{1,0:T(8,128)(2,1)S(1)}, u32[]{:S(2)}, u32[]{:S(2)}) collective-permute-start(bf16[768,384]{1,0:T(8,128)(2,1)S(1)} %add_convert_fusion), channel_id=1, source_target_pairs={{0,2},{1,3},{2,0},{3,1},{4,6},{5,7},{6,4},{7,5},{8,10},{9,11},{10,... | collective-permute-start | bytes 1769480 | tf_op jit(solution)/shard_map/ppermute | solution.py:345
  441.3 79.0 %reduce-scatter.7.cloned.1.call-start = ((), (), s32[]{:S(2)}) async-start(), calls=%async_computation.17 | async-start | bytes 1474560 | tf_op jit(solution)/shard_map/reduce_scatter | solution.py:459
  442.0 102.8 %reduce-scatter.5.cloned.1.call-start = ((), (), s32[]{:S(2)}) async-start(), calls=%async_computation.16 | async-start | bytes 1474560 | tf_op jit(solution)/shard_map/reduce_scatter | solution.py:459
  450.9 41.3 %all-to-all-start.9 = ((bf16[16,48,384]{2,1,0:T(8,128)(2,1)}), bf16[16,48,384]{2,1,0:T(8,128)(2,1)S(1)}, u32[]{:S(2)}, u32[]{:S(2)}) async-start(bf16[16,48,384]{2,1,0:T(8,128)(2,1)} %bitcast.38), calls=%async_computation.9 | async-start | bytes 1179648 | tf_op jit(solution)/shard_map/all_to_all | solution.py:382
  454.7 137.2 %all-gather.5.cloned.1.call-start = ((), (), s32[]{:S(2)}) async-start(), calls=%async_computation.21 | async-start | bytes 1474560 | tf_op jit(solution)/shard_map/all_gather | solution.py:467
  502.7 45.3 %all-to-all-start.10 = ((bf16[16,48,384]{2,1,0:T(8,128)(2,1)}), bf16[16,48,384]{2,1,0:T(8,128)(2,1)S(1)}, u32[]{:S(2)}, u32[]{:S(2)}) async-start(bf16[16,48,384]{2,1,0:T(8,128)(2,1)} %shard_map.255), calls=%async_computation.10 | async-start | bytes 1179648 | tf_op jit(solution)/shard_map/all_to_all | solution.py:384
  519.7 32.8 %collective-permute-start.30 = (f32[64,128]{1,0:T(8,128)}, f32[64,128]{1,0:T(8,128)}, u32[]{:S(2)}, u32[]{:S(2)}) collective-permute-start(f32[64,128]{1,0:T(8,128)} %pad_bitcast_fusion), channel_id=1, source_target_pairs={{0,1},{1,0},{2,3},{3,2},{4,5},{5,4},{6,7},{7,6},{8,9},{9,8},{10,11... | collective-permute-start | bytes 98312 | tf_op jit(solution)/shard_map/ppermute | solution.py:472
  548.0 20.0 %all-to-all-start.5 = ((bf16[8,192,384]{2,1,0:T(8,128)(2,1)}), bf16[8,192,384]{2,1,0:T(8,128)(2,1)S(1)}, u32[]{:S(2)}, u32[]{:S(2)}) async-start(bf16[8,192,384]{2,1,0:T(8,128)(2,1)} %bitcast.24), calls=%async_computation.5 | async-start | bytes 2359296 | tf_op jit(solution)/shard_map/all_to_all | solution.py:377
  551.7 54.8 %all-gather.3.cloned.1.call-start = ((), (), s32[]{:S(2)}) async-start(), calls=%async_computation.18 | async-start | bytes 1474560 | tf_op jit(solution)/shard_map/all_gather | solution.py:467
  553.9 17.9 %collective-permute-start.31 = (f32[64,128]{1,0:T(8,128)}, f32[64,128]{1,0:T(8,128)}, u32[]{:S(2)}, u32[]{:S(2)}) collective-permute-start(f32[64,128]{1,0:T(8,128)} %fusion.54), channel_id=1, source_target_pairs={{0,2},{1,3},{2,0},{3,1},{4,6},{5,7},{6,4},{7,5},{8,10},{9,11},{10,... | collective-permute-start | bytes 98312 | tf_op jit(solution)/shard_map/ppermute | solution.py:472
  568.0 22.3 %all-to-all-start.11 = ((bf16[8,192,384]{2,1,0:T(8,128)(2,1)}), bf16[8,192,384]{2,1,0:T(8,128)(2,1)S(1)}, u32[]{:S(2)}, u32[]{:S(2)}) async-start(bf16[8,192,384]{2,1,0:T(8,128)(2,1)} %bitcast.43), calls=%async_computation.11 | async-start | bytes 2359296 | tf_op jit(solution)/shard_map/all_to_all | solution.py:377
  (173 other events, 1495.9 us)
Sparse Core Ops, SparseCore 0:
  414.3 27.5 reduce-scatter.10
  444.3 37.3 reduce-scatter.8
  484.0 29.8 reduce-scatter.6
  516.6 28.1 reduce-scatter.4
  546.2 29.2 all-gather.4
  576.9 29.5 all-gather.2

commit v2 on v0

v2 whole, which is shorter than its diff:
```python
import math

import jax
import jax.numpy as jnp
import ml_dtypes
import numpy as np
from jax import lax
from jax.experimental import pallas as pl
from jax.experimental.pallas import tpu as pltpu
from jax.sharding import Mesh
from jax.sharding import PartitionSpec as P

EPSILON = 1e-05
BF = jnp.bfloat16
F32 = jnp.float32
MIB = 1 << 20
AXES = ("section", "half", "rest", "side", "core")
RING = ("section", "rest", "side", "core")
PLANE = ("half", "side", "core")
SQUARE = ("section", "half", "side", "core")
VMEM = pl.BlockSpec(memory_space=pltpu.VMEM)
HBM = pl.BlockSpec(memory_space=pltpu.HBM)
SMEM = pl.BlockSpec(memory_space=pltpu.SMEM)


def trig(rows, columns, points):
    phases = (rows.astype(np.int64)[:, None] * columns.astype(np.int64)[None, :]) % points
    angles = phases.astype(np.float64) * (2.0 * math.pi / points)
    return np.cos(angles), np.sin(angles)


def low_table(table):
    return table.astype(np.float32).astype(ml_dtypes.bfloat16)


def feature_tables(width, group):
    pairs = width // group // 2
    ids = np.arange(width // 2)
    cos, sin = trig(ids, np.arange(width), width)
    sin[0] = trig(np.array([width // 2]), np.arange(width), width)[0][0]
    packed = np.stack([cos.reshape(group, pairs, width), sin.reshape(group, pairs, width)], 1)
    unpack = np.zeros((width, width), np.float32)
    for k in range(width // 2):
        place = (k // pairs) * 2 * pairs + k % pairs
        if k == 0:
            unpack[0, place] = 1.0
            unpack[width // 2, place + pairs] = 1.0
        else:
            unpack[k, place] = 1.0
            unpack[k, place + pairs] = -1.0
            unpack[width - k, place] = 1.0
            unpack[width - k, place + pairs] = 1.0
    return low_table(packed.reshape(width, width)), low_table(unpack)


def token_tables(sections, rests, mps, part):
    parity, rest, place, i = np.meshgrid(
        np.arange(sections), np.arange(rests), np.arange(mps), np.arange(part), indexing="ij"
    )
    first = rest * sections * mps * part + sections * (place * part + i) + parity
    length = 2 * first.size
    every = np.stack([first, first + length // 2], 3).reshape(-1)
    cos, sin = trig(every, first.reshape(-1), length)
    return low_table(cos), low_table(sin)


def sorting_table(sections, count):
    table = np.zeros((count, count), np.float32)
    order = np.arange(count).reshape(-1, sections).T.reshape(-1)
    table[order, np.arange(count)] = 1.0
    return low_table(table)


def mm(left, right):
    return jnp.dot(left, right, preferred_element_type=F32)


def mm_nt(left, right):
    return lax.dot_general(left, right, (((1,), (1,)), ((), ())), preferred_element_type=F32)


def blocks(size, step):
    step = step if size % step == 0 else size
    return [(i, i + step) for i in range(0, size, step)]


def shape(dims, dtype=BF):
    return jax.ShapeDtypeStruct(tuple(dims), dtype)


def call(kernel, outs, args, specs=None, scratch=(), limit=57, flops=0, **extra):
    return pl.pallas_call(
        kernel,
        out_shape=outs,
        in_specs=specs or [VMEM] * len(args),
        scratch_shapes=list(scratch),
        compiler_params=pltpu.CompilerParams(vmem_limit_bytes=limit * MIB),
        cost_estimate=pl.CostEstimate(flops=flops, bytes_accessed=6 << 20, transcendentals=0),
        **extra,
    )(*args)


def paired(first, second):
    left = lax.broadcasted_iota(jnp.int32, first.shape, 1) < 64
    return (
        jnp.where(left, first, pltpu.roll(second, 64, axis=1)),
        jnp.where(left, pltpu.roll(first, 64, axis=1), second),
    )


def send_pencils(local, section, sections, halves, mps, sorting):
    batches, features, tokens = local.shape
    count, part, rows = batches // halves, tokens // sections // mps, features // 2
    out = shape((halves * mps, count * rows, 2 * part), local.dtype)
    if part != 64 or mps % 2:
        own = local.reshape(halves, count, 2, rows, mps, part, sections)
        own = lax.dynamic_index_in_dim(own, section, 6, keepdims=False)
        return own.transpose(0, 4, 1, 3, 2, 5).reshape(out.shape)
    sorting = sorting.reshape(tokens, sections, tokens // sections).transpose(1, 0, 2)

    def kernel(section_ref, x_ref, sorting_ref, o_ref):
        for seq in range(batches):
            half, m = seq // count, seq % count
            values = mm(x_ref[seq], sorting_ref[0])
            for place in range(0, mps, 2):
                a = place * part
                pair = paired(values[:rows, a : a + 128], values[rows:, a : a + 128])
                for k in range(2):
                    d = half * mps + place + k
                    o_ref[d, m * rows : (m + 1) * rows] = pair[k].astype(BF)

    return pl.pallas_call(
        kernel,
        grid_spec=pltpu.PrefetchScalarGridSpec(
            num_scalar_prefetch=1,
            grid=(1,),
            in_specs=[
                pl.BlockSpec(local.shape, lambda i, s: (0, 0, 0)),
                pl.BlockSpec((1,) + sorting.shape[1:], lambda i, s: (s[0], 0, 0)),
            ],
            out_specs=pl.BlockSpec(out.shape, lambda i, s: (0, 0, 0)),
        ),
        out_shape=out,
        compiler_params=pltpu.CompilerParams(vmem_limit_bytes=57 * MIB),
    )(section.reshape(1), local, sorting)


def take_pencils(got, halves, mps, count, packed=None):
    rows, part = got.shape[1] // count, got.shape[2] // 2
    width, columns = mps * 2 * rows, count * halves * part
    if part != 64:
        got = got.reshape(halves, mps, count, rows, 2, part)
        low = got.transpose(1, 4, 3, 2, 0, 5).reshape(width, columns)
        return low, None if packed is None else mm(packed, low).astype(BF)

    def kernel(*refs):
        x_ref, o_ref = refs[0], refs[1 if packed is None else 2]
        for mp in range(mps):
            for m in range(count):
                pair = paired(
                    *(x_ref[h * mps + mp, m * rows : (m + 1) * rows].astype(F32) for h in range(2))
                )
                for k in range(2):
                    a = (mp * 2 + k) * rows
                    o_ref[a : a + rows, m * 128 : (m + 1) * 128] = pair[k].astype(BF)
        if packed is not None:
            refs[3][...] = mm(refs[1][...], o_ref[...]).astype(BF)

    low = shape((width, columns))
    if packed is None:
        return call(kernel, low, (got,)), None
    return call(kernel, (low, low), (got, packed))


def send_blocks(layers, extra, sections, halves, mps, count, part):
    width, columns = layers[0].shape
    rows = width // mps // 2
    more = extra.shape[1]
    out = shape((sections * halves * mps, count * rows + more, 2 * part))
    if part != 64:
        sent = jnp.stack(layers).reshape(sections, mps, 2, rows, count, halves, part)
        sent = sent.transpose(0, 5, 1, 4, 3, 2, 6).reshape(-1, count * rows, 2 * part)
        return jnp.concatenate([sent, extra], axis=1)

    def kernel(*refs):
        o_ref = refs[-1]
        o_ref[:, count * rows :] = refs[sections][...]
        for layer in range(sections):
            for mp in range(mps):
                for m in range(count):
                    a, b = mp * 2 * rows, m * 128
                    pair = paired(
                        refs[layer][a : a + rows, b : b + 128].astype(F32),
                        refs[layer][a + rows : a + 2 * rows, b : b + 128].astype(F32),
                    )
                    for k in range(2):
                        d = (layer * halves + k) * mps + mp
                        o_ref[d, m * rows : (m + 1) * rows] = pair[k].astype(BF)

    return call(kernel, out, (*layers, extra))


def take_blocks(got, rows, sections, halves, mps, count, unsorting):
    part = got.shape[2] // 2
    out = (1, halves * count, 2 * rows, sections * mps * part)
    if part != 64 or mps % 2:
        got = got[:, : count * rows].reshape(sections, halves, mps, count, rows, 2, part)
        return got.transpose(1, 3, 5, 4, 2, 6, 0).reshape(out).astype(F32)
    got = got.reshape(sections, halves, mps, got.shape[1], 128)

    def kernel(x_ref, table_ref, o_ref, s_ref):
        for x in range(sections):
            for place in range(0, mps, 2):
                a = x * mps * part + place * part
                for m in range(count):
                    pair = paired(
                        *(
                            x_ref[x, 0, place + k, m * rows : (m + 1) * rows].astype(F32)
                            for k in range(2)
                        )
                    )
                    for k in range(2):
                        s_ref[(2 * m + k) * rows : (2 * m + k + 1) * rows, a : a + 128] = pair[
                            k
                        ].astype(BF)
        for m in range(count):
            o_ref[0, m] = mm(s_ref[2 * m * rows : 2 * (m + 1) * rows], table_ref[...])

    return pl.pallas_call(
        kernel,
        grid=(halves,),
        in_specs=[
            pl.BlockSpec((sections, 1, mps, got.shape[3], 128), lambda i: (0, i, 0, 0, 0)),
            pl.BlockSpec(unsorting.shape, lambda i: (0, 0)),
        ],
        out_specs=pl.BlockSpec((1, count) + out[2:], lambda i: (i, 0, 0, 0)),
        out_shape=shape((halves, count) + out[2:], F32),
        scratch_shapes=[pltpu.VMEM((count * 2 * rows, out[3]), BF)],
        compiler_params=pltpu.CompilerParams(vmem_limit_bytes=57 * MIB),
    )(got, unsorting).reshape(out)


def token_transform(data, mask, cos, sin, count):
    group, rows, columns = data.shape
    length, spread = cos.shape
    tokens = columns // count
    part = tokens // 2
    if part != 64:
        x = data.reshape(group, rows, count, tokens).transpose(2, 1, 0, 3)
        x = x.reshape(count * rows, length)
        mixed = [
            jnp.where(mask > 0.0, mm(x[:, a:b], cos[a:b]), mm(x[:, a:b], sin[a:b]))
            for a, b in ((0, spread), (spread, length))
        ]
        both = jnp.stack([mixed[0] + mixed[1], mixed[0] - mixed[1]]).astype(BF)
        both = both.reshape(2, count, rows, group, part).transpose(3, 2, 1, 0, 4)
        return both.reshape(data.shape)
    step = 256

    def kernel(d_ref, m_ref, c_hbm, s_hbm, o_ref, x_ref, c_ref, s_ref, sems):
        copies = []
        for n in range(spread // step):
            window = slice(n * step, (n + 1) * step)
            copies.append(
                [
                    pltpu.make_async_copy(src.at[:, window], dst.at[n], sems.at[n, k])
                    for k, (src, dst) in enumerate(((c_hbm, c_ref), (s_hbm, s_ref)))
                ]
            )
            for copy in copies[-1]:
                copy.start()
        for m in range(count):
            for g in range(group):
                x_ref[m * rows : (m + 1) * rows, g * tokens : (g + 1) * tokens] = d_ref[
                    g, :, m * tokens : (m + 1) * tokens
                ]
        keep = m_ref[...] > 0.0
        for n in range(spread // step):
            for copy in copies[n]:
                copy.wait()
            even, odd = (
                jnp.where(
                    keep,
                    mm(x_ref[:, a : a + spread], c_ref[n, a : a + spread]),
                    mm(x_ref[:, a : a + spread], s_ref[n, a : a + spread]),
                )
                for a in (0, spread)
            )
            total, other = even + odd, even - odd
            for p in range(step // 128):
                pair = paired(total[:, p * 128 : (p + 1) * 128], other[:, p * 128 : (p + 1) * 128])
                for k in range(2):
                    g = n * (step // part) + 2 * p + k
                    low = pair[k].astype(BF)
                    for m in range(count):
                        o_ref[g, :, m * tokens : (m + 1) * tokens] = low[m * rows : (m + 1) * rows]

    return call(
        kernel,
        shape(data.shape),
        (data, mask, cos, sin),
        [VMEM, VMEM, HBM, HBM],
        [pltpu.VMEM((count * rows, length), BF)]
        + [pltpu.VMEM((spread // step, length, step), BF)] * 2
        + [pltpu.SemaphoreType.DMA((spread // step, 2))],
        limit=57,
        flops=4 * count * rows * length * spread,
    )


def standardize(values):
    average = jnp.mean(values, axis=0, keepdims=True)
    centered = values - average
    spread = jnp.mean(centered * centered, axis=0, keepdims=True)
    inverse = lax.rsqrt(spread + EPSILON)
    return centered * inverse, inverse


def norm_back(upstream, standard, inverse, scaling):
    weighted = upstream * scaling
    return inverse * (
        weighted
        - jnp.mean(weighted, axis=0, keepdims=True)
        - standard * jnp.mean(weighted * standard, axis=0, keepdims=True)
    )


def column(table_ref, layer, i):
    k = layer * 5 + i
    return table_ref[:, k : k + 1]


def first_norm(got, low, unpack, factor, table, layer):
    width, columns = low.shape

    def kernel(r_ref, x_ref, unpack_ref, table_ref, unit_ref, inverse_ref, low_ref):
        mixed = mm(unpack_ref[...], r_ref[...])
        gain, shift = column(table_ref, layer, 1), column(table_ref, layer, 2)
        for a, b in blocks(columns, 128):
            unit, inverse = standardize(x_ref[:, a:b].astype(F32) + mixed[:, a:b] * factor)
            unit_ref[:, a:b] = unit.astype(BF)
            inverse_ref[:, a:b] = inverse
            low_ref[:, a:b] = (unit * gain + shift).astype(BF)

    outs = (shape((width, columns)), shape((1, columns), F32), shape((width, columns)))
    return call(kernel, outs, (got, low, unpack, table), flops=2 * width * width * columns)


def second_norm(unit1, parts, table, layer, labels, scored, packed):
    width, columns = unit1.shape
    count = len(parts)

    def kernel(*refs):
        unit1_ref, part_refs = refs[0], refs[1 : 1 + count]
        table_ref, labels_ref, scored_ref = refs[1 + count : 4 + count]
        bias, gain1, shift1, gain2, shift2 = (column(table_ref, layer, i) for i in range(5))
        bias = bias + shift1
        unit_ref, inverse_ref, low_ref, hits_ref = refs[len(refs) - outs_count :][:4]
        for a, b in blocks(columns, 128):
            values = unit1_ref[:, a:b].astype(F32) * gain1 + bias
            for part in part_refs:
                values = values + part[:, a:b].astype(F32)
            unit, inverse = standardize(values)
            unit_ref[:, a:b] = unit.astype(BF)
            inverse_ref[:, a:b] = inverse
            out = unit * gain2 + shift2
            low_ref[:, a:b] = out.astype(BF)
            exponent = jnp.exp(out)
            match = lax.broadcasted_iota(jnp.int32, out.shape, 0) == labels_ref[:, a:b]
            picked = jnp.sum(jnp.where(match, exponent, 0.0), axis=0, keepdims=True)
            total = jnp.sum(exponent, axis=0, keepdims=True)
            hits_ref[:, a:b] = picked / total * scored_ref[:, a:b]
        if packed is not None:
            refs[-1][...] = mm(refs[4 + count][...], low_ref[...]).astype(BF)

    row = shape((1, columns), F32)
    outs = [shape((width, columns)), row, shape((width, columns)), row]
    args = [unit1, *parts, table, labels, scored]
    if packed is not None:
        outs, args = outs + [shape((width, columns))], args + [packed]
    outs_count = len(outs)
    return call(kernel, tuple(outs), tuple(args), flops=2 * width * width * columns)


def row_sums(terms, width):
    total = jnp.zeros((8, width), F32)
    for row, term in terms:
        mark = (lax.broadcasted_iota(jnp.int32, (8, term.shape[1]), 0) == row).astype(BF)
        total = total + mm_nt(mark, term)
    return total


def second_back(up, unit, inverse, table, layer, mix=None):
    width, columns = unit.shape

    def kernel(*refs):
        up_ref, unit_ref, inverse_ref, table_ref = refs[:4]
        if mix is None:
            low_ref, sums_ref, product_ref = refs[4:]
            source_ref = up_ref
        else:
            got_ref, unpack_ref, low_ref, sums_ref, source_ref, product_ref = refs[4:]
            mixed = mm(unpack_ref[...], got_ref[...])
        gain = column(table_ref, layer, 3)
        for a, b in blocks(columns, 128):
            if mix is not None:
                values = up_ref[:, a:b].astype(F32) + mixed[:, a:b] * mix[2]
                source_ref[:, a:b] = values.astype(BF)
            values, unit = source_ref[:, a:b].astype(F32), unit_ref[:, a:b].astype(F32)
            low_ref[:, a:b] = norm_back(values, unit, inverse_ref[:, a:b], gain).astype(BF)
            product_ref[:, a:b] = (values * unit).astype(BF)
        sums_ref[...] = row_sums(
            ((0, low_ref[...]), (3, product_ref[...]), (4, source_ref[...])), width
        )

    outs = (shape(unit.shape), shape((8, width), F32))
    args = (up, unit, inverse, table)
    if mix is not None:
        outs, args = outs + (shape(unit.shape),), args + mix[:2]
    scratch = [pltpu.VMEM(unit.shape, BF)]
    return call(kernel, outs, args, None, scratch, flops=2 * width * width * columns)


def first_back(grad_second, parts, unit, inverse, table, layer, packed):
    width, columns = unit.shape
    count = len(parts)

    def kernel(second_ref, *refs):
        part_refs = refs[:count]
        unit_ref, inverse_ref, table_ref, packed_ref = refs[count : count + 4]
        low_ref, sums_ref, sent_ref, product_ref, normed_ref = refs[count + 4 :]
        gain = column(table_ref, layer, 1)
        for a, b in blocks(columns, 128):
            values, unit = second_ref[:, a:b].astype(F32), unit_ref[:, a:b].astype(F32)
            for part in part_refs:
                values = values + part[:, a:b].astype(F32)
            low_ref[:, a:b] = norm_back(values, unit, inverse_ref[:, a:b], gain).astype(BF)
            product_ref[:, a:b] = (values * unit).astype(BF)
            normed_ref[:, a:b] = values.astype(BF)
        sent_ref[...] = mm(packed_ref[...], low_ref[...]).astype(BF)
        sums_ref[...] = row_sums(((1, product_ref[...]), (2, normed_ref[...])), width)

    outs = (shape(unit.shape), shape((8, width), F32), shape(unit.shape))
    args = (grad_second, *parts, unit, inverse, table, packed)
    scratch = [pltpu.VMEM(unit.shape, BF)] * 2
    return call(kernel, outs, args, None, scratch, flops=2 * width * width * columns)


def last_mix(got, grad, unpack, factor):
    width, columns = grad.shape

    def kernel(got_ref, grad_ref, unpack_ref, o_ref):
        mixed = mm(unpack_ref[...], got_ref[...])
        o_ref[...] = (grad_ref[...].astype(F32) + mixed * factor).astype(BF)

    args = (got, grad, unpack)
    return call(kernel, shape(grad.shape), args, flops=2 * width * width * columns)


def gelu_parts(x):
    cdf = 0.5 + 0.5 * lax.erf(x * (1.0 / math.sqrt(2.0)))
    return cdf, jnp.exp(-0.5 * x * x) * (1.0 / math.sqrt(2.0 * math.pi))


def mm_tn(left, right):
    return lax.dot_general(left, right, (((0,), (0,)), ((), ())), preferred_element_type=F32)


def staged(pairs, sems):
    copies = [
        pltpu.make_async_copy(src, dst, sems.at[i]) for i, (src, dst) in enumerate(pairs)
    ]
    for copy in copies:
        copy.start()
    return copies


def chosen(flag, pairs, sems):
    copies = []
    for i, (sources, target) in enumerate(pairs):
        either = [pltpu.make_async_copy(src, target, sems.at[i]) for src in sources]

        @pl.when(flag == 1)
        def _():
            either[0].start()

        @pl.when(flag != 1)
        def _():
            either[1].start()

        copies.append(either[0])
    return copies


def ffn(flag, first, second, own, other, biases, layer):
    width, columns = first.shape
    units = own[0].shape[0]
    steps = blocks(units, 256)

    def kernel(flag_ref, a_ref, b_ref, own1, own2, other1, other2, bias_ref, *refs):
        oa_ref, ob_ref, act_hbm, slope_hbm, one_ref, two_ref, act_ref, slope_ref, sems, sent = refs
        copies = chosen(
            flag_ref[0],
            [((own1.at[a:b], other1.at[a:b]), one_ref.at[a:b]) for a, b in steps]
            + [((own2, other2), two_ref)],
            sems,
        )
        x = jnp.concatenate([a_ref[...], b_ref[...]], axis=1)
        writes = []
        for i, (a, b) in enumerate(steps):
            copies[i].wait()
            hidden = mm(one_ref[a:b], x) + bias_ref[a:b, layer : layer + 1]
            cdf, density = gelu_parts(hidden)
            act_ref[a:b] = (hidden * cdf).astype(BF)
            slope_ref[a:b] = (cdf + hidden * density).astype(BF)
            for k, (src, dst) in enumerate(((act_ref, act_hbm), (slope_ref, slope_hbm))):
                writes.append(pltpu.make_async_copy(src.at[a:b], dst.at[a:b], sent.at[i, k]))
                writes[-1].start()
        copies[-1].wait()
        for a, b in blocks(width, 256):
            part = mm(two_ref[a:b], act_ref[...])
            oa_ref[a:b] = part[:, :columns].astype(BF)
            ob_ref[a:b] = part[:, columns:].astype(BF)
        for write in writes:
            write.wait()

    half, full = shape((width, columns)), shape((units, 2 * columns))
    return call(
        kernel,
        (half, half, full, full),
        (flag, first, second, *own, *other, biases),
        [SMEM] + [VMEM] * 2 + [HBM] * 4 + [VMEM],
        [
            pltpu.VMEM((units, width), BF),
            pltpu.VMEM((width, units), BF),
            pltpu.VMEM(full.shape, BF),
            pltpu.VMEM(full.shape, BF),
            pltpu.SemaphoreType.DMA((len(steps) + 1,)),
            pltpu.SemaphoreType.DMA((len(steps), 2)),
        ],
        limit=57,
        flops=8 * width * units * columns,
        out_specs=(VMEM, VMEM, HBM, HBM),
    )


def ffn_back(flag, first, second, own, other, slope):
    width, columns = first.shape
    units = own[0].shape[0]
    steps = blocks(units, 256)

    def kernel(flag_ref, a_ref, b_ref, own1, own2, other1, other2, slope_hbm, *refs):
        oa_ref, ob_ref, pre_hbm, sums_ref, one_ref, two_ref, pre_ref, slope_ref, sems, sent = refs
        copies = chosen(
            flag_ref[0],
            [((own2, other2), two_ref)]
            + [((slope_hbm.at[a:b],) * 2, slope_ref.at[a:b]) for a, b in steps]
            + [((own1, other1), one_ref)],
            sems,
        )
        g = jnp.concatenate([a_ref[...], b_ref[...]], axis=1)
        copies[0].wait()
        writes = []
        for i, (a, b) in enumerate(steps):
            grad = mm_tn(two_ref[:, a:b], g)
            copies[1 + i].wait()
            pre_ref[a:b] = (grad * slope_ref[a:b].astype(F32)).astype(BF)
            writes.append(pltpu.make_async_copy(pre_ref.at[a:b], pre_hbm.at[a:b], sent.at[i]))
            writes[-1].start()
        copies[-1].wait()
        for a, b in blocks(width, 256):
            part = mm_tn(one_ref[:, a:b], pre_ref[...])
            oa_ref[a:b] = part[:, :columns].astype(BF)
            ob_ref[a:b] = part[:, columns:].astype(BF)
        sums_ref[...] = row_sums(((0, pre_ref[...]),), units)
        for write in writes:
            write.wait()

    half, full = shape((width, columns)), shape((units, 2 * columns))
    return call(
        kernel,
        (half, half, full, shape((8, units), F32)),
        (flag, first, second, *own, *other, slope),
        [SMEM] + [VMEM] * 2 + [HBM] * 5,
        [
            pltpu.VMEM((units, width), BF),
            pltpu.VMEM((width, units), BF),
            pltpu.VMEM(full.shape, BF),
            pltpu.VMEM(full.shape, BF),
            pltpu.SemaphoreType.DMA((len(steps) + 2,)),
            pltpu.SemaphoreType.DMA((len(steps),)),
        ],
        limit=57,
        flops=8 * width * units * columns,
        out_specs=(VMEM, VMEM, HBM, VMEM),
    )


def weight_grads(flag, xs, pres, gs, acts):
    units, width = pres[0].shape[0], xs[0].shape[0]
    tokens = sum(p.shape[1] for p in pres)
    groups = (gs, acts, pres, xs)
    sizes = [len(group) for group in groups]

    def kernel(flag_ref, *refs):
        inputs, rest = refs[: sum(sizes)], refs[sum(sizes) :]
        keep_hbm, give_hbm, one_ref, two_ref = rest[:4]
        scratch, sems, sent = rest[4:8], rest[8], rest[9]
        pairs, ends, k = [], [], 0
        for size, whole in zip(sizes, scratch):
            at = 0
            for _ in range(size):
                step = inputs[k].shape[1]
                pairs.append((inputs[k], whole.at[:, at : at + step]))
                at, k = at + step, k + 1
            ends.append(k)
        copies = staged(pairs, sems)

        def put(src, first, second, sem):
            either = [pltpu.make_async_copy(src, dst, sem) for dst in (first, second)]

            @pl.when(flag_ref[0] == 1)
            def _():
                either[0].start()

            @pl.when(flag_ref[0] != 1)
            def _():
                either[1].start()

            return either[0]

        for copy in copies[: ends[1]]:
            copy.wait()
        for a, b in blocks(width, 256):
            two_ref[a:b] = mm_nt(scratch[0][a:b], scratch[1][...]).astype(BF)
        writes = [put(two_ref, give_hbm, keep_hbm, sent.at[0])]
        for copy in copies[ends[1] :]:
            copy.wait()
        for a, b in blocks(units, 256):
            one_ref[a:b] = mm_nt(scratch[2][a:b], scratch[3][...]).astype(BF)
        writes.append(put(one_ref, keep_hbm, give_hbm, sent.at[1]))
        for write in writes:
            write.wait()

    if units != width:
        pre, x, g, act = (jnp.concatenate(group, axis=1) for group in (pres, xs, gs, acts))
        one, two = mm_nt(pre, x).astype(BF), mm_nt(g, act).astype(BF).reshape(units, width)
        return jnp.where(flag == 1, one, two), jnp.where(flag == 1, two, one)
    return call(
        kernel,
        (shape((units, width)),) * 2,
        (flag, *gs, *acts, *pres, *xs),
        [SMEM] + [HBM] * sum(sizes),
        [pltpu.VMEM((units, width), BF)] * 2
        + [pltpu.VMEM((rows, tokens), BF) for rows in (width, units, units, width)]
        + [pltpu.SemaphoreType.DMA((sum(sizes),)), pltpu.SemaphoreType.DMA((2,))],
        limit=57,
        flops=4 * width * units * tokens,
        out_specs=(HBM, HBM),
    )


def widened(gathered):
    planes, _, rows, width = gathered.shape

    def kernel(x_hbm, one_hbm, two_hbm, in_ref, out_ref, sems, sent):
        order = [(p, k) for k in range(2) for p in range(planes)]
        copies = [
            pltpu.make_async_copy(x_hbm.at[p, k], in_ref.at[p, k], sems.at[p, k]) for p, k in order
        ]
        for copy in copies:
            copy.start()
        writes = []
        for copy, (p, k) in zip(copies, order):
            copy.wait()
            out_ref[p, k] = in_ref[p, k].astype(F32)
            target = (one_hbm, two_hbm)[k].at[p * rows : (p + 1) * rows]
            writes.append(pltpu.make_async_copy(out_ref.at[p, k], target, sent.at[p, k]))
            writes[-1].start()
        for write in writes:
            write.wait()

    return call(
        kernel,
        (shape((planes * rows, width), F32),) * 2,
        (gathered,),
        [HBM],
        [
            pltpu.VMEM(gathered.shape, BF),
            pltpu.VMEM(gathered.shape, F32),
            pltpu.SemaphoreType.DMA((planes, 2)),
            pltpu.SemaphoreType.DMA((planes, 2)),
        ],
        out_specs=(HBM, HBM),
    )


def shards(
    inputs,
    cotangent,
    labels,
    scored,
    expand_weight,
    expand_bias,
    reduce_weight,
    reduce_bias,
    first_gain,
    first_shift,
    second_gain,
    second_shift,
):
    batches, feature_count, token_count = inputs.shape
    sections, halves, rests, sides, cores = (lax.axis_size(axis) for axis in AXES)
    mps = sides * cores
    group = sections * rests * mps
    width = feature_count * mps
    length = token_count * halves * rests
    units = expand_weight.shape[1]
    count = batches // halves
    part = token_count // sections // mps
    columns = count * halves * part
    rows = width // group
    factor = 1.0 / math.sqrt(length * width)
    section, half, rest, side, core = (lax.axis_index(axis) for axis in AXES)
    mp_index = side * cores + core
    is_first = section == 0

    packed, unpack = (jnp.asarray(t) for t in feature_tables(width, group))
    token_cos, token_sin = (jnp.asarray(t) for t in token_tables(sections, rests, mps, part))
    sorting = sorting_table(sections, token_count)
    unsorting, sorting = jnp.asarray(sorting.T), jnp.asarray(sorting)
    row_ids = jnp.arange(count * rows, dtype=jnp.int32) % rows
    corner = (section == 0) & (rest == 0) & (mp_index == 0)
    mask = (row_ids < rows // 2) | ((row_ids == rows // 2) & corner)
    mask = mask.astype(F32)[:, None]

    def swapped(array, axis, by=1):
        size = lax.axis_size(axis)
        return lax.ppermute(array, axis, [(i, (i + by) % size) for i in range(size)])

    own_one, own_two = expand_weight[0], reduce_weight[0]
    other_one, other_two = swapped(own_one, "section"), swapped(own_two, "section")

    def ordered(own, other):
        return [jnp.where(is_first, own, other), jnp.where(is_first, other, own)]

    small = [expand_bias, reduce_bias, first_gain, first_shift, second_gain, second_shift]
    small = jnp.concatenate([vector[0] for vector in small])
    small = jnp.stack(ordered(small, swapped(small, "section")))
    biases, vectors = small[:, :units].T, small[:, units:].reshape(sections * 5, 1, feature_count)
    vectors = jnp.concatenate(ordered_by(core, vectors, swapped(vectors, "core")), axis=1)
    chips = [swapped(vectors, "side", -j) if j else vectors for j in range(sides)]
    chips = jnp.stack(chips, axis=1)
    order = [(i - side) % sides for i in range(sides)]
    table = jnp.stack(
        [lax.dynamic_index_in_dim(chips, i, 1, keepdims=False) for i in order], axis=1
    ).reshape(sections * 5, width)
    table = jnp.pad(table, ((0, -table.shape[0] % 16), (0, 0))).T

    def to_pencils(local, table=None, *others):
        sent = send_pencils(local, section, sections, halves, mps, sorting)
        got = lax.all_to_all(sent, PLANE, 0, 0, tiled=True)
        if others:
            got, others = lax.optimization_barrier((got, others))
        return *take_pencils(got, halves, mps, count, table), *others

    def to_blocks(layers, extra):
        sent = send_blocks(layers, extra, sections, halves, mps, count, part)
        got = lax.all_to_all(sent, SQUARE, 0, 0, tiled=True)
        most = got.shape[1] - extra.shape[1]
        small = jnp.sum(got[:, most:].astype(F32), axis=0).reshape(-1)
        return got, small, sent

    def from_blocks(got):
        rows = feature_count // 2
        return take_blocks(got, rows, sections, halves, mps, count, unsorting)

    def fourier(sent, *others):
        sent = sent.reshape(group, rows, columns)
        got = lax.all_to_all(sent, RING, 0, 0, tiled=True)
        mixed = token_transform(got, mask, token_cos, token_sin, count)
        if others:
            mixed, others = lax.optimization_barrier((mixed, others))
        mixed = lax.all_to_all(mixed, RING, 0, 0, tiled=True).reshape(width, columns)
        return (mixed, *others) if others else mixed

    def gathered(own):
        return [own] + [swapped(own, "side", j) for j in range(1, sides)]

    def reduced(parts):
        terms = [parts[0][0], swapped(parts[0][1], "core")]
        for j in range(1, sides):
            keep, give = parts[j]
            chip = keep.astype(F32) + swapped(give, "core").astype(F32)
            terms.append(swapped(chip.astype(BF), "side", -j))
        return terms

    def added(first, second):
        return (first.astype(F32) + second.astype(F32)).astype(BF)

    def scattered(array):
        return lax.psum_scatter(array, ("half", "rest"), scatter_dimension=0, tiled=True)

    def in_turn(step, firsts):
        done, pairs = [], []
        for i, first in enumerate(firsts):
            if done:
                first, done[-1] = lax.optimization_barrier((first, done[-1]))
            pairs.append((first, swapped(first, "core")))
            done.append(step(*pairs[-1], i))
        return done, pairs

    marks = 2 * labels + scored
    marks = jnp.stack(ordered_by(half, marks, swapped(marks, "half")))
    marks = lax.dynamic_slice_in_dim(marks, half * count, count, 1)
    marks = marks.reshape(halves, count, mps, part, sections)
    marks = lax.dynamic_index_in_dim(marks, section, 4, keepdims=False)
    marks = lax.dynamic_index_in_dim(marks, mp_index, 2, keepdims=False)
    marks = marks.transpose(1, 0, 2).reshape(1, columns)
    local_labels, local_scored = marks // 2, (marks % 2).astype(F32)

    low, sent, other_one = to_pencils(inputs, packed, other_one)
    flags = [is_first.astype(jnp.int32).reshape(1), (1 - is_first.astype(jnp.int32)).reshape(1)]
    saved, outs, hits = [], [], jnp.zeros((), F32)
    for layer in range(2):
        if layer == 0:
            mixed, other_two, table, biases = fourier(sent, other_two, table, biases)
        else:
            mixed = fourier(sent)
        unit1, inv1, normed = first_norm(mixed, low, unpack, factor, table, layer)
        runs, xs = in_turn(
            lambda a, b, i: ffn(
                flags[layer], a, b, (own_one, own_two), (other_one, other_two), biases, layer
            ),
            gathered(normed),
        )
        terms = reduced([run[:2] for run in runs])
        if layer == 0:
            up, _ = lax.optimization_barrier((cotangent, runs[-1][0]))
            up = to_pencils(up)[0]
            terms, up = lax.optimization_barrier((terms, up))
        result = second_norm(
            unit1,
            terms,
            table,
            layer,
            local_labels,
            local_scored,
            packed if layer == 0 else None,
        )
        unit2, inv2, low, hit = result[:4]
        sent = result[-1]
        outs.append(low)
        hits = hits + jnp.sum(hit)
        saved.append((unit1, inv1, xs, runs, unit2, inv2))
    lanes = 2 * part
    outputs = to_blocks(outs, jnp.zeros((sections * halves * mps, 16, lanes), BF))[0]

    grads_in, weights_out, smalls, bias_rows = [None, None], [None, None], [None, None], [None, None]
    mix = None
    for layer in (1, 0):
        unit1, inv1, xs, runs, unit2, inv2 = saved[layer]
        result = second_back(up, unit2, inv2, table, layer, mix)
        grad_low, sums2 = result[:2]
        if mix is not None:
            grads_in[1] = result[2]
        backs, gs = in_turn(
            lambda a, b, i: ffn_back(
                flags[layer], a, b, (own_one, own_two), (other_one, other_two), runs[i][3]
            ),
            gathered(grad_low),
        )
        if layer == 0:
            late, _ = lax.optimization_barrier((late, backs[-1][0]))
            weights_out[1] = scattered(added(*late))
        terms = reduced([back[:2] for back in backs])
        keep, give = weight_grads(
            flags[0],
            [x for pair in xs for x in pair],
            [back[2] for back in backs],
            [g for pair in gs for g in pair],
            [run[2] for run in runs],
        )
        terms, keep, give = lax.optimization_barrier((terms, keep, give))
        if layer == 1:
            terms, outputs = lax.optimization_barrier((terms, outputs))
        up, sums1, sent = first_back(grad_low, terms, unit1, inv1, table, layer, packed)
        if layer == 1:
            mixed = fourier(sent)
            give, _ = lax.optimization_barrier((give, mixed))
            late = (keep, swapped(give, "section"))
        else:
            taken = swapped(give, "section")
            mixed, weights_out[1] = fourier(sent, weights_out[1])
            taken, _ = lax.optimization_barrier((taken, mixed))
            both = added(keep, taken)
            both, _ = lax.optimization_barrier((both, weights_out[1]))
            weights_out[0] = scattered(both)
        mix = (mixed, unpack, factor)
        smalls[layer] = sums1 + sums2
        bias_rows[layer] = sum(back[3][0] for back in backs)
    grads_in[0] = last_mix(mix[0], up, unpack, factor)

    high = hits.astype(BF)
    middle = (hits - high.astype(F32)).astype(BF)
    lowest = (hits - high.astype(F32) - middle.astype(F32)).astype(BF)
    counted = jnp.stack([high, middle, lowest])
    per = 5 * feature_count
    rows_of = []
    for layer in range(sections):
        vectors_of = smalls[layer][:5].reshape(5, mps, feature_count).transpose(1, 0, 2)
        mine = jnp.arange(mps, dtype=jnp.int32)[:, None] == mp_index
        rows_of.append(
            jnp.concatenate(
                [
                    vectors_of.reshape(mps, per).astype(BF),
                    jnp.where(mine, bias_rows[layer][None], 0.0).astype(BF),
                    jnp.broadcast_to(counted[None], (mps, 3)),
                ],
                axis=1,
            )
        )
    extra = jnp.stack(rows_of)
    extra = jnp.pad(extra, ((0, 0), (0, 0), (0, -extra.shape[2] % (8 * lanes))))
    extra = jnp.broadcast_to(extra[:, None], (sections, halves) + extra.shape[1:])
    got, small, sent = to_blocks(grads_in, extra.reshape(sections * halves * mps, -1, lanes))
    input_grads = from_blocks(got)
    outputs = from_blocks(outputs)
    small, step = small.reshape(-1, lanes), 1
    while step < rests:
        small = small + lax.ppermute(small, "rest", [(i, i ^ step) for i in range(rests)])
        step *= 2
    small = small.reshape(-1)
    features = small[:per].reshape(5, feature_count)
    bias_sum = small[per : per + units]
    accuracy = jnp.sum(small[per + units : per + units + 3])

    early, late = weights_out
    early, late, _ = lax.optimization_barrier((early, late, got))
    mine, other = jnp.where(is_first, early, late), jnp.where(is_first, late, early)
    other = swapped(other, "section")
    pair = jnp.stack(ordered(mine, other))
    pair = lax.all_gather(pair, ("half", "rest"), axis=0, tiled=False)
    one, two = widened(pair.reshape((-1,) + pair.shape[-3:]))
    weight_sums = [one, two.reshape(width, units)]

    return (
        outputs,
        input_grads,
        weight_sums[0][None],
        bias_sum[None],
        weight_sums[1][None],
        features[0][None],
        features[1][None],
        features[2][None],
        features[3][None],
        features[4][None],
        accuracy,
    )


def ordered_by(index, own, other):
    return [jnp.where(index == 0, own, other), jnp.where(index == 0, other, own)]


def solution(mesh):
    sizes = mesh.shape
    dims = (sizes["section"], 2, sizes["seq"] // 2, sizes["mp"] // 2, 2)
    names = ("section", ("half", "rest"), ("side", "core"))
    section, seq, mp = names
    placed = (
        P(None, mp, seq),
        P(None, mp, seq),
        P(None, seq),
        P(None, seq),
        P(section, mp, None),
        P(section, mp),
        P(section, None, mp),
        P(section, mp),
        P(section, mp),
        P(section, mp),
        P(section, mp),
        P(section, mp),
    )
    return jax.shard_map(
        shards,
        mesh=Mesh(mesh.devices.reshape(dims), AXES),
        in_specs=placed,
        out_specs=(
            P(section, None, mp, seq),
            P(section, None, mp, seq),
            P(section, mp, None),
            P(section, mp),
            P(section, None, mp),
            P(section, mp),
            P(section, mp),
            P(section, mp),
            P(section, mp),
            P(section, mp),
            P(),
        ),
        check_vma=False,
    )
```

time: 2050 us -> 585 us (0.29)
  blocking collectives: 907 us -> 133 us
  matrix products: 649 us -> 0 us
  Pallas kernels: 0 us -> 160 us
  waiting for transfers between devices: 314 us -> 188 us
  other arithmetic: 101 us -> 13.6 us
    all_gather x56 -> x0, blocking collectives: 705 us -> none  [the longest x7 145 us: shards(): lax.all_gather(grad_first.astype(jnp.bfloat16), 'seq', axis=1, tiled=True)]
    dot_general x98 -> x0, matrix products: 649 us -> none  [the longest x7 114 us: shards(): jnp.dot(back_pieces, token_cos, preferred_element_type=jnp.float32)]
    reduce_scatter x14 -> x2, waiting for transfers between devices: 252 us -> 0.02 us  [scattered(): lax.psum_scatter(array, ('half', 'rest'), scatter_dimension=0, tiled=True)]
    psum x30 -> x0, blocking collectives: 202 us -> none  [the longest x28 170 us: row_totals(): return lax.psum((first_rows, second_rows), 'mp')]
    pallas_call x0 -> x32, Pallas kernels: none -> 160 us  [the longest x28 148 us: call(): pl.pallas_call(kernel, out_shape=outs, in_specs=specs or [VMEM] * len(arg...]
    all_to_all x0 -> x6, blocking collectives: none -> 133 us  [the longest x1 54.5 us: to_blocks(): got = lax.all_to_all(sent, SQUARE, 0, 0, tiled=True)]
    all_to_all x0 -> x6, waiting for transfers between devices: none -> 50.7 us  [the longest x2 26 us: to_pencils(): got = lax.all_to_all(sent, PLANE, 0, 0, tiled=True)]
    reduce_sum x29 -> x4, other arithmetic: 49.2 us -> 1.89 us  [the longest x2 1.21 us: shards(): hits = hits + jnp.sum(hit)]
  transfers between devices with their start and end apart: 27 -> 43, of which waited for: 26 -> 29; matrix products, arithmetic and copies ran while one was open for 5% -> 3% of each run, Pallas kernels for 0% -> 18%
where the time goes in v2:
time: 585 us; the launch traced here: 579 us
  waiting for transfers between devices  188 us (32%)
  Pallas kernels  160 us (27%)
  blocking collectives  133 us (23%)
  starting transfers between devices  48.4 us (8%)
  local copies, waits for them, and re-layouts  19.4 us (3%)
  between operations  16.2 us (3%)
  other arithmetic  13.6 us (2%)
    pallas_call x28, Pallas kernels, call(): pl.pallas_call(kernel, out_shape=outs, in_specs=specs or [VMEM] * len(arg...  148 us
    ppermute x33, waiting for transfers between devices, swapped(): lax.ppermute(array, axis, [(i, (i + by) % size) for i in range(size)])  97.8 us
    all_to_all x1, blocking collectives, to_blocks(): got = lax.all_to_all(sent, SQUARE, 0, 0, tiled=True)  54.5 us
    all_to_all x3, blocking collectives, fourier(): lax.all_to_all(mixed, RING, 0, 0, tiled=True).reshape(width, columns)  47.1 us
    all_gather x1, waiting for transfers between devices, shards(): pair = lax.all_gather(pair, ('half', 'rest'), axis=0, tiled=False)  39.2 us
    all_to_all x2, blocking collectives, fourier(): got = lax.all_to_all(sent, RING, 0, 0, tiled=True)  31.4 us
    all_to_all x2, waiting for transfers between devices, to_pencils(): got = lax.all_to_all(sent, PLANE, 0, 0, tiled=True)  26 us
    all_to_all x2, waiting for transfers between devices, fourier(): got = lax.all_to_all(sent, RING, 0, 0, tiled=True)  22.4 us
  transfers between devices with their start and end apart: 43, of which 29 were waited for; matrix products, arithmetic and copies ran while one was open for 3% of the time, Pallas kernels for 18%

profile of v2, /device:TPU:0, one launch (start us, length us, event | category | flops | bytes accessed | tf_op | source)
XLA Modules:
  0.0 578.5 jit_solution(6327042434210730830)
XLA Ops:
  20.1 14.7 %all-to-all-done.refs_0_ = bf16[8,288,128]{2,1,0:T(8,128)(2,1)} async-done(((bf16[8,288,128]{2,1,0:T(8,128)(2,1)}), bf16[8,288,128]{2,1,0:T(8,128)(2,1)}, u32[]{:S(2)}, u32[]{:S(2)}) %all-to-all-start) | async-done | bytes 589856 | tf_op jit(solution)/shard_map/all_to_all | solution.py:762
  53.5 14.7 %all-to-all-done.1.d_ref = bf16[16,48,384]{2,1,0:T(8,128)(2,1)} async-done(((bf16[16,48,384]{2,1,0:T(8,128)(2,1)}), bf16[16,48,384]{2,1,0:T(8,128)(2,1)}, u32[]{:S(2)}, u32[]{:S(2)}) %all-to-all-start.1) | async-done | bytes 589856 | tf_op jit(solution)/shard_map/all_to_all | solution.py:780
  74.3 16.1 %all_to_all.60 = bf16[16,48,384]{2,1,0:T(8,128)(2,1)} all-to-all(bf16[16,48,384]{2,1,0:T(8,128)(2,1)} %shard_map.259), channel_id=1, replica_groups=mesh['section'=2,'half'=2,'rest'=2,'side'=2,'core'=2] {'section','rest',..., dimensions={0} | all-to-all | bytes 1179648 | tf_op jit(solution)/shard_map/all_to_all | solution.py:784
  97.5 6.7 %shard_map.261 = (bf16[768,384]{1,0:T(8,128)(2,1)}, bf16[768,384]{1,0:T(8,128)(2,1)}, bf16[768,768]{1,0:T(8,128)(2,1)}, bf16[768,768]{1,0:T(8,128)(2,1)}) custom-call(s32[1]{0:T(128)} %bitcast.15.flag_ref, bf16[768,384]{1,0:T(8,128)(2,1)} %get-tuple-element.136.a_ref.refs_8_, bf16[768,384]{1,0:T(8,128)(2,1)} %copy-done.42, bf16[768,768]{1,0:T(8,128)(2,1)} %bitcast.62, ...), custom_call_target="tpu_custom_call" | custom-call | flops 1811939328 | bytes 6291456 | tf_op jit(solution)/shard_map/pallas_call | solution.py:92
  113.3 6.7 %shard_map.262 = (bf16[768,384]{1,0:T(8,128)(2,1)}, bf16[768,384]{1,0:T(8,128)(2,1)}, bf16[768,768]{1,0:T(8,128)(2,1)}, bf16[768,768]{1,0:T(8,128)(2,1)}) custom-call(s32[1]{0:T(128)} %bitcast.15.flag_ref, bf16[768,384]{1,0:T(8,128)(2,1)} %copy-done.43, bf16[768,384]{1,0:T(8,128)(2,1)} %copy-done.44, bf16[768,768]{1,0:T(8,128)(2,1)} %bitcast.63, ...), custom_call_target="tpu_custom_call" | custom-call | flops 1811939328 | bytes 6291456 | tf_op jit(solution)/shard_map/pallas_call | solution.py:92
  134.5 11.3 %all-to-all-done.3.refs_0_ = bf16[8,288,128]{2,1,0:T(8,128)(2,1)S(1)} async-done(((bf16[8,288,128]{2,1,0:T(8,128)(2,1)}), bf16[8,288,128]{2,1,0:T(8,128)(2,1)S(1)}, u32[]{:S(2)}, u32[]{:S(2)}) %all-to-all-start.3) | async-done | bytes 589856 | tf_op jit(solution)/shard_map/all_to_all | solution.py:762
  157.0 16.0 %all_to_all.61.d_ref = bf16[16,48,384]{2,1,0:T(8,128)(2,1)} all-to-all(bf16[16,48,384]{2,1,0:T(8,128)(2,1)} %bitcast.92), channel_id=1, replica_groups=mesh['section'=2,'half'=2,'rest'=2,'side'=2,'core'=2] {'section','rest',..., dimensions={0} | all-to-all | bytes 1179648 | tf_op jit(solution)/shard_map/all_to_all | solution.py:780
  179.0 15.5 %all_to_all.62 = bf16[16,48,384]{2,1,0:T(8,128)(2,1)} all-to-all(bf16[16,48,384]{2,1,0:T(8,128)(2,1)} %shard_map.266), channel_id=1, replica_groups=mesh['section'=2,'half'=2,'rest'=2,'side'=2,'core'=2] {'section','rest',..., dimensions={0} | all-to-all | bytes 1179648 | tf_op jit(solution)/shard_map/all_to_all | solution.py:784
  217.3 6.7 %shard_map.269 = (bf16[768,384]{1,0:T(8,128)(2,1)}, bf16[768,384]{1,0:T(8,128)(2,1)}, bf16[768,768]{1,0:T(8,128)(2,1)}, bf16[768,768]{1,0:T(8,128)(2,1)}) custom-call(s32[1]{0:T(128)} %bitcast.21.flag_ref, bf16[768,384]{1,0:T(8,128)(2,1)} %copy-done.46, bf16[768,384]{1,0:T(8,128)(2,1)} %copy-done.47, bf16[768,768]{1,0:T(8,128)(2,1)} %bitcast.65, ...), custom_call_target="tpu_custom_call" | custom-call | flops 1811939328 | bytes 6291456 | tf_op jit(solution)/shard_map/pallas_call | solution.py:92
  227.9 15.1 %collective-permute-done.17.refs_3_ = bf16[768,384]{1,0:T(8,128)(2,1)S(1)} collective-permute-done((bf16[768,384]{1,0:T(8,128)(2,1)S(1)}, bf16[768,384]{1,0:T(8,128)(2,1)S(1)}, u32[]{:S(2)}, u32[]{:S(2)}) %collective-permute-start.17) | collective-permute-done | bytes 589856 | tf_op jit(solution)/shard_map/ppermute | solution.py:739
  260.7 6.9 %shard_map.272 = (bf16[768,384]{1,0:T(8,128)(2,1)}, bf16[768,384]{1,0:T(8,128)(2,1)}, bf16[768,768]{1,0:T(8,128)(2,1)}, f32[8,768]{1,0:T(8,128)}) custom-call(s32[1]{0:T(128)} %bitcast.21.flag_ref, bf16[768,384]{1,0:T(8,128)(2,1)} %get-tuple-element.170.a_ref.refs_0_.second_ref, bf16[768,384]{1,0:T(8,128)(2,1)} %copy-done.13, bf16[768,768]{1,0:T(8,128)(2,1)} %bitcast.66, ...), custom_call_target="tpu_custom_call" | custom-call | flops 1811939328 | bytes 6291456 | tf_op jit(solution)/shard_map/pallas_call | solution.py:92
  273.5 7.0 %shard_map.273 = (bf16[768,384]{1,0:T(8,128)(2,1)}, bf16[768,384]{1,0:T(8,128)(2,1)}, bf16[768,768]{1,0:T(8,128)(2,1)}, f32[8,768]{1,0:T(8,128)}) custom-call(s32[1]{0:T(128)} %bitcast.21.flag_ref, bf16[768,384]{1,0:T(8,128)(2,1)} %copy-done.14, bf16[768,384]{1,0:T(8,128)(2,1)} %copy-done.16, bf16[768,768]{1,0:T(8,128)(2,1)} %bitcast.67, ...), custom_call_target="tpu_custom_call" | custom-call | flops 1811939328 | bytes 6291456 | tf_op jit(solution)/shard_map/pallas_call | solution.py:92
  284.2 8.0 %shard_map.274 = (bf16[768,768]{1,0:T(8,128)(2,1)}, bf16[768,768]{1,0:T(8,128)(2,1)}) custom-call(s32[1]{0:T(128)} %bitcast.15.flag_ref, bf16[768,384]{1,0:T(8,128)(2,1)} %get-tuple-element.170.a_ref.refs_0_.second_ref, bf16[768,384]{1,0:T(8,128)(2,1)} %copy-done.13, bf16[768,384]{1,0:T(8,128)(2,1)} %copy-done.14, bf16[768,384]{1,0:T(8,128)(2,1)} %copy-done.16, ...), custom_call_target="tpu_custom_call" | custom-call | flops 3623878656 | bytes 6291456 | tf_op jit(solution)/shard_map/pallas_call | solution.py:92
  292.2 10.0 %collective-permute-done.23.refs_2_ = bf16[768,384]{1,0:T(8,128)(2,1)S(1)} collective-permute-done((bf16[768,384]{1,0:T(8,128)(2,1)S(1)}, bf16[768,384]{1,0:T(8,128)(2,1)S(1)}, u32[]{:S(2)}, u32[]{:S(2)}) %collective-permute-start.23) | collective-permute-done | bytes 589856 | tf_op jit(solution)/shard_map/ppermute | solution.py:739
  308.2 15.5 %all_to_all.63.d_ref = bf16[16,48,384]{2,1,0:T(8,128)(2,1)} all-to-all(bf16[16,48,384]{2,1,0:T(8,128)(2,1)} %bitcast.91), channel_id=1, replica_groups=mesh['section'=2,'half'=2,'rest'=2,'side'=2,'core'=2] {'section','rest',..., dimensions={0} | all-to-all | bytes 1179648 | tf_op jit(solution)/shard_map/all_to_all | solution.py:780
  329.7 15.5 %all_to_all.64 = bf16[16,48,384]{2,1,0:T(8,128)(2,1)} all-to-all(bf16[16,48,384]{2,1,0:T(8,128)(2,1)} %shard_map.278), channel_id=1, replica_groups=mesh['section'=2,'half'=2,'rest'=2,'side'=2,'core'=2] {'section','rest',..., dimensions={0} | all-to-all | bytes 1179648 | tf_op jit(solution)/shard_map/all_to_all | solution.py:784
  353.0 7.0 %shard_map.280 = (bf16[768,384]{1,0:T(8,128)(2,1)}, bf16[768,384]{1,0:T(8,128)(2,1)}, bf16[768,768]{1,0:T(8,128)(2,1)}, f32[8,768]{1,0:T(8,128)}) custom-call(s32[1]{0:T(128)} %bitcast.15.flag_ref, bf16[768,384]{1,0:T(8,128)(2,1)} %get-tuple-element.201.a_ref.refs_0_.second_ref, bf16[768,384]{1,0:T(8,128)(2,1)} %copy-done.11, bf16[768,768]{1,0:T(8,128)(2,1)} %bitcast.68, ...), custom_call_target="tpu_custom_call" | custom-call | flops 1811939328 | bytes 6291456 | tf_op jit(solution)/shard_map/pallas_call | solution.py:92
  368.8 7.0 %shard_map.281 = (bf16[768,384]{1,0:T(8,128)(2,1)}, bf16[768,384]{1,0:T(8,128)(2,1)}, bf16[768,768]{1,0:T(8,128)(2,1)}, f32[8,768]{1,0:T(8,128)}) custom-call(s32[1]{0:T(128)} %bitcast.15.flag_ref, bf16[768,384]{1,0:T(8,128)(2,1)} %copy-done.12, bf16[768,384]{1,0:T(8,128)(2,1)} %copy-done.15, bf16[768,768]{1,0:T(8,128)(2,1)} %bitcast.69, ...), custom_call_target="tpu_custom_call" | custom-call | flops 1811939328 | bytes 6291456 | tf_op jit(solution)/shard_map/pallas_call | solution.py:92
  382.9 7.9 %shard_map.282 = (bf16[768,768]{1,0:T(8,128)(2,1)}, bf16[768,768]{1,0:T(8,128)(2,1)}) custom-call(s32[1]{0:T(128)} %bitcast.15.flag_ref, bf16[768,384]{1,0:T(8,128)(2,1)} %get-tuple-element.201.a_ref.refs_0_.second_ref, bf16[768,384]{1,0:T(8,128)(2,1)} %copy-done.11, bf16[768,384]{1,0:T(8,128)(2,1)} %copy-done.12, bf16[768,384]{1,0:T(8,128)(2,1)} %copy-done.15, ...), custom_call_target="tpu_custom_call" | custom-call | flops 3623878656 | bytes 6291456 | tf_op jit(solution)/shard_map/pallas_call | solution.py:92
  411.2 7.7 %all-to-all-done.9.d_ref = bf16[16,48,384]{2,1,0:T(8,128)(2,1)S(1)} async-done(((bf16[16,48,384]{2,1,0:T(8,128)(2,1)}), bf16[16,48,384]{2,1,0:T(8,128)(2,1)S(1)}, u32[]{:S(2)}, u32[]{:S(2)}) %all-to-all-start.9) | async-done | bytes 589856 | tf_op jit(solution)/shard_map/all_to_all | solution.py:780
  432.6 12.4 %collective-permute-done.31 = bf16[768,768]{1,0:T(8,128)(2,1)S(1)} collective-permute-done((bf16[768,768]{1,0:T(8,128)(2,1)}, bf16[768,768]{1,0:T(8,128)(2,1)S(1)}, u32[]{:S(2)}, u32[]{:S(2)}) %collective-permute-start.31) | collective-permute-done | bytes 1179680 | tf_op jit(solution)/shard_map/ppermute | solution.py:739
  454.7 54.5 %all_to_all.65 = bf16[16,304,128]{2,1,0:T(8,128)(2,1)S(1)} all-to-all(bf16[16,304,128]{2,1,0:T(8,128)(2,1)} %shard_map.286), channel_id=1, replica_groups=mesh['section'=2,'half'=2,'rest'=2,'side'=2,'core'=2] {'section','half',..., dimensions={0} | all-to-all | bytes 2490368 | tf_op jit(solution)/shard_map/all_to_all | solution.py:769
  511.0 7.3 %collective-permute-done.32 = bf16[192,768]{1,0:T(8,128)(2,1)S(1)} collective-permute-done((bf16[192,768]{1,0:T(8,128)(2,1)S(1)}, bf16[192,768]{1,0:T(8,128)(2,1)S(1)}, u32[]{:S(2)}, u32[]{:S(2)}) %collective-permute-start.32) | collective-permute-done | bytes 294944 | tf_op jit(solution)/shard_map/ppermute | solution.py:739
  529.0 39.2 %all-gather.3.cloned.1.call-done = bf16[8,192,768]{2,1,0:T(8,128)(2,1)} async-done(((bf16[2,192,768]{2,1,0:T(8,128)(2,1)}), bf16[8,192,768]{2,1,0:T(8,128)(2,1)}) %all-gather.3.cloned.1.call-update) | async-done | bytes 2359312 | tf_op jit(solution)/shard_map/all_gather | solution.py:943
  (267 shorter events, 233.1 us)
Async XLA Ops:
  7.2 30.0 %collective-permute-start = (bf16[768,768]{1,0:T(8,128)(2,1)}, bf16[768,768]{1,0:T(8,128)(2,1)S(1)}, u32[]{:S(2)}, u32[]{:S(2)}) collective-permute-start(bf16[768,768]{1,0:T(8,128)(2,1)} %bitcast.61), channel_id=1, source_target_pairs={{0,16},{16,0},{1,17},{17,1},{2,18},{18,2},{3,19},{19,3},{4,20},{20... | collective-permute-start | bytes 3538952 | tf_op jit(solution)/shard_map/ppermute | solution.py:739
  13.0 21.8 %all-to-all-start = ((bf16[8,288,128]{2,1,0:T(8,128)(2,1)}), bf16[8,288,128]{2,1,0:T(8,128)(2,1)}, u32[]{:S(2)}, u32[]{:S(2)}) async-start(bf16[8,288,128]{2,1,0:T(8,128)(2,1)} %shard_map.257), calls=%async_computation | async-start | bytes 1179648 | tf_op jit(solution)/shard_map/all_to_all | solution.py:762
  18.1 28.2 %collective-permute-start.2 = (f32[1728]{0:T(1024)S(1)}, f32[1728]{0:T(1024)S(1)}, u32[]{:S(2)}, u32[]{:S(2)}) collective-permute-start(f32[1728]{0:T(1024)S(1)} %concatenate.12), channel_id=1, source_target_pairs={{0,16},{16,0},{1,17},{17,1},{2,18},{18,2},{3,19},{19,3},{4,20},{20... | collective-permute-start | bytes 20744 | tf_op jit(solution)/shard_map/ppermute | solution.py:739
  18.6 55.6 %collective-permute-start.1 = (bf16[768,768]{1,0:T(8,128)(2,1)S(1)}, bf16[768,768]{1,0:T(8,128)(2,1)S(1)}, u32[]{:S(2)}, u32[]{:S(2)}) collective-permute-start(bf16[768,768]{1,0:T(8,128)(2,1)S(1)} %bitcast.78), channel_id=1, source_target_pairs={{0,16},{16,0},{1,17},{17,1},{2,18},{18,2},{3,19},{19,3},{4,20},{20... | collective-permute-start | bytes 3538952 | tf_op jit(solution)/shard_map/ppermute | solution.py:739
  40.8 27.4 %all-to-all-start.1 = ((bf16[16,48,384]{2,1,0:T(8,128)(2,1)}), bf16[16,48,384]{2,1,0:T(8,128)(2,1)}, u32[]{:S(2)}, u32[]{:S(2)}) async-start(bf16[16,48,384]{2,1,0:T(8,128)(2,1)} %bitcast.89), calls=%async_computation.1 | async-start | bytes 1179648 | tf_op jit(solution)/shard_map/all_to_all | solution.py:780
  94.5 16.0 %collective-permute-start.5 = (bf16[768,384]{1,0:T(8,128)(2,1)}, bf16[768,384]{1,0:T(8,128)(2,1)S(1)}, u32[]{:S(2)}, u32[]{:S(2)}) collective-permute-start(bf16[768,384]{1,0:T(8,128)(2,1)} %get-tuple-element.136.a_ref.refs_8_), channel_id=1, source_target_pairs={{0,2},{2,0},{1,3},{3,1},{4,6},{6,4},{5,7},{7,5},{8,10},{10,8},{9,1... | collective-permute-start | bytes 1769480 | tf_op jit(solution)/shard_map/ppermute | solution.py:739
  122.8 25.8 %collective-permute-start.7 = (bf16[768,384]{1,0:T(8,128)(2,1)}, bf16[768,384]{1,0:T(8,128)(2,1)S(1)}, u32[]{:S(2)}, u32[]{:S(2)}) collective-permute-start(bf16[768,384]{1,0:T(8,128)(2,1)} %get-tuple-element.145), channel_id=1, source_target_pairs={{0,1},{1,0},{2,3},{3,2},{4,5},{5,4},{6,7},{7,6},{8,9},{9,8},{10,11... | collective-permute-start | bytes 1769480 | tf_op jit(solution)/shard_map/ppermute | solution.py:739
  125.7 20.1 %all-to-all-start.3 = ((bf16[8,288,128]{2,1,0:T(8,128)(2,1)}), bf16[8,288,128]{2,1,0:T(8,128)(2,1)S(1)}, u32[]{:S(2)}, u32[]{:S(2)}) async-start(bf16[8,288,128]{2,1,0:T(8,128)(2,1)} %shard_map.263), calls=%async_computation.3 | async-start | bytes 1179648 | tf_op jit(solution)/shard_map/all_to_all | solution.py:762
  129.4 21.9 %collective-permute-start.10 = (bf16[768,384]{1,0:T(8,128)(2,1)S(1)}, bf16[768,384]{1,0:T(8,128)(2,1)S(1)}, u32[]{:S(2)}, u32[]{:S(2)}) collective-permute-start(bf16[768,384]{1,0:T(8,128)(2,1)S(1)} %add_convert_fusion.5), channel_id=1, source_target_pairs={{0,2},{2,0},{1,3},{3,1},{4,6},{6,4},{5,7},{7,5},{8,10},{10,8},{9,1... | collective-permute-start | bytes 1769480 | tf_op jit(solution)/shard_map/ppermute | solution.py:739
  198.5 16.0 %collective-permute-start.12 = (bf16[768,384]{1,0:T(8,128)(2,1)}, bf16[768,384]{1,0:T(8,128)(2,1)S(1)}, u32[]{:S(2)}, u32[]{:S(2)}) collective-permute-start(bf16[768,384]{1,0:T(8,128)(2,1)} %get-tuple-element.158.a_ref.refs_8_), channel_id=1, source_target_pairs={{0,2},{2,0},{1,3},{3,1},{4,6},{6,4},{5,7},{7,5},{8,10},{10,8},{9,1... | collective-permute-start | bytes 1769480 | tf_op jit(solution)/shard_map/ppermute | solution.py:739
  227.5 15.4 %collective-permute-start.17 = (bf16[768,384]{1,0:T(8,128)(2,1)S(1)}, bf16[768,384]{1,0:T(8,128)(2,1)S(1)}, u32[]{:S(2)}, u32[]{:S(2)}) collective-permute-start(bf16[768,384]{1,0:T(8,128)(2,1)S(1)} %add_convert_fusion.4), channel_id=1, source_target_pairs={{0,2},{2,0},{1,3},{3,1},{4,6},{6,4},{5,7},{7,5},{8,10},{10,8},{9,1... | collective-permute-start | bytes 1769480 | tf_op jit(solution)/shard_map/ppermute | solution.py:739
  251.0 19.7 %collective-permute-start.18 = (bf16[768,384]{1,0:T(8,128)(2,1)}, bf16[768,384]{1,0:T(8,128)(2,1)S(1)}, u32[]{:S(2)}, u32[]{:S(2)}) collective-permute-start(bf16[768,384]{1,0:T(8,128)(2,1)} %get-tuple-element.170.a_ref.refs_0_.second_ref), channel_id=1, source_target_pairs={{0,2},{2,0},{1,3},{3,1},{4,6},{6,4},{5,7},{7,5},{8,10},{10,8},{9,1... | collective-permute-start | bytes 1769480 | tf_op jit(solution)/shard_map/ppermute | solution.py:739
  254.7 47.5 %all-to-all-start.6 = ((bf16[16,304,128]{2,1,0:T(8,128)(2,1)}), bf16[16,304,128]{2,1,0:T(8,128)(2,1)S(1)}, u32[]{:S(2)}, u32[]{:S(2)}) async-start(bf16[16,304,128]{2,1,0:T(8,128)(2,1)} %shard_map.275), calls=%async_computation.6 | async-start | bytes 2490368 | tf_op jit(solution)/shard_map/all_to_all | solution.py:769
  259.6 166.1 %reduce-scatter.3.cloned.1.call-start = ((), (), s32[]{:S(2)}) async-start(), calls=%async_computation.14 | async-start | bytes 1474560 | tf_op jit(solution)/shard_map/reduce_scatter | solution.py:802
  280.8 11.4 %collective-permute-start.20 = (bf16[768,384]{1,0:T(8,128)(2,1)S(1)}, bf16[768,384]{1,0:T(8,128)(2,1)S(1)}, u32[]{:S(2)}, u32[]{:S(2)}) collective-permute-start(bf16[768,384]{1,0:T(8,128)(2,1)S(1)} %copy-done.49), channel_id=1, source_target_pairs={{0,1},{1,0},{2,3},{3,2},{4,5},{5,4},{6,7},{7,6},{8,9},{9,8},{10,11... | collective-permute-start | bytes 1769480 | tf_op jit(solution)/shard_map/ppermute | solution.py:739
  284.1 18.1 %collective-permute-start.23 = (bf16[768,384]{1,0:T(8,128)(2,1)S(1)}, bf16[768,384]{1,0:T(8,128)(2,1)S(1)}, u32[]{:S(2)}, u32[]{:S(2)}) collective-permute-start(bf16[768,384]{1,0:T(8,128)(2,1)S(1)} %add_convert_fusion.3), channel_id=1, source_target_pairs={{0,2},{2,0},{1,3},{3,1},{4,6},{6,4},{5,7},{7,5},{8,10},{10,8},{9,1... | collective-permute-start | bytes 1769480 | tf_op jit(solution)/shard_map/ppermute | solution.py:739
  350.0 16.0 %collective-permute-start.24 = (bf16[768,384]{1,0:T(8,128)(2,1)}, bf16[768,384]{1,0:T(8,128)(2,1)S(1)}, u32[]{:S(2)}, u32[]{:S(2)}) collective-permute-start(bf16[768,384]{1,0:T(8,128)(2,1)} %get-tuple-element.201.a_ref.refs_0_.second_ref), channel_id=1, source_target_pairs={{0,2},{2,0},{1,3},{3,1},{4,6},{6,4},{5,7},{7,5},{8,10},{10,8},{9,1... | collective-permute-start | bytes 1769480 | tf_op jit(solution)/shard_map/ppermute | solution.py:739
  350.4 28.0 %collective-permute-start.30 = (bf16[768,768]{1,0:T(8,128)(2,1)S(1)}, bf16[768,768]{1,0:T(8,128)(2,1)S(1)}, u32[]{:S(2)}, u32[]{:S(2)}) collective-permute-start(bf16[768,768]{1,0:T(8,128)(2,1)S(1)} %copy-done.41), channel_id=1, source_target_pairs={{0,16},{16,0},{1,17},{17,1},{2,18},{18,2},{3,19},{19,3},{4,20},{20... | collective-permute-start | bytes 3538952 | tf_op jit(solution)/shard_map/ppermute | solution.py:739
  381.1 15.6 %collective-permute-start.29 = (bf16[768,384]{1,0:T(8,128)(2,1)S(1)}, bf16[768,384]{1,0:T(8,128)(2,1)S(1)}, u32[]{:S(2)}, u32[]{:S(2)}) collective-permute-start(bf16[768,384]{1,0:T(8,128)(2,1)S(1)} %add_convert_fusion.2), channel_id=1, source_target_pairs={{0,2},{2,0},{1,3},{3,1},{4,6},{6,4},{5,7},{7,5},{8,10},{10,8},{9,1... | collective-permute-start | bytes 1769480 | tf_op jit(solution)/shard_map/ppermute | solution.py:739
  403.0 15.9 %all-to-all-start.9 = ((bf16[16,48,384]{2,1,0:T(8,128)(2,1)}), bf16[16,48,384]{2,1,0:T(8,128)(2,1)S(1)}, u32[]{:S(2)}, u32[]{:S(2)}) async-start(bf16[16,48,384]{2,1,0:T(8,128)(2,1)} %bitcast.90), calls=%async_computation.9 | async-start | bytes 1179648 | tf_op jit(solution)/shard_map/all_to_all | solution.py:780
  409.3 35.7 %collective-permute-start.31 = (bf16[768,768]{1,0:T(8,128)(2,1)}, bf16[768,768]{1,0:T(8,128)(2,1)S(1)}, u32[]{:S(2)}, u32[]{:S(2)}) collective-permute-start(bf16[768,768]{1,0:T(8,128)(2,1)} %get-tuple-element.243), channel_id=1, source_target_pairs={{0,16},{16,0},{1,17},{17,1},{2,18},{18,2},{3,19},{19,3},{4,20},{20... | collective-permute-start | bytes 3538952 | tf_op jit(solution)/shard_map/ppermute | solution.py:739
  425.8 21.5 %all-to-all-start.10 = ((bf16[16,48,384]{2,1,0:T(8,128)(2,1)}), bf16[16,48,384]{2,1,0:T(8,128)(2,1)S(1)}, u32[]{:S(2)}, u32[]{:S(2)}) async-start(bf16[16,48,384]{2,1,0:T(8,128)(2,1)} %shard_map.284), calls=%async_computation.11 | async-start | bytes 1179648 | tf_op jit(solution)/shard_map/all_to_all | solution.py:784
  429.5 79.6 %reduce-scatter.5.cloned.1.call-start = ((), (), s32[]{:S(2)}) async-start(), calls=%async_computation.15 | async-start | bytes 1474560 | tf_op jit(solution)/shard_map/reduce_scatter | solution.py:802
  448.6 119.6 %all-gather.3.cloned.1.call-start = ((), (), s32[]{:S(2)}) async-start(), calls=%async_computation.16 | async-start | bytes 2949120 | tf_op jit(solution)/shard_map/all_gather | solution.py:943
  (70 other events, 413.8 us)
Sparse Core Ops, SparseCore 0:
  379.9 32.4 reduce-scatter.2
  448.8 48.6 reduce-scatter.4
  520.3 47.9 all-gather.2

commit v3 on v2

--- a/solution.py
+++ b/solution.py
@@ -88,7 +88,7 @@
     return jax.ShapeDtypeStruct(tuple(dims), dtype)
 
 
-def call(kernel, outs, args, specs=None, scratch=(), limit=57, flops=0, **extra):
+def call(kernel, outs, args, specs=None, scratch=(), limit=52, flops=0, **extra):
     return pl.pallas_call(
         kernel,
         out_shape=outs,
@@ -108,48 +108,49 @@
     )
 
 
-def send_pencils(local, section, sections, halves, mps, sorting):
-    batches, features, tokens = local.shape
+def send_pencils(locals_, section, sections, halves, mps, sorting):
+    batches, features, tokens = locals_[0].shape
     count, part, rows = batches // halves, tokens // sections // mps, features // 2
-    out = shape((halves * mps, count * rows, 2 * part), local.dtype)
+    kinds = len(locals_)
+    out = shape((halves * mps, kinds * count * rows, 2 * part))
     if part != 64 or mps % 2:
-        own = local.reshape(halves, count, 2, rows, mps, part, sections)
-        own = lax.dynamic_index_in_dim(own, section, 6, keepdims=False)
-        return own.transpose(0, 4, 1, 3, 2, 5).reshape(out.shape)
+        own = jnp.stack(locals_).reshape(kinds, halves, count, 2, rows, mps, part, sections)
+        own = lax.dynamic_index_in_dim(own, section, 7, keepdims=False)
+        return own.transpose(1, 5, 0, 2, 4, 3, 6).reshape(out.shape)
     sorting = sorting.reshape(tokens, sections, tokens // sections).transpose(1, 0, 2)
 
-    def kernel(section_ref, x_ref, sorting_ref, o_ref):
-        for seq in range(batches):
-            half, m = seq // count, seq % count
-            values = mm(x_ref[seq], sorting_ref[0])
-            for place in range(0, mps, 2):
-                a = place * part
-                pair = paired(values[:rows, a : a + 128], values[rows:, a : a + 128])
-                for k in range(2):
-                    d = half * mps + place + k
-                    o_ref[d, m * rows : (m + 1) * rows] = pair[k].astype(BF)
+    def kernel(section_ref, *refs):
+        x_refs, sorting_ref, o_ref = refs[:kinds], refs[kinds], refs[kinds + 1]
+        for kind in range(kinds):
+            for seq in range(batches):
+                half, m = seq // count, seq % count
+                values = mm(x_refs[kind][seq], sorting_ref[0])
+                for place in range(0, mps, 2):
+                    a = place * part
+                    pair = paired(values[:rows, a : a + 128], values[rows:, a : a + 128])
+                    for k in range(2):
+                        d, at = half * mps + place + k, (kind * count + m) * rows
+                        o_ref[d, at : at + rows] = pair[k].astype(BF)
 
     return pl.pallas_call(
         kernel,
         grid_spec=pltpu.PrefetchScalarGridSpec(
             num_scalar_prefetch=1,
             grid=(1,),
-            in_specs=[
-                pl.BlockSpec(local.shape, lambda i, s: (0, 0, 0)),
-                pl.BlockSpec((1,) + sorting.shape[1:], lambda i, s: (s[0], 0, 0)),
-            ],
+            in_specs=[pl.BlockSpec(locals_[0].shape, lambda i, s: (0, 0, 0))] * kinds
+            + [pl.BlockSpec((1,) + sorting.shape[1:], lambda i, s: (s[0], 0, 0))],
             out_specs=pl.BlockSpec(out.shape, lambda i, s: (0, 0, 0)),
         ),
         out_shape=out,
-        compiler_params=pltpu.CompilerParams(vmem_limit_bytes=57 * MIB),
-    )(section.reshape(1), local, sorting)
-
-
-def take_pencils(got, halves, mps, count, packed=None):
-    rows, part = got.shape[1] // count, got.shape[2] // 2
+        compiler_params=pltpu.CompilerParams(vmem_limit_bytes=52 * MIB),
+    )(section.reshape(1), *locals_, sorting)
+
+
+def take_pencils(got, kind, kinds, halves, mps, count, packed=None):
+    rows, part = got.shape[1] // count // kinds, got.shape[2] // 2
     width, columns = mps * 2 * rows, count * halves * part
     if part != 64:
-        got = got.reshape(halves, mps, count, rows, 2, part)
+        got = got.reshape(halves, mps, kinds, count, rows, 2, part)[:, :, kind]
         low = got.transpose(1, 4, 3, 2, 0, 5).reshape(width, columns)
         return low, None if packed is None else mm(packed, low).astype(BF)
 
@@ -157,9 +158,8 @@
         x_ref, o_ref = refs[0], refs[1 if packed is None else 2]
         for mp in range(mps):
             for m in range(count):
-                pair = paired(
-                    *(x_ref[h * mps + mp, m * rows : (m + 1) * rows].astype(F32) for h in range(2))
-                )
+                at = (kind * count + m) * rows
+                pair = paired(*(x_ref[h * mps + mp, at : at + rows].astype(F32) for h in range(2)))
                 for k in range(2):
                     a = (mp * 2 + k) * rows
                     o_ref[a : a + rows, m * 128 : (m + 1) * 128] = pair[k].astype(BF)
@@ -172,20 +172,20 @@
     return call(kernel, (low, low), (got, packed))
 
 
-def send_blocks(layers, extra, sections, halves, mps, count, part):
+def send_blocks(layers, extra, halves, mps, count, part):
     width, columns = layers[0].shape
-    rows = width // mps // 2
+    rows, kinds = width // mps // 2, len(layers)
     more = extra.shape[1]
-    out = shape((sections * halves * mps, count * rows + more, 2 * part))
+    out = shape((kinds * halves * mps, count * rows + more, 2 * part))
     if part != 64:
-        sent = jnp.stack(layers).reshape(sections, mps, 2, rows, count, halves, part)
+        sent = jnp.stack(layers).reshape(kinds, mps, 2, rows, count, halves, part)
         sent = sent.transpose(0, 5, 1, 4, 3, 2, 6).reshape(-1, count * rows, 2 * part)
         return jnp.concatenate([sent, extra], axis=1)
 
     def kernel(*refs):
         o_ref = refs[-1]
-        o_ref[:, count * rows :] = refs[sections][...]
-        for layer in range(sections):
+        o_ref[:, count * rows :] = refs[kinds][...]
+        for layer in range(kinds):
             for mp in range(mps):
                 for m in range(count):
                     a, b = mp * 2 * rows, m * 128
@@ -200,22 +200,26 @@
     return call(kernel, out, (*layers, extra))
 
 
-def take_blocks(got, rows, sections, halves, mps, count, unsorting):
-    part = got.shape[2] // 2
-    out = (1, halves * count, 2 * rows, sections * mps * part)
+def take_blocks(got, places, flipped, rows, halves, mps, count, unsorting):
+    part = got[0].shape[-1] // 2
+    out = (1, halves * count, 2 * rows, 2 * mps * part)
+    got = [array.reshape(-1, halves, mps, array.shape[-2], 2 * part) for array in got]
     if part != 64 or mps % 2:
-        got = got[:, : count * rows].reshape(sections, halves, mps, count, rows, 2, part)
-        return got.transpose(1, 3, 5, 4, 2, 6, 0).reshape(out).astype(F32)
-    got = got.reshape(sections, halves, mps, got.shape[1], 128)
-
-    def kernel(x_ref, table_ref, o_ref, s_ref):
-        for x in range(sections):
+        both = jnp.stack([array[place, :, :, : count * rows] for array, place in zip(got, places)])
+        both = jnp.where(flipped == 1, both[::-1], both)
+        both = both.reshape(2, halves, mps, count, rows, 2, part)
+        return both.transpose(1, 3, 5, 4, 2, 6, 0).reshape(out).astype(F32)
+    tables = unsorting.reshape(2, -1, out[3])
+    tables = jnp.stack([unsorting, tables[::-1].reshape(unsorting.shape)])
+
+    def kernel(flag_ref, a_ref, b_ref, table_ref, o_ref, s_ref):
+        for x, x_ref in enumerate((a_ref, b_ref)):
             for place in range(0, mps, 2):
                 a = x * mps * part + place * part
                 for m in range(count):
                     pair = paired(
                         *(
-                            x_ref[x, 0, place + k, m * rows : (m + 1) * rows].astype(F32)
+                            x_ref[0, 0, place + k, m * rows : (m + 1) * rows].astype(F32)
                             for k in range(2)
                         )
                     )
@@ -224,20 +228,27 @@
                             k
                         ].astype(BF)
         for m in range(count):
-            o_ref[0, m] = mm(s_ref[2 * m * rows : 2 * (m + 1) * rows], table_ref[...])
+            o_ref[0, m] = mm(s_ref[2 * m * rows : 2 * (m + 1) * rows], table_ref[0])
+
+    def block(place):
+        return pl.BlockSpec((1, 1) + got[0].shape[2:], lambda i, s: (place, i, 0, 0, 0))
 
     return pl.pallas_call(
         kernel,
-        grid=(halves,),
-        in_specs=[
-            pl.BlockSpec((sections, 1, mps, got.shape[3], 128), lambda i: (0, i, 0, 0, 0)),
-            pl.BlockSpec(unsorting.shape, lambda i: (0, 0)),
-        ],
-        out_specs=pl.BlockSpec((1, count) + out[2:], lambda i: (i, 0, 0, 0)),
+        grid_spec=pltpu.PrefetchScalarGridSpec(
+            num_scalar_prefetch=1,
+            grid=(halves,),
+            in_specs=[
+                block(places[0]),
+                block(places[1]),
+                pl.BlockSpec((1,) + unsorting.shape, lambda i, s: (s[0], 0, 0)),
+            ],
+            out_specs=pl.BlockSpec((1, count) + out[2:], lambda i, s: (i, 0, 0, 0)),
+            scratch_shapes=[pltpu.VMEM((count * 2 * rows, out[3]), BF)],
+        ),
         out_shape=shape((halves, count) + out[2:], F32),
-        scratch_shapes=[pltpu.VMEM((count * 2 * rows, out[3]), BF)],
-        compiler_params=pltpu.CompilerParams(vmem_limit_bytes=57 * MIB),
-    )(got, unsorting).reshape(out)
+        compiler_params=pltpu.CompilerParams(vmem_limit_bytes=52 * MIB),
+    )(flipped, *got, tables).reshape(out)
 
 
 def token_transform(data, mask, cos, sin, count):
@@ -303,7 +314,7 @@
         [pltpu.VMEM((count * rows, length), BF)]
         + [pltpu.VMEM((spread // step, length, step), BF)] * 2
         + [pltpu.SemaphoreType.DMA((spread // step, 2))],
-        limit=57,
+        limit=52,
         flops=4 * count * rows * length * spread,
     )
 
@@ -325,9 +336,9 @@
     )
 
 
-def column(table_ref, layer, i):
+def column(table, layer, i):
     k = layer * 5 + i
-    return table_ref[:, k : k + 1]
+    return table[:, k : k + 1]
 
 
 def first_norm(got, low, unpack, factor, table, layer):
@@ -335,7 +346,8 @@
 
     def kernel(r_ref, x_ref, unpack_ref, table_ref, unit_ref, inverse_ref, low_ref):
         mixed = mm(unpack_ref[...], r_ref[...])
-        gain, shift = column(table_ref, layer, 1), column(table_ref, layer, 2)
+        table = table_ref[...].T
+        gain, shift = column(table, layer, 1), column(table, layer, 2)
         for a, b in blocks(columns, 128):
             unit, inverse = standardize(x_ref[:, a:b].astype(F32) + mixed[:, a:b] * factor)
             unit_ref[:, a:b] = unit.astype(BF)
@@ -353,7 +365,8 @@
     def kernel(*refs):
         unit1_ref, part_refs = refs[0], refs[1 : 1 + count]
         table_ref, labels_ref, scored_ref = refs[1 + count : 4 + count]
-        bias, gain1, shift1, gain2, shift2 = (column(table_ref, layer, i) for i in range(5))
+        vectors = table_ref[...].T
+        bias, gain1, shift1, gain2, shift2 = (column(vectors, layer, i) for i in range(5))
         bias = bias + shift1
         unit_ref, inverse_ref, low_ref, hits_ref = refs[len(refs) - outs_count :][:4]
         for a, b in blocks(columns, 128):
@@ -401,7 +414,7 @@
         else:
             got_ref, unpack_ref, low_ref, sums_ref, source_ref, product_ref = refs[4:]
             mixed = mm(unpack_ref[...], got_ref[...])
-        gain = column(table_ref, layer, 3)
+        gain = column(table_ref[...].T, layer, 3)
         for a, b in blocks(columns, 128):
             if mix is not None:
                 values = up_ref[:, a:b].astype(F32) + mixed[:, a:b] * mix[2]
@@ -429,7 +442,7 @@
         part_refs = refs[:count]
         unit_ref, inverse_ref, table_ref, packed_ref = refs[count : count + 4]
         low_ref, sums_ref, sent_ref, product_ref, normed_ref = refs[count + 4 :]
-        gain = column(table_ref, layer, 1)
+        gain = column(table_ref[...].T, layer, 1)
         for a, b in blocks(columns, 128):
             values, unit = second_ref[:, a:b].astype(F32), unit_ref[:, a:b].astype(F32)
             for part in part_refs:
@@ -506,10 +519,11 @@
             sems,
         )
         x = jnp.concatenate([a_ref[...], b_ref[...]], axis=1)
+        bias = bias_ref[...].T
         writes = []
         for i, (a, b) in enumerate(steps):
             copies[i].wait()
-            hidden = mm(one_ref[a:b], x) + bias_ref[a:b, layer : layer + 1]
+            hidden = mm(one_ref[a:b], x) + bias[a:b, layer : layer + 1]
             cdf, density = gelu_parts(hidden)
             act_ref[a:b] = (hidden * cdf).astype(BF)
             slope_ref[a:b] = (cdf + hidden * density).astype(BF)
@@ -538,7 +552,7 @@
             pltpu.SemaphoreType.DMA((len(steps) + 1,)),
             pltpu.SemaphoreType.DMA((len(steps), 2)),
         ],
-        limit=57,
+        limit=52,
         flops=8 * width * units * columns,
         out_specs=(VMEM, VMEM, HBM, HBM),
     )
@@ -590,7 +604,7 @@
             pltpu.SemaphoreType.DMA((len(steps) + 2,)),
             pltpu.SemaphoreType.DMA((len(steps),)),
         ],
-        limit=57,
+        limit=52,
         flops=8 * width * units * columns,
         out_specs=(VMEM, VMEM, HBM, VMEM),
     )
@@ -654,7 +668,7 @@
         [pltpu.VMEM((units, width), BF)] * 2
         + [pltpu.VMEM((rows, tokens), BF) for rows in (width, units, units, width)]
         + [pltpu.SemaphoreType.DMA((sum(sizes),)), pltpu.SemaphoreType.DMA((2,))],
-        limit=57,
+        limit=52,
         flops=4 * width * units * tokens,
         out_specs=(HBM, HBM),
     )
@@ -747,7 +761,8 @@
     small = [expand_bias, reduce_bias, first_gain, first_shift, second_gain, second_shift]
     small = jnp.concatenate([vector[0] for vector in small])
     small = jnp.stack(ordered(small, swapped(small, "section")))
-    biases, vectors = small[:, :units].T, small[:, units:].reshape(sections * 5, 1, feature_count)
+    biases = jnp.pad(small[:, :units], ((0, 8 - sections), (0, 0)))
+    vectors = small[:, units:].reshape(sections * 5, 1, feature_count)
     vectors = jnp.concatenate(ordered_by(core, vectors, swapped(vectors, "core")), axis=1)
     chips = [swapped(vectors, "side", -j) if j else vectors for j in range(sides)]
     chips = jnp.stack(chips, axis=1)
@@ -755,25 +770,28 @@
     table = jnp.stack(
         [lax.dynamic_index_in_dim(chips, i, 1, keepdims=False) for i in order], axis=1
     ).reshape(sections * 5, width)
-    table = jnp.pad(table, ((0, -table.shape[0] % 16), (0, 0))).T
-
-    def to_pencils(local, table=None, *others):
-        sent = send_pencils(local, section, sections, halves, mps, sorting)
-        got = lax.all_to_all(sent, PLANE, 0, 0, tiled=True)
-        if others:
-            got, others = lax.optimization_barrier((got, others))
-        return *take_pencils(got, halves, mps, count, table), *others
-
-    def to_blocks(layers, extra):
-        sent = send_blocks(layers, extra, sections, halves, mps, count, part)
-        got = lax.all_to_all(sent, SQUARE, 0, 0, tiled=True)
+    table = jnp.pad(table, ((0, -table.shape[0] % 16), (0, 0)))
+
+    lanes = 2 * part
+
+    def small_rows(layer, hits):
+        high = hits.astype(BF)
+        middle = (hits - high.astype(F32)).astype(BF)
+        lowest = (hits - high.astype(F32) - middle.astype(F32)).astype(BF)
+        counted = jnp.broadcast_to(jnp.stack([high, middle, lowest])[None], (mps, 3))
+        of_features = smalls[layer][:5].reshape(5, mps, feature_count).transpose(1, 0, 2)
+        mine = jnp.arange(mps, dtype=jnp.int32)[:, None] == mp_index
+        bias = jnp.where(mine, bias_rows[layer][None], 0.0)
+        extra = jnp.concatenate(
+            [of_features.reshape(mps, -1).astype(BF), bias.astype(BF), counted], axis=1
+        )
+        extra = jnp.pad(extra, ((0, 0), (0, -extra.shape[1] % (8 * lanes))))
+        extra = jnp.broadcast_to(extra[None], (halves,) + extra.shape)
+        return extra.reshape(halves * mps, -1, lanes)
+
+    def small_sums(got, extra):
         most = got.shape[1] - extra.shape[1]
-        small = jnp.sum(got[:, most:].astype(F32), axis=0).reshape(-1)
-        return got, small, sent
-
-    def from_blocks(got):
-        rows = feature_count // 2
-        return take_blocks(got, rows, sections, halves, mps, count, unsorting)
+        return jnp.sum(got[:, most:].astype(F32), axis=0).reshape(-1)
 
     def fourier(sent, *others):
         sent = sent.reshape(group, rows, columns)
@@ -819,7 +837,11 @@
     marks = marks.transpose(1, 0, 2).reshape(1, columns)
     local_labels, local_scored = marks // 2, (marks % 2).astype(F32)
 
-    low, sent, other_one = to_pencils(inputs, packed, other_one)
+    got = send_pencils((inputs, cotangent), section, sections, halves, mps, sorting)
+    got = lax.all_to_all(got, PLANE, 0, 0, tiled=True)
+    got, other_one = lax.optimization_barrier((got, other_one))
+    low, sent = take_pencils(got, 0, 2, halves, mps, count, packed)
+    up, _ = lax.optimization_barrier((got, sent))
     flags = [is_first.astype(jnp.int32).reshape(1), (1 - is_first.astype(jnp.int32)).reshape(1)]
     saved, outs, hits = [], [], jnp.zeros((), F32)
     for layer in range(2):
@@ -836,8 +858,7 @@
         )
         terms = reduced([run[:2] for run in runs])
         if layer == 0:
-            up, _ = lax.optimization_barrier((cotangent, runs[-1][0]))
-            up = to_pencils(up)[0]
+            up, _ = take_pencils(up, 1, 2, halves, mps, count)
             terms, up = lax.optimization_barrier((terms, up))
         result = second_norm(
             unit1,
@@ -853,8 +874,9 @@
         outs.append(low)
         hits = hits + jnp.sum(hit)
         saved.append((unit1, inv1, xs, runs, unit2, inv2))
-    lanes = 2 * part
-    outputs = to_blocks(outs, jnp.zeros((sections * halves * mps, 16, lanes), BF))[0]
+    nothing = jnp.zeros((sections * halves * mps, 16, lanes), BF)
+    outputs = send_blocks(outs, nothing, halves, mps, count, part)
+    outputs = lax.all_to_all(outputs, SQUARE, 0, 0, tiled=True)
 
     grads_in, weights_out, smalls, bias_rows = [None, None], [None, None], [None, None], [None, None]
     mix = None
@@ -890,53 +912,45 @@
             give, _ = lax.optimization_barrier((give, mixed))
             late = (keep, swapped(give, "section"))
         else:
-            taken = swapped(give, "section")
-            mixed, weights_out[1] = fourier(sent, weights_out[1])
-            taken, _ = lax.optimization_barrier((taken, mixed))
-            both = added(keep, taken)
-            both, _ = lax.optimization_barrier((both, weights_out[1]))
-            weights_out[0] = scattered(both)
+            extra = small_rows(1, hits)
+            got_late, _ = lax.optimization_barrier((grads_in[1], sent))
+            got_late = send_blocks([got_late], extra, halves, mps, count, part)
+            got_late = lax.all_to_all(got_late, PLANE, 0, 0, tiled=True)
+            sent, taken, weights_out[1], got_late = lax.optimization_barrier(
+                (sent, swapped(give, "section"), weights_out[1], got_late)
+            )
+            weights_out[0] = scattered(added(keep, taken))
+            mixed = fourier(sent)
+            rows_of = feature_count // 2
+            outputs = take_blocks(
+                (outputs, outputs), (0, 1), 0 * flags[0], rows_of, halves, mps, count, unsorting
+            )
+            mixed, outputs = lax.optimization_barrier((mixed, outputs))
         mix = (mixed, unpack, factor)
         smalls[layer] = sums1 + sums2
         bias_rows[layer] = sum(back[3][0] for back in backs)
     grads_in[0] = last_mix(mix[0], up, unpack, factor)
 
-    high = hits.astype(BF)
-    middle = (hits - high.astype(F32)).astype(BF)
-    lowest = (hits - high.astype(F32) - middle.astype(F32)).astype(BF)
-    counted = jnp.stack([high, middle, lowest])
-    per = 5 * feature_count
-    rows_of = []
-    for layer in range(sections):
-        vectors_of = smalls[layer][:5].reshape(5, mps, feature_count).transpose(1, 0, 2)
-        mine = jnp.arange(mps, dtype=jnp.int32)[:, None] == mp_index
-        rows_of.append(
-            jnp.concatenate(
-                [
-                    vectors_of.reshape(mps, per).astype(BF),
-                    jnp.where(mine, bias_rows[layer][None], 0.0).astype(BF),
-                    jnp.broadcast_to(counted[None], (mps, 3)),
-                ],
-                axis=1,
-            )
-        )
-    extra = jnp.stack(rows_of)
-    extra = jnp.pad(extra, ((0, 0), (0, 0), (0, -extra.shape[2] % (8 * lanes))))
-    extra = jnp.broadcast_to(extra[:, None], (sections, halves) + extra.shape[1:])
-    got, small, sent = to_blocks(grads_in, extra.reshape(sections * halves * mps, -1, lanes))
-    input_grads = from_blocks(got)
-    outputs = from_blocks(outputs)
-    small, step = small.reshape(-1, lanes), 1
+    extra = small_rows(0, hits)
+    sent = send_blocks(grads_in[:1], extra, halves, mps, count, part)
+    got = lax.all_to_all(sent, PLANE, 0, 0, tiled=True)
+    mine, other = jnp.where(is_first, got, got_late), jnp.where(is_first, got_late, got)
+    other = swapped(other, "section")
+    rows_of = feature_count // 2
+    input_grads = take_blocks(
+        (mine, other), (0, 0), flags[1], rows_of, halves, mps, count, unsorting
+    )
+    small, step = (small_sums(mine, extra) + small_sums(other, extra)).reshape(-1, lanes), 1
     while step < rests:
         small = small + lax.ppermute(small, "rest", [(i, i ^ step) for i in range(rests)])
         step *= 2
-    small = small.reshape(-1)
+    small, per = small.reshape(-1), 5 * feature_count
     features = small[:per].reshape(5, feature_count)
     bias_sum = small[per : per + units]
     accuracy = jnp.sum(small[per + units : per + units + 3])
 
     early, late = weights_out
-    early, late, _ = lax.optimization_barrier((early, late, got))
+    early, late, _ = lax.optimization_barrier((early, late, sent))
     mine, other = jnp.where(is_first, early, late), jnp.where(is_first, late, early)
     other = swapped(other, "section")
     pair = jnp.stack(ordered(mine, other))

time: 585 us -> 535 us (0.915)
  Pallas kernels: 160 us -> 126 us
  waiting for transfers between devices: 188 us -> 181 us
  starting transfers between devices: 48.4 us -> 41.7 us
    ppermute x33 -> x34, waiting for transfers between devices: 97.8 us -> 141 us  [swapped(): lax.ppermute(array, axis, [(i, (i + by) % size) for i in range(size)])]
    all_gather x1, waiting for transfers between devices: 39.2 us -> 1.84 us  [shards(): pair = lax.all_gather(pair, ('half', 'rest'), axis=0, tiled=False)]
    pallas_call x28 -> x29, Pallas kernels: 148 us -> 116 us  [call(): pl.pallas_call(kernel, out_shape=outs, in_specs=specs or [VMEM] * len(arg...]
    all_to_all x3 -> x2, waiting for transfers between devices: 26 us -> 0.45 us  [the longest x1 0.45 us: shards(): got = lax.all_to_all(got, PLANE, 0, 0, tiled=True)]
    all_to_all x1, waiting for transfers between devices: 2.33 us -> 14.6 us  [fourier(): lax.all_to_all(mixed, RING, 0, 0, tiled=True).reshape(width, columns)]
    ppermute x33 -> x34, starting transfers between devices: 21.7 us -> 17.8 us  [swapped(): lax.ppermute(array, axis, [(i, (i + by) % size) for i in range(size)])]
    all_to_all x1 -> x2, blocking collectives: 54.5 us -> 57.2 us  [the longest x1 34.6 us: shards(): got = lax.all_to_all(sent, PLANE, 0, 0, tiled=True)]
    all_to_all x3 -> x2, starting transfers between devices: 13.4 us -> 10.8 us  [the longest x1 6.41 us: shards(): got = lax.all_to_all(got, PLANE, 0, 0, tiled=True)]
  transfers between devices with their start and end apart: 43 -> 43, of which waited for: 29 -> 31; matrix products, arithmetic and copies ran while one was open for 3% -> 3% of each run, Pallas kernels for 18% -> 15%
where the time goes in v3:
time: 535 us; the launch traced here: 530 us
  waiting for transfers between devices  181 us (34%)
  blocking collectives  133 us (25%)
  Pallas kernels  126 us (24%)
  starting transfers between devices  41.7 us (8%)
  local copies, waits for them, and re-layouts  18.6 us (3%)
  between operations  16.4 us (3%)
  other arithmetic  13.2 us (2%)
    ppermute x34, waiting for transfers between devices, swapped(): lax.ppermute(array, axis, [(i, (i + by) % size) for i in range(size)])  141 us
    pallas_call x29, Pallas kernels, call(): pl.pallas_call(kernel, out_shape=outs, in_specs=specs or [VMEM] * len(arg...  116 us
    all_to_all x3, blocking collectives, fourier(): lax.all_to_all(mixed, RING, 0, 0, tiled=True).reshape(width, columns)  44.9 us
    all_to_all x1, blocking collectives, shards(): got = lax.all_to_all(sent, PLANE, 0, 0, tiled=True)  34.6 us
    all_to_all x2, blocking collectives, fourier(): got = lax.all_to_all(sent, RING, 0, 0, tiled=True)  30.7 us
    all_to_all x1, blocking collectives, shards(): got_late = lax.all_to_all(got_late, PLANE, 0, 0, tiled=True)  22.6 us
    all_to_all x2, waiting for transfers between devices, fourier(): got = lax.all_to_all(sent, RING, 0, 0, tiled=True)  22.3 us
    ppermute x34, starting transfers between devices, swapped(): lax.ppermute(array, axis, [(i, (i + by) % size) for i in range(size)])  17.8 us
  transfers between devices with their start and end apart: 43, of which 31 were waited for; matrix products, arithmetic and copies ran while one was open for 3% of the time, Pallas kernels for 15%

profile of v3, /device:TPU:0, one launch (start us, length us, event | category | flops | bytes accessed | tf_op | source)
XLA Modules:
  0.0 529.5 jit_solution(6181222143036279875)
XLA Ops:
  11.8 6.4 %all-to-all-start = ((bf16[8,576,128]{2,1,0:T(8,128)(2,1)}), bf16[8,576,128]{2,1,0:T(8,128)(2,1)S(1)}, u32[]{:S(2)}, u32[]{:S(2)}) async-start(bf16[8,576,128]{2,1,0:T(8,128)(2,1)} %shard_map.257), calls=%async_computation | async-start | bytes 2359296 | tf_op jit(solution)/shard_map/all_to_all | solution.py:841
  22.0 25.2 %collective-permute-done.other1 = bf16[768,768]{1,0:T(8,128)(2,1)} collective-permute-done((bf16[768,768]{1,0:T(8,128)(2,1)S(1)}, bf16[768,768]{1,0:T(8,128)(2,1)}, u32[]{:S(2)}, u32[]{:S(2)}) %collective-permute-start) | collective-permute-done | bytes 1179680 | tf_op jit(solution)/shard_map/ppermute | solution.py:753
  64.1 13.8 %all-to-all-done.1.d_ref = bf16[16,48,384]{2,1,0:T(8,128)(2,1)S(1)} async-done(((bf16[16,48,384]{2,1,0:T(8,128)(2,1)}), bf16[16,48,384]{2,1,0:T(8,128)(2,1)S(1)}, u32[]{:S(2)}, u32[]{:S(2)}) %all-to-all-start.1) | async-done | bytes 589856 | tf_op jit(solution)/shard_map/all_to_all | solution.py:798
  82.0 16.1 %all_to_all.60 = bf16[16,48,384]{2,1,0:T(8,128)(2,1)S(1)} all-to-all(bf16[16,48,384]{2,1,0:T(8,128)(2,1)S(1)} %shard_map.259), channel_id=1, replica_groups=mesh['section'=2,'half'=2,'rest'=2,'side'=2,'core'=2] {'section','rest',..., dimensions={0} | all-to-all | bytes 1179648 | tf_op jit(solution)/shard_map/all_to_all | solution.py:802
  111.0 6.7 %collective-permute-done.5.a_ref.refs_10_ = bf16[768,384]{1,0:T(8,128)(2,1)S(1)} collective-permute-done((bf16[768,384]{1,0:T(8,128)(2,1)S(1)}, bf16[768,384]{1,0:T(8,128)(2,1)S(1)}, u32[]{:S(2)}, u32[]{:S(2)}) %collective-permute-start.5) | collective-permute-done | bytes 589856 | tf_op jit(solution)/shard_map/ppermute | solution.py:753
  132.4 13.3 %collective-permute-done.10.refs_3_ = bf16[768,384]{1,0:T(8,128)(2,1)} collective-permute-done((bf16[768,384]{1,0:T(8,128)(2,1)}, bf16[768,384]{1,0:T(8,128)(2,1)}, u32[]{:S(2)}, u32[]{:S(2)}) %collective-permute-start.10) | collective-permute-done | bytes 589856 | tf_op jit(solution)/shard_map/ppermute | solution.py:753
  151.4 13.8 %all_to_all.61.d_ref = bf16[16,48,384]{2,1,0:T(8,128)(2,1)S(1)} all-to-all(bf16[16,48,384]{2,1,0:T(8,128)(2,1)S(1)} %bitcast.62), channel_id=1, replica_groups=mesh['section'=2,'half'=2,'rest'=2,'side'=2,'core'=2] {'section','rest',..., dimensions={0} | all-to-all | bytes 1179648 | tf_op jit(solution)/shard_map/all_to_all | solution.py:798
  169.4 14.2 %all_to_all.62 = bf16[16,48,384]{2,1,0:T(8,128)(2,1)S(1)} all-to-all(bf16[16,48,384]{2,1,0:T(8,128)(2,1)S(1)} %shard_map.265), channel_id=1, replica_groups=mesh['section'=2,'half'=2,'rest'=2,'side'=2,'core'=2] {'section','rest',..., dimensions={0} | all-to-all | bytes 1179648 | tf_op jit(solution)/shard_map/all_to_all | solution.py:802
  195.0 7.4 %collective-permute-done.12.a_ref.refs_10_ = bf16[768,384]{1,0:T(8,128)(2,1)S(1)} collective-permute-done((bf16[768,384]{1,0:T(8,128)(2,1)S(1)}, bf16[768,384]{1,0:T(8,128)(2,1)S(1)}, u32[]{:S(2)}, u32[]{:S(2)}) %collective-permute-start.12) | collective-permute-done | bytes 589856 | tf_op jit(solution)/shard_map/ppermute | solution.py:753
  213.6 14.8 %collective-permute-done.17.refs_3_ = bf16[768,384]{1,0:T(8,128)(2,1)S(1)} collective-permute-done((bf16[768,384]{1,0:T(8,128)(2,1)S(1)}, bf16[768,384]{1,0:T(8,128)(2,1)S(1)}, u32[]{:S(2)}, u32[]{:S(2)}) %collective-permute-start.17) | collective-permute-done | bytes 589856 | tf_op jit(solution)/shard_map/ppermute | solution.py:753
  246.6 6.4 %collective-permute-done.18.a_ref.refs_2_ = bf16[768,384]{1,0:T(8,128)(2,1)S(1)} collective-permute-done((bf16[768,384]{1,0:T(8,128)(2,1)S(1)}, bf16[768,384]{1,0:T(8,128)(2,1)S(1)}, u32[]{:S(2)}, u32[]{:S(2)}) %collective-permute-start.18) | collective-permute-done | bytes 589856 | tf_op jit(solution)/shard_map/ppermute | solution.py:753
  264.2 7.6 %shard_map.273 = (bf16[768,768]{1,0:T(8,128)(2,1)}, bf16[768,768]{1,0:T(8,128)(2,1)}) custom-call(s32[1]{0:T(128)} %bitcast.12.flag_ref, bf16[768,384]{1,0:T(8,128)(2,1)S(1)} %get-tuple-element.173.a_ref.refs_0_.second_ref, bf16[768,384]{1,0:T(8,128)(2,1)S(1)} %copy-done.12, bf16[768,384]{1,0:T(8,128)(2,1)S(1)} %collective-permute-done.18.a_ref.refs_2_, ...), custom_call_target="tpu_custom_call" | custom-call | flops 3623878656 | bytes 6291456 | tf_op jit(solution)/shard_map/pallas_call | solution.py:92
  271.8 10.4 %collective-permute-done.23.refs_2_ = bf16[768,384]{1,0:T(8,128)(2,1)S(1)} collective-permute-done((bf16[768,384]{1,0:T(8,128)(2,1)S(1)}, bf16[768,384]{1,0:T(8,128)(2,1)S(1)}, u32[]{:S(2)}, u32[]{:S(2)}) %collective-permute-start.23) | collective-permute-done | bytes 589856 | tf_op jit(solution)/shard_map/ppermute | solution.py:753
  287.1 16.9 %all_to_all.63.d_ref = bf16[16,48,384]{2,1,0:T(8,128)(2,1)S(1)} all-to-all(bf16[16,48,384]{2,1,0:T(8,128)(2,1)S(1)} %bitcast.61), channel_id=1, replica_groups=mesh['section'=2,'half'=2,'rest'=2,'side'=2,'core'=2] {'section','rest',..., dimensions={0} | all-to-all | bytes 1179648 | tf_op jit(solution)/shard_map/all_to_all | solution.py:798
  308.2 14.5 %all_to_all.64 = bf16[16,48,384]{2,1,0:T(8,128)(2,1)} all-to-all(bf16[16,48,384]{2,1,0:T(8,128)(2,1)S(1)} %shard_map.276), channel_id=1, replica_groups=mesh['section'=2,'half'=2,'rest'=2,'side'=2,'core'=2] {'section','rest',..., dimensions={0} | all-to-all | bytes 1179648 | tf_op jit(solution)/shard_map/all_to_all | solution.py:802
  335.0 7.1 %collective-permute-done.24.a_ref.refs_2_ = bf16[768,384]{1,0:T(8,128)(2,1)S(1)} collective-permute-done((bf16[768,384]{1,0:T(8,128)(2,1)S(1)}, bf16[768,384]{1,0:T(8,128)(2,1)S(1)}, u32[]{:S(2)}, u32[]{:S(2)}) %collective-permute-start.24) | collective-permute-done | bytes 589856 | tf_op jit(solution)/shard_map/ppermute | solution.py:753
  344.9 6.5 %shard_map.279 = (bf16[768,384]{1,0:T(8,128)(2,1)S(1)}, bf16[768,384]{1,0:T(8,128)(2,1)}, bf16[768,768]{1,0:T(8,128)(2,1)}, f32[8,768]{1,0:T(8,128)S(1)}) custom-call(s32[1]{0:T(128)} %bitcast.12.flag_ref, bf16[768,384]{1,0:T(8,128)(2,1)S(1)} %collective-permute-done.24.a_ref.refs_2_, bf16[768,384]{1,0:T(8,128)(2,1)} %copy-done.27, ...), custom_call_target="tpu_custom_call" | custom-call | flops 1811939328 | bytes 6291456 | tf_op jit(solution)/shard_map/pallas_call | solution.py:92
  362.2 8.0 %shard_map.280 = (bf16[768,768]{1,0:T(8,128)(2,1)}, bf16[768,768]{1,0:T(8,128)(2,1)}) custom-call(s32[1]{0:T(128)} %bitcast.12.flag_ref, bf16[768,384]{1,0:T(8,128)(2,1)S(1)} %get-tuple-element.203.a_ref.refs_0_.second_ref, bf16[768,384]{1,0:T(8,128)(2,1)S(1)} %copy-done.9, bf16[768,384]{1,0:T(8,128)(2,1)S(1)} %collective-permute-done.24.a_ref.refs_2_, ...), custom_call_target="tpu_custom_call" | custom-call | flops 3623878656 | bytes 6291456 | tf_op jit(solution)/shard_map/pallas_call | solution.py:92
  382.1 22.6 %all_to_all.65 = bf16[8,304,128]{2,1,0:T(8,128)(2,1)} all-to-all(bf16[8,304,128]{2,1,0:T(8,128)(2,1)S(1)} %shard_map.282), channel_id=1, replica_groups=mesh['section'=2,'half'=2,'rest'=2,'side'=2,'core'=2] {'half','side','co..., dimensions={0} | all-to-all | bytes 1245184 | tf_op jit(solution)/shard_map/all_to_all | solution.py:918
  411.0 8.6 %all-to-all-done.9.d_ref = bf16[16,48,384]{2,1,0:T(8,128)(2,1)S(1)} async-done(((bf16[16,48,384]{2,1,0:T(8,128)(2,1)}), bf16[16,48,384]{2,1,0:T(8,128)(2,1)S(1)}, u32[]{:S(2)}, u32[]{:S(2)}) %all-to-all-start.9) | async-done | bytes 589856 | tf_op jit(solution)/shard_map/all_to_all | solution.py:798
  431.9 14.6 %all-to-all-done.10 = bf16[16,48,384]{2,1,0:T(8,128)(2,1)S(1)} async-done(((bf16[16,48,384]{2,1,0:T(8,128)(2,1)}), bf16[16,48,384]{2,1,0:T(8,128)(2,1)S(1)}, u32[]{:S(2)}, u32[]{:S(2)}) %all-to-all-start.10) | async-done | bytes 589856 | tf_op jit(solution)/shard_map/all_to_all | solution.py:802
  451.1 7.5 %collective-permute-done.33 = bf16[192,768]{1,0:T(8,128)(2,1)S(1)} collective-permute-done((bf16[192,768]{1,0:T(8,128)(2,1)S(1)}, bf16[192,768]{1,0:T(8,128)(2,1)S(1)}, u32[]{:S(2)}, u32[]{:S(2)}) %collective-permute-start.33) | collective-permute-done | bytes 294944 | tf_op jit(solution)/shard_map/ppermute | solution.py:753
  460.6 34.6 %all_to_all.66 = bf16[8,304,128]{2,1,0:T(8,128)(2,1)S(1)} all-to-all(bf16[8,304,128]{2,1,0:T(8,128)(2,1)S(1)} %shard_map.286), channel_id=1, replica_groups=mesh['section'=2,'half'=2,'rest'=2,'side'=2,'core'=2] {'half','side','co..., dimensions={0} | all-to-all | bytes 1245184 | tf_op jit(solution)/shard_map/all_to_all | solution.py:936
  495.6 15.2 %collective-permute-done.32 = bf16[8,304,128]{2,1,0:T(8,128)(2,1)S(1)} collective-permute-done((bf16[8,304,128]{2,1,0:T(8,128)(2,1)S(1)}, bf16[8,304,128]{2,1,0:T(8,128)(2,1)S(1)}, u32[]{:S(2)}, u32[]{:S(2)}) %collective-permute-start.32) | collective-permute-done | bytes 622624 | tf_op jit(solution)/shard_map/ppermute | solution.py:753
  (262 shorter events, 200.8 us)
Async XLA Ops:
  11.8 35.8 %all-to-all-start = ((bf16[8,576,128]{2,1,0:T(8,128)(2,1)}), bf16[8,576,128]{2,1,0:T(8,128)(2,1)S(1)}, u32[]{:S(2)}, u32[]{:S(2)}) async-start(bf16[8,576,128]{2,1,0:T(8,128)(2,1)} %shard_map.257), calls=%async_computation | async-start | bytes 2359296 | tf_op jit(solution)/shard_map/all_to_all | solution.py:841
  18.2 28.9 %collective-permute-start = (bf16[768,768]{1,0:T(8,128)(2,1)S(1)}, bf16[768,768]{1,0:T(8,128)(2,1)}, u32[]{:S(2)}, u32[]{:S(2)}) collective-permute-start(bf16[768,768]{1,0:T(8,128)(2,1)S(1)} %bitcast.71), channel_id=1, source_target_pairs={{0,16},{16,0},{1,17},{17,1},{2,18},{18,2},{3,19},{19,3},{4,20},{20... | collective-permute-start | bytes 3538952 | tf_op jit(solution)/shard_map/ppermute | solution.py:753
  19.9 37.8 %collective-permute-start.2 = (f32[1728]{0:T(1024)S(1)}, f32[1728]{0:T(1024)S(1)}, u32[]{:S(2)}, u32[]{:S(2)}) collective-permute-start(f32[1728]{0:T(1024)S(1)} %concatenate.12), channel_id=1, source_target_pairs={{0,16},{16,0},{1,17},{17,1},{2,18},{18,2},{3,19},{19,3},{4,20},{20... | collective-permute-start | bytes 20744 | tf_op jit(solution)/shard_map/ppermute | solution.py:753
  20.5 61.6 %collective-permute-start.1 = (bf16[768,768]{1,0:T(8,128)(2,1)}, bf16[768,768]{1,0:T(8,128)(2,1)}, u32[]{:S(2)}, u32[]{:S(2)}) collective-permute-start(bf16[768,768]{1,0:T(8,128)(2,1)} %bitcast.72), channel_id=1, source_target_pairs={{0,16},{16,0},{1,17},{17,1},{2,18},{18,2},{3,19},{19,3},{4,20},{20... | collective-permute-start | bytes 3538952 | tf_op jit(solution)/shard_map/ppermute | solution.py:753
  52.8 25.1 %all-to-all-start.1 = ((bf16[16,48,384]{2,1,0:T(8,128)(2,1)}), bf16[16,48,384]{2,1,0:T(8,128)(2,1)S(1)}, u32[]{:S(2)}, u32[]{:S(2)}) async-start(bf16[16,48,384]{2,1,0:T(8,128)(2,1)} %bitcast.2), calls=%async_computation.1 | async-start | bytes 1179648 | tf_op jit(solution)/shard_map/all_to_all | solution.py:798
  101.9 15.7 %collective-permute-start.5 = (bf16[768,384]{1,0:T(8,128)(2,1)S(1)}, bf16[768,384]{1,0:T(8,128)(2,1)S(1)}, u32[]{:S(2)}, u32[]{:S(2)}) collective-permute-start(bf16[768,384]{1,0:T(8,128)(2,1)S(1)} %get-tuple-element.139.a_ref.refs_8_), channel_id=1, source_target_pairs={{0,2},{2,0},{1,3},{3,1},{4,6},{6,4},{5,7},{7,5},{8,10},{10,8},{9,1... | collective-permute-start | bytes 1769480 | tf_op jit(solution)/shard_map/ppermute | solution.py:753
  129.7 16.0 %collective-permute-start.10 = (bf16[768,384]{1,0:T(8,128)(2,1)}, bf16[768,384]{1,0:T(8,128)(2,1)}, u32[]{:S(2)}, u32[]{:S(2)}) collective-permute-start(bf16[768,384]{1,0:T(8,128)(2,1)} %add_convert_fusion.5), channel_id=1, source_target_pairs={{0,2},{2,0},{1,3},{3,1},{4,6},{6,4},{5,7},{7,5},{8,10},{10,8},{9,1... | collective-permute-start | bytes 1769480 | tf_op jit(solution)/shard_map/ppermute | solution.py:753
  186.7 15.7 %collective-permute-start.12 = (bf16[768,384]{1,0:T(8,128)(2,1)S(1)}, bf16[768,384]{1,0:T(8,128)(2,1)S(1)}, u32[]{:S(2)}, u32[]{:S(2)}) collective-permute-start(bf16[768,384]{1,0:T(8,128)(2,1)S(1)} %get-tuple-element.161.a_ref.refs_8_), channel_id=1, source_target_pairs={{0,2},{2,0},{1,3},{3,1},{4,6},{6,4},{5,7},{7,5},{8,10},{10,8},{9,1... | collective-permute-start | bytes 1769480 | tf_op jit(solution)/shard_map/ppermute | solution.py:753
  212.9 15.4 %collective-permute-start.17 = (bf16[768,384]{1,0:T(8,128)(2,1)S(1)}, bf16[768,384]{1,0:T(8,128)(2,1)S(1)}, u32[]{:S(2)}, u32[]{:S(2)}) collective-permute-start(bf16[768,384]{1,0:T(8,128)(2,1)S(1)} %add_convert_fusion.4), channel_id=1, source_target_pairs={{0,2},{2,0},{1,3},{3,1},{4,6},{6,4},{5,7},{7,5},{8,10},{10,8},{9,1... | collective-permute-start | bytes 1769480 | tf_op jit(solution)/shard_map/ppermute | solution.py:753
  233.5 19.5 %collective-permute-start.18 = (bf16[768,384]{1,0:T(8,128)(2,1)S(1)}, bf16[768,384]{1,0:T(8,128)(2,1)S(1)}, u32[]{:S(2)}, u32[]{:S(2)}) collective-permute-start(bf16[768,384]{1,0:T(8,128)(2,1)S(1)} %get-tuple-element.173.a_ref.refs_0_.second_ref), channel_id=1, source_target_pairs={{0,2},{2,0},{1,3},{3,1},{4,6},{6,4},{5,7},{7,5},{8,10},{10,8},{9,1... | collective-permute-start | bytes 1769480 | tf_op jit(solution)/shard_map/ppermute | solution.py:753
  235.4 46.8 %all-to-all-start.5 = ((bf16[16,304,128]{2,1,0:T(8,128)(2,1)}), bf16[16,304,128]{2,1,0:T(8,128)(2,1)}, u32[]{:S(2)}, u32[]{:S(2)}) async-start(bf16[16,304,128]{2,1,0:T(8,128)(2,1)} %shard_map.274), calls=%async_computation.5 | async-start | bytes 2490368 | tf_op jit(solution)/shard_map/all_to_all | solution.py:879
  239.8 164.9 %reduce-scatter.3.cloned.1.call-start = ((), (), s32[]{:S(2)}) async-start(), calls=%async_computation.14 | async-start | bytes 1474560 | tf_op jit(solution)/shard_map/reduce_scatter | solution.py:820
  261.8 10.0 %collective-permute-start.20 = (bf16[768,384]{1,0:T(8,128)(2,1)S(1)}, bf16[768,384]{1,0:T(8,128)(2,1)S(1)}, u32[]{:S(2)}, u32[]{:S(2)}) collective-permute-start(bf16[768,384]{1,0:T(8,128)(2,1)S(1)} %get-tuple-element.180), channel_id=1, source_target_pairs={{0,1},{1,0},{2,3},{3,2},{4,5},{5,4},{6,7},{7,6},{8,9},{9,8},{10,11... | collective-permute-start | bytes 1769480 | tf_op jit(solution)/shard_map/ppermute | solution.py:753
  263.8 18.5 %collective-permute-start.23 = (bf16[768,384]{1,0:T(8,128)(2,1)S(1)}, bf16[768,384]{1,0:T(8,128)(2,1)S(1)}, u32[]{:S(2)}, u32[]{:S(2)}) collective-permute-start(bf16[768,384]{1,0:T(8,128)(2,1)S(1)} %add_convert_fusion.3), channel_id=1, source_target_pairs={{0,2},{2,0},{1,3},{3,1},{4,6},{6,4},{5,7},{7,5},{8,10},{10,8},{9,1... | collective-permute-start | bytes 1769480 | tf_op jit(solution)/shard_map/ppermute | solution.py:753
  326.3 15.8 %collective-permute-start.24 = (bf16[768,384]{1,0:T(8,128)(2,1)S(1)}, bf16[768,384]{1,0:T(8,128)(2,1)S(1)}, u32[]{:S(2)}, u32[]{:S(2)}) collective-permute-start(bf16[768,384]{1,0:T(8,128)(2,1)S(1)} %get-tuple-element.203.a_ref.refs_0_.second_ref), channel_id=1, source_target_pairs={{0,2},{2,0},{1,3},{3,1},{4,6},{6,4},{5,7},{7,5},{8,10},{10,8},{9,1... | collective-permute-start | bytes 1769480 | tf_op jit(solution)/shard_map/ppermute | solution.py:753
  326.8 28.3 %collective-permute-start.31 = (bf16[768,768]{1,0:T(8,128)(2,1)}, bf16[768,768]{1,0:T(8,128)(2,1)}, u32[]{:S(2)}, u32[]{:S(2)}) collective-permute-start(bf16[768,768]{1,0:T(8,128)(2,1)} %get-tuple-element.229), channel_id=1, source_target_pairs={{0,16},{16,0},{1,17},{17,1},{2,18},{18,2},{3,19},{19,3},{4,20},{20... | collective-permute-start | bytes 3538952 | tf_op jit(solution)/shard_map/ppermute | solution.py:753
  358.1 12.1 %collective-permute-start.26 = (bf16[768,384]{1,0:T(8,128)(2,1)}, bf16[768,384]{1,0:T(8,128)(2,1)}, u32[]{:S(2)}, u32[]{:S(2)}) collective-permute-start(bf16[768,384]{1,0:T(8,128)(2,1)} %copy-done.22), channel_id=1, source_target_pairs={{0,1},{1,0},{2,3},{3,2},{4,5},{5,4},{6,7},{7,6},{8,9},{9,8},{10,11... | collective-permute-start | bytes 1769480 | tf_op jit(solution)/shard_map/ppermute | solution.py:753
  360.3 15.9 %collective-permute-start.29 = (bf16[768,384]{1,0:T(8,128)(2,1)}, bf16[768,384]{1,0:T(8,128)(2,1)S(1)}, u32[]{:S(2)}, u32[]{:S(2)}) collective-permute-start(bf16[768,384]{1,0:T(8,128)(2,1)} %add_convert_fusion.2), channel_id=1, source_target_pairs={{0,2},{2,0},{1,3},{3,1},{4,6},{6,4},{5,7},{7,5},{8,10},{10,8},{9,1... | collective-permute-start | bytes 1769480 | tf_op jit(solution)/shard_map/ppermute | solution.py:753
  376.1 28.6 %collective-permute-start.30 = (bf16[768,768]{1,0:T(8,128)(2,1)}, bf16[768,768]{1,0:T(8,128)(2,1)}, u32[]{:S(2)}, u32[]{:S(2)}) collective-permute-start(bf16[768,768]{1,0:T(8,128)(2,1)} %get-tuple-element.226), channel_id=1, source_target_pairs={{0,16},{16,0},{1,17},{17,1},{2,18},{18,2},{3,19},{19,3},{4,20},{20... | collective-permute-start | bytes 3538952 | tf_op jit(solution)/shard_map/ppermute | solution.py:753
  404.7 14.8 %all-to-all-start.9 = ((bf16[16,48,384]{2,1,0:T(8,128)(2,1)}), bf16[16,48,384]{2,1,0:T(8,128)(2,1)S(1)}, u32[]{:S(2)}, u32[]{:S(2)}) async-start(bf16[16,48,384]{2,1,0:T(8,128)(2,1)} %bitcast.25), calls=%async_computation.10 | async-start | bytes 1179648 | tf_op jit(solution)/shard_map/all_to_all | solution.py:798
  408.3 40.5 %reduce-scatter.5.cloned.1.call-start = ((), (), s32[]{:S(2)}) async-start(), calls=%async_computation.15 | async-start | bytes 1474560 | tf_op jit(solution)/shard_map/reduce_scatter | solution.py:820
  424.5 22.0 %all-to-all-start.10 = ((bf16[16,48,384]{2,1,0:T(8,128)(2,1)}), bf16[16,48,384]{2,1,0:T(8,128)(2,1)S(1)}, u32[]{:S(2)}, u32[]{:S(2)}) async-start(bf16[16,48,384]{2,1,0:T(8,128)(2,1)} %shard_map.283), calls=%async_computation.11 | async-start | bytes 1179648 | tf_op jit(solution)/shard_map/all_to_all | solution.py:802
  428.2 91.0 %all-gather.3.cloned.1.call-start = ((), (), s32[]{:S(2)}) async-start(), calls=%async_computation.16 | async-start | bytes 2949120 | tf_op jit(solution)/shard_map/all_gather | solution.py:957
  495.2 15.6 %collective-permute-start.32 = (bf16[8,304,128]{2,1,0:T(8,128)(2,1)S(1)}, bf16[8,304,128]{2,1,0:T(8,128)(2,1)S(1)}, u32[]{:S(2)}, u32[]{:S(2)}) collective-permute-start(bf16[8,304,128]{2,1,0:T(8,128)(2,1)S(1)} %get-tuple-element.259), channel_id=1, source_target_pairs={{0,16},{16,0},{1,17},{17,1},{2,18},{18,2},{3,19},{19,3},{4,20},{20... | collective-permute-start | bytes 1867784 | tf_op jit(solution)/shard_map/ppermute | solution.py:753
  (64 other events, 377.3 us)
Sparse Core Ops, SparseCore 0:
  358.2 28.2 reduce-scatter.2
  412.1 35.8 reduce-scatter.4
  460.7 58.4 all-gather.2

commit v4 on v3

--- a/solution.py
+++ b/solution.py
@@ -610,68 +610,67 @@
     )
 
 
+def weight_grad(flag, lefts, rights):
+    rows, width = lefts[0][0].shape[0], rights[0][0].shape[0]
+    sizes = [[array.shape[1] for array in either] for either in (lefts[1], rights[1])]
+    tokens = sum(sizes[0])
+    parts = [(side, either) for side in range(2) for either in range(2)]
+    lists = {(side, either): (lefts, rights)[side][either] for side, either in parts}
+
+    def kernel(flag_ref, *refs):
+        inputs, (out_ref, left_ref, right_ref, sems) = refs[:-4], refs[-4:]
+        at, groups = 0, {}
+        for part in parts:
+            groups[part] = inputs[at : at + len(lists[part])]
+            at += len(lists[part])
+        wholes = (left_ref, right_ref)
+
+        def fill(either, act):
+            k = 0
+            for side in range(2):
+                place = 0
+                for src in groups[side, either]:
+                    step = src.shape[1]
+                    target = wholes[side].at[:, place : place + step]
+                    act(pltpu.make_async_copy(src, target, sems.at[either, k]))
+                    place, k = place + step, k + 1
+
+        for act in (lambda copy: copy.start(), lambda copy: copy.wait()):
+            for either in range(2):
+
+                @pl.when((flag_ref[0] == 1) == (either == 0))
+                def _():
+                    fill(either, act)
+
+        for a, b in blocks(rows, 256):
+            out_ref[a:b] = mm_nt(left_ref[a:b], right_ref[...]).astype(BF)
+
+    count = max(len(lists[0, e]) + len(lists[1, e]) for e in range(2))
+    args = [array for part in parts for array in lists[part]]
+    return call(
+        kernel,
+        shape((rows, width)),
+        (flag, *args),
+        [SMEM] + [HBM] * len(args),
+        [
+            pltpu.VMEM((rows, tokens), BF),
+            pltpu.VMEM((width, tokens), BF),
+            pltpu.SemaphoreType.DMA((2, count)),
+        ],
+        limit=52,
+        flops=2 * width * rows * tokens,
+    )
+
+
 def weight_grads(flag, xs, pres, gs, acts):
     units, width = pres[0].shape[0], xs[0].shape[0]
-    tokens = sum(p.shape[1] for p in pres)
-    groups = (gs, acts, pres, xs)
-    sizes = [len(group) for group in groups]
-
-    def kernel(flag_ref, *refs):
-        inputs, rest = refs[: sum(sizes)], refs[sum(sizes) :]
-        keep_hbm, give_hbm, one_ref, two_ref = rest[:4]
-        scratch, sems, sent = rest[4:8], rest[8], rest[9]
-        pairs, ends, k = [], [], 0
-        for size, whole in zip(sizes, scratch):
-            at = 0
-            for _ in range(size):
-                step = inputs[k].shape[1]
-                pairs.append((inputs[k], whole.at[:, at : at + step]))
-                at, k = at + step, k + 1
-            ends.append(k)
-        copies = staged(pairs, sems)
-
-        def put(src, first, second, sem):
-            either = [pltpu.make_async_copy(src, dst, sem) for dst in (first, second)]
-
-            @pl.when(flag_ref[0] == 1)
-            def _():
-                either[0].start()
-
-            @pl.when(flag_ref[0] != 1)
-            def _():
-                either[1].start()
-
-            return either[0]
-
-        for copy in copies[: ends[1]]:
-            copy.wait()
-        for a, b in blocks(width, 256):
-            two_ref[a:b] = mm_nt(scratch[0][a:b], scratch[1][...]).astype(BF)
-        writes = [put(two_ref, give_hbm, keep_hbm, sent.at[0])]
-        for copy in copies[ends[1] :]:
-            copy.wait()
-        for a, b in blocks(units, 256):
-            one_ref[a:b] = mm_nt(scratch[2][a:b], scratch[3][...]).astype(BF)
-        writes.append(put(one_ref, keep_hbm, give_hbm, sent.at[1]))
-        for write in writes:
-            write.wait()
-
     if units != width:
         pre, x, g, act = (jnp.concatenate(group, axis=1) for group in (pres, xs, gs, acts))
         one, two = mm_nt(pre, x).astype(BF), mm_nt(g, act).astype(BF).reshape(units, width)
         return jnp.where(flag == 1, one, two), jnp.where(flag == 1, two, one)
-    return call(
-        kernel,
-        (shape((units, width)),) * 2,
-        (flag, *gs, *acts, *pres, *xs),
-        [SMEM] + [HBM] * sum(sizes),
-        [pltpu.VMEM((units, width), BF)] * 2
-        + [pltpu.VMEM((rows, tokens), BF) for rows in (width, units, units, width)]
-        + [pltpu.SemaphoreType.DMA((sum(sizes),)), pltpu.SemaphoreType.DMA((2,))],
-        limit=52,
-        flops=4 * width * units * tokens,
-        out_specs=(HBM, HBM),
-    )
+    give = weight_grad(flag, (gs, pres), (acts, xs))
+    keep = weight_grad(flag, (pres, gs), (xs, acts))
+    return keep, give
 
 
 def widened(gathered):
@@ -916,10 +915,11 @@
             got_late, _ = lax.optimization_barrier((grads_in[1], sent))
             got_late = send_blocks([got_late], extra, halves, mps, count, part)
             got_late = lax.all_to_all(got_late, PLANE, 0, 0, tiled=True)
-            sent, taken, weights_out[1], got_late = lax.optimization_barrier(
-                (sent, swapped(give, "section"), weights_out[1], got_late)
+            both, weights_out[1] = lax.optimization_barrier(
+                (added(keep, swapped(give, "section")), weights_out[1])
             )
-            weights_out[0] = scattered(added(keep, taken))
+            weights_out[0] = scattered(both)
+            sent, got_late, _ = lax.optimization_barrier((sent, got_late, both))
             mixed = fourier(sent)
             rows_of = feature_count // 2
             outputs = take_blocks(

time: 535 us -> 535 us (level)
  blocking collectives: 133 us -> 112 us
  Pallas kernels: 126 us -> 134 us
  waiting for transfers between devices: 181 us -> 187 us
    all_to_all x1 -> x0, blocking collectives: 22.6 us -> none  [shards(): got_late = lax.all_to_all(got_late, PLANE, 0, 0, tiled=True)]
    pallas_call x29 -> x31, Pallas kernels: 116 us -> 124 us  [call(): pl.pallas_call(kernel, out_shape=outs, in_specs=specs or [VMEM] * len(arg...]
  transfers between devices with their start and end apart: 43 -> 44, of which waited for: 31 -> 30; matrix products, arithmetic and copies ran while one was open for 3% -> 3% of each run, Pallas kernels for 15% -> 16%
where the time goes in v4:
time: 535 us; the launch traced here: 529 us
  waiting for transfers between devices  187 us (35%)
  Pallas kernels  134 us (25%)
  blocking collectives  112 us (21%)
  starting transfers between devices  46.7 us (9%)
  local copies, waits for them, and re-layouts  21.7 us (4%)
  between operations  16.2 us (3%)
  other arithmetic  11.6 us (2%)
    ppermute x34, waiting for transfers between devices, swapped(): lax.ppermute(array, axis, [(i, (i + by) % size) for i in range(size)])  145 us
    pallas_call x31, Pallas kernels, call(): pl.pallas_call(kernel, out_shape=outs, in_specs=specs or [VMEM] * len(arg...  124 us
    all_to_all x3, blocking collectives, fourier(): lax.all_to_all(mixed, RING, 0, 0, tiled=True).reshape(width, columns)  44.7 us
    all_to_all x1, blocking collectives, shards(): got = lax.all_to_all(sent, PLANE, 0, 0, tiled=True)  36.4 us
    all_to_all x2, blocking collectives, fourier(): got = lax.all_to_all(sent, RING, 0, 0, tiled=True)  30.7 us
    all_to_all x2, waiting for transfers between devices, fourier(): got = lax.all_to_all(sent, RING, 0, 0, tiled=True)  24.3 us
    ppermute x34, starting transfers between devices, swapped(): lax.ppermute(array, axis, [(i, (i + by) % size) for i in range(size)])  17.9 us
    unnamed x90, local copies, waits for them, and re-layouts  17.5 us
  transfers between devices with their start and end apart: 44, of which 30 were waited for; matrix products, arithmetic and copies ran while one was open for 3% of the time, Pallas kernels for 16%

profile of v4, /device:TPU:0, one launch (start us, length us, event | category | flops | bytes accessed | tf_op | source)
XLA Modules:
  0.0 529.2 jit_solution(13366347453066426148)
XLA Ops:
  11.7 6.4 %all-to-all-start = ((bf16[8,576,128]{2,1,0:T(8,128)(2,1)}), bf16[8,576,128]{2,1,0:T(8,128)(2,1)S(1)}, u32[]{:S(2)}, u32[]{:S(2)}) async-start(bf16[8,576,128]{2,1,0:T(8,128)(2,1)} %shard_map.257), calls=%async_computation | async-start | bytes 2359296 | tf_op jit(solution)/shard_map/all_to_all | solution.py:840
  22.6 24.4 %collective-permute-done.other1 = bf16[768,768]{1,0:T(8,128)(2,1)S(1)} collective-permute-done((bf16[768,768]{1,0:T(8,128)(2,1)S(1)}, bf16[768,768]{1,0:T(8,128)(2,1)S(1)}, u32[]{:S(2)}, u32[]{:S(2)}) %collective-permute-start) | collective-permute-done | bytes 1179680 | tf_op jit(solution)/shard_map/ppermute | solution.py:752
  64.0 13.9 %all-to-all-done.1.d_ref = bf16[16,48,384]{2,1,0:T(8,128)(2,1)S(1)} async-done(((bf16[16,48,384]{2,1,0:T(8,128)(2,1)}), bf16[16,48,384]{2,1,0:T(8,128)(2,1)S(1)}, u32[]{:S(2)}, u32[]{:S(2)}) %all-to-all-start.1) | async-done | bytes 589856 | tf_op jit(solution)/shard_map/all_to_all | solution.py:797
  82.0 16.1 %all_to_all.60 = bf16[16,48,384]{2,1,0:T(8,128)(2,1)S(1)} all-to-all(bf16[16,48,384]{2,1,0:T(8,128)(2,1)S(1)} %shard_map.259), channel_id=1, replica_groups=mesh['section'=2,'half'=2,'rest'=2,'side'=2,'core'=2] {'section','rest',..., dimensions={0} | all-to-all | bytes 1179648 | tf_op jit(solution)/shard_map/all_to_all | solution.py:801
  104.7 6.3 %shard_map.261 = (bf16[768,384]{1,0:T(8,128)(2,1)S(1)}, bf16[768,384]{1,0:T(8,128)(2,1)}, bf16[768,768]{1,0:T(8,128)(2,1)}, bf16[768,768]{1,0:T(8,128)(2,1)}) custom-call(s32[1]{0:T(128)} %bitcast.12.flag_ref, bf16[768,384]{1,0:T(8,128)(2,1)S(1)} %get-tuple-element.135.a_ref.refs_6_.refs_8_, bf16[768,384]{1,0:T(8,128)(2,1)} %copy-done.30, ...), custom_call_target="tpu_custom_call" | custom-call | flops 1811939328 | bytes 6291456 | tf_op jit(solution)/shard_map/pallas_call | solution.py:92
  111.8 5.8 %collective-permute-done.5.a_ref.refs_8_.refs_10_ = bf16[768,384]{1,0:T(8,128)(2,1)S(1)} collective-permute-done((bf16[768,384]{1,0:T(8,128)(2,1)S(1)}, bf16[768,384]{1,0:T(8,128)(2,1)S(1)}, u32[]{:S(2)}, u32[]{:S(2)}) %collective-permute-start.5) | collective-permute-done | bytes 589856 | tf_op jit(solution)/shard_map/ppermute | solution.py:752
  132.3 13.3 %collective-permute-done.10.refs_3_ = bf16[768,384]{1,0:T(8,128)(2,1)} collective-permute-done((bf16[768,384]{1,0:T(8,128)(2,1)}, bf16[768,384]{1,0:T(8,128)(2,1)}, u32[]{:S(2)}, u32[]{:S(2)}) %collective-permute-start.10) | collective-permute-done | bytes 589856 | tf_op jit(solution)/shard_map/ppermute | solution.py:752
  151.3 13.8 %all_to_all.61.d_ref = bf16[16,48,384]{2,1,0:T(8,128)(2,1)S(1)} all-to-all(bf16[16,48,384]{2,1,0:T(8,128)(2,1)S(1)} %bitcast.62), channel_id=1, replica_groups=mesh['section'=2,'half'=2,'rest'=2,'side'=2,'core'=2] {'section','rest',..., dimensions={0} | all-to-all | bytes 1179648 | tf_op jit(solution)/shard_map/all_to_all | solution.py:797
  169.3 14.0 %all_to_all.62 = bf16[16,48,384]{2,1,0:T(8,128)(2,1)S(1)} all-to-all(bf16[16,48,384]{2,1,0:T(8,128)(2,1)S(1)} %shard_map.265), channel_id=1, replica_groups=mesh['section'=2,'half'=2,'rest'=2,'side'=2,'core'=2] {'section','rest',..., dimensions={0} | all-to-all | bytes 1179648 | tf_op jit(solution)/shard_map/all_to_all | solution.py:801
  195.4 6.7 %collective-permute-done.12.a_ref.refs_8_.refs_10_ = bf16[768,384]{1,0:T(8,128)(2,1)S(1)} collective-permute-done((bf16[768,384]{1,0:T(8,128)(2,1)S(1)}, bf16[768,384]{1,0:T(8,128)(2,1)S(1)}, u32[]{:S(2)}, u32[]{:S(2)}) %collective-permute-start.12) | collective-permute-done | bytes 589856 | tf_op jit(solution)/shard_map/ppermute | solution.py:752
  213.3 14.7 %collective-permute-done.17.refs_3_ = bf16[768,384]{1,0:T(8,128)(2,1)S(1)} collective-permute-done((bf16[768,384]{1,0:T(8,128)(2,1)S(1)}, bf16[768,384]{1,0:T(8,128)(2,1)S(1)}, u32[]{:S(2)}, u32[]{:S(2)}) %collective-permute-start.17) | collective-permute-done | bytes 589856 | tf_op jit(solution)/shard_map/ppermute | solution.py:752
  255.5 5.7 %shard_map.272 = (bf16[768,384]{1,0:T(8,128)(2,1)S(1)}, bf16[768,384]{1,0:T(8,128)(2,1)S(1)}, bf16[768,768]{1,0:T(8,128)(2,1)}, f32[8,768]{1,0:T(8,128)S(1)}) custom-call(s32[1]{0:T(128)} %bitcast.18.flag_ref, bf16[768,384]{1,0:T(8,128)(2,1)S(1)} %collective-permute-done.18.a_ref.refs_4_.refs_2_, bf16[768,384]{1,0:T(8,128)(2,1)} %copy-done.25, ...), custom_call_target="tpu_custom_call" | custom-call | flops 1811939328 | bytes 6291456 | tf_op jit(solution)/shard_map/pallas_call | solution.py:92
  274.5 7.4 %collective-permute-done.23.refs_2_ = bf16[768,384]{1,0:T(8,128)(2,1)S(1)} collective-permute-done((bf16[768,384]{1,0:T(8,128)(2,1)S(1)}, bf16[768,384]{1,0:T(8,128)(2,1)S(1)}, u32[]{:S(2)}, u32[]{:S(2)}) %collective-permute-start.23) | collective-permute-done | bytes 589856 | tf_op jit(solution)/shard_map/ppermute | solution.py:752
  286.8 16.9 %all_to_all.63.d_ref = bf16[16,48,384]{2,1,0:T(8,128)(2,1)S(1)} all-to-all(bf16[16,48,384]{2,1,0:T(8,128)(2,1)S(1)} %bitcast.61), channel_id=1, replica_groups=mesh['section'=2,'half'=2,'rest'=2,'side'=2,'core'=2] {'section','rest',..., dimensions={0} | all-to-all | bytes 1179648 | tf_op jit(solution)/shard_map/all_to_all | solution.py:797
  307.8 14.5 %all_to_all.64 = bf16[16,48,384]{2,1,0:T(8,128)(2,1)} all-to-all(bf16[16,48,384]{2,1,0:T(8,128)(2,1)S(1)} %shard_map.277), channel_id=1, replica_groups=mesh['section'=2,'half'=2,'rest'=2,'side'=2,'core'=2] {'section','rest',..., dimensions={0} | all-to-all | bytes 1179648 | tf_op jit(solution)/shard_map/all_to_all | solution.py:801
  328.9 6.5 %shard_map.279 = (bf16[768,384]{1,0:T(8,128)(2,1)S(1)}, bf16[768,384]{1,0:T(8,128)(2,1)}, bf16[768,768]{1,0:T(8,128)(2,1)}, f32[8,768]{1,0:T(8,128)S(1)}) custom-call(s32[1]{0:T(128)} %bitcast.12.flag_ref, bf16[768,384]{1,0:T(8,128)(2,1)S(1)} %get-tuple-element.197.a_ref.refs_2_.refs_0_.second_ref, bf16[768,384]{1,0:T(8,128)(2,1)} %copy-done.2, ...), custom_call_target="tpu_custom_call" | custom-call | flops 1811939328 | bytes 6291456 | tf_op jit(solution)/shard_map/pallas_call | solution.py:92
  335.4 6.4 %collective-permute-done.24.a_ref.refs_4_.refs_2_ = bf16[768,384]{1,0:T(8,128)(2,1)S(1)} collective-permute-done((bf16[768,384]{1,0:T(8,128)(2,1)S(1)}, bf16[768,384]{1,0:T(8,128)(2,1)S(1)}, u32[]{:S(2)}, u32[]{:S(2)}) %collective-permute-start.24) | collective-permute-done | bytes 589856 | tf_op jit(solution)/shard_map/ppermute | solution.py:752
  344.6 6.6 %shard_map.280 = (bf16[768,384]{1,0:T(8,128)(2,1)S(1)}, bf16[768,384]{1,0:T(8,128)(2,1)}, bf16[768,768]{1,0:T(8,128)(2,1)}, f32[8,768]{1,0:T(8,128)S(1)}) custom-call(s32[1]{0:T(128)} %bitcast.12.flag_ref, bf16[768,384]{1,0:T(8,128)(2,1)S(1)} %collective-permute-done.24.a_ref.refs_4_.refs_2_, bf16[768,384]{1,0:T(8,128)(2,1)} %copy-done.24, ...), custom_call_target="tpu_custom_call" | custom-call | flops 1811939328 | bytes 6291456 | tf_op jit(solution)/shard_map/pallas_call | solution.py:92
  384.2 16.2 %collective-permute-done.30 = bf16[768,768]{1,0:T(8,128)(2,1)} collective-permute-done((bf16[768,768]{1,0:T(8,128)(2,1)}, bf16[768,768]{1,0:T(8,128)(2,1)}, u32[]{:S(2)}, u32[]{:S(2)}) %collective-permute-start.30) | collective-permute-done | bytes 1179680 | tf_op jit(solution)/shard_map/ppermute | solution.py:752
  408.1 10.5 %all-to-all-done.9.d_ref = bf16[16,48,384]{2,1,0:T(8,128)(2,1)S(1)} async-done(((bf16[16,48,384]{2,1,0:T(8,128)(2,1)}), bf16[16,48,384]{2,1,0:T(8,128)(2,1)S(1)}, u32[]{:S(2)}, u32[]{:S(2)}) %all-to-all-start.9) | async-done | bytes 589856 | tf_op jit(solution)/shard_map/all_to_all | solution.py:797
  430.9 15.4 %all-to-all-done.10 = bf16[16,48,384]{2,1,0:T(8,128)(2,1)S(1)} async-done(((bf16[16,48,384]{2,1,0:T(8,128)(2,1)}), bf16[16,48,384]{2,1,0:T(8,128)(2,1)S(1)}, u32[]{:S(2)}, u32[]{:S(2)}) %all-to-all-start.10) | async-done | bytes 589856 | tf_op jit(solution)/shard_map/all_to_all | solution.py:801
  450.8 7.7 %collective-permute-done.33 = bf16[192,768]{1,0:T(8,128)(2,1)S(1)} collective-permute-done((bf16[192,768]{1,0:T(8,128)(2,1)S(1)}, bf16[192,768]{1,0:T(8,128)(2,1)S(1)}, u32[]{:S(2)}, u32[]{:S(2)}) %collective-permute-start.33) | collective-permute-done | bytes 294944 | tf_op jit(solution)/shard_map/ppermute | solution.py:752
  460.5 36.4 %all_to_all.65 = bf16[8,304,128]{2,1,0:T(8,128)(2,1)S(1)} all-to-all(bf16[8,304,128]{2,1,0:T(8,128)(2,1)S(1)} %shard_map.288), channel_id=1, replica_groups=mesh['section'=2,'half'=2,'rest'=2,'side'=2,'core'=2] {'half','side','co..., dimensions={0} | all-to-all | bytes 1245184 | tf_op jit(solution)/shard_map/all_to_all | solution.py:936
  497.1 14.0 %collective-permute-done.32 = bf16[8,304,128]{2,1,0:T(8,128)(2,1)S(1)} collective-permute-done((bf16[8,304,128]{2,1,0:T(8,128)(2,1)S(1)}, bf16[8,304,128]{2,1,0:T(8,128)(2,1)S(1)}, u32[]{:S(2)}, u32[]{:S(2)}) %collective-permute-start.32) | collective-permute-done | bytes 622624 | tf_op jit(solution)/shard_map/ppermute | solution.py:752
  (265 shorter events, 213.4 us)
Async XLA Ops:
  11.7 35.8 %all-to-all-start = ((bf16[8,576,128]{2,1,0:T(8,128)(2,1)}), bf16[8,576,128]{2,1,0:T(8,128)(2,1)S(1)}, u32[]{:S(2)}, u32[]{:S(2)}) async-start(bf16[8,576,128]{2,1,0:T(8,128)(2,1)} %shard_map.257), calls=%async_computation | async-start | bytes 2359296 | tf_op jit(solution)/shard_map/all_to_all | solution.py:840
  18.2 28.8 %collective-permute-start = (bf16[768,768]{1,0:T(8,128)(2,1)S(1)}, bf16[768,768]{1,0:T(8,128)(2,1)S(1)}, u32[]{:S(2)}, u32[]{:S(2)}) collective-permute-start(bf16[768,768]{1,0:T(8,128)(2,1)S(1)} %bitcast.71), channel_id=1, source_target_pairs={{0,16},{16,0},{1,17},{17,1},{2,18},{18,2},{3,19},{19,3},{4,20},{20... | collective-permute-start | bytes 3538952 | tf_op jit(solution)/shard_map/ppermute | solution.py:752
  20.5 37.0 %collective-permute-start.2 = (f32[1728]{0:T(1024)S(1)}, f32[1728]{0:T(1024)S(1)}, u32[]{:S(2)}, u32[]{:S(2)}) collective-permute-start(f32[1728]{0:T(1024)S(1)} %concatenate.12), channel_id=1, source_target_pairs={{0,16},{16,0},{1,17},{17,1},{2,18},{18,2},{3,19},{19,3},{4,20},{20... | collective-permute-start | bytes 20744 | tf_op jit(solution)/shard_map/ppermute | solution.py:752
  21.1 60.9 %collective-permute-start.1 = (bf16[768,768]{1,0:T(8,128)(2,1)}, bf16[768,768]{1,0:T(8,128)(2,1)}, u32[]{:S(2)}, u32[]{:S(2)}) collective-permute-start(bf16[768,768]{1,0:T(8,128)(2,1)} %bitcast.3.own2), channel_id=1, source_target_pairs={{0,16},{16,0},{1,17},{17,1},{2,18},{18,2},{3,19},{19,3},{4,20},{20... | collective-permute-start | bytes 3538952 | tf_op jit(solution)/shard_map/ppermute | solution.py:752
  52.8 25.0 %all-to-all-start.1 = ((bf16[16,48,384]{2,1,0:T(8,128)(2,1)}), bf16[16,48,384]{2,1,0:T(8,128)(2,1)S(1)}, u32[]{:S(2)}, u32[]{:S(2)}) async-start(bf16[16,48,384]{2,1,0:T(8,128)(2,1)} %bitcast.2), calls=%async_computation.1 | async-start | bytes 1179648 | tf_op jit(solution)/shard_map/all_to_all | solution.py:797
  101.8 15.7 %collective-permute-start.5 = (bf16[768,384]{1,0:T(8,128)(2,1)S(1)}, bf16[768,384]{1,0:T(8,128)(2,1)S(1)}, u32[]{:S(2)}, u32[]{:S(2)}) collective-permute-start(bf16[768,384]{1,0:T(8,128)(2,1)S(1)} %get-tuple-element.135.a_ref.refs_6_.refs_8_), channel_id=1, source_target_pairs={{0,2},{2,0},{1,3},{3,1},{4,6},{6,4},{5,7},{7,5},{8,10},{10,8},{9,1... | collective-permute-start | bytes 1769480 | tf_op jit(solution)/shard_map/ppermute | solution.py:752
  129.6 16.0 %collective-permute-start.10 = (bf16[768,384]{1,0:T(8,128)(2,1)}, bf16[768,384]{1,0:T(8,128)(2,1)}, u32[]{:S(2)}, u32[]{:S(2)}) collective-permute-start(bf16[768,384]{1,0:T(8,128)(2,1)} %add_convert_fusion.5), channel_id=1, source_target_pairs={{0,2},{2,0},{1,3},{3,1},{4,6},{6,4},{5,7},{7,5},{8,10},{10,8},{9,1... | collective-permute-start | bytes 1769480 | tf_op jit(solution)/shard_map/ppermute | solution.py:752
  186.3 15.7 %collective-permute-start.12 = (bf16[768,384]{1,0:T(8,128)(2,1)S(1)}, bf16[768,384]{1,0:T(8,128)(2,1)S(1)}, u32[]{:S(2)}, u32[]{:S(2)}) collective-permute-start(bf16[768,384]{1,0:T(8,128)(2,1)S(1)} %get-tuple-element.157.a_ref.refs_6_.refs_8_), channel_id=1, source_target_pairs={{0,2},{2,0},{1,3},{3,1},{4,6},{6,4},{5,7},{7,5},{8,10},{10,8},{9,1... | collective-permute-start | bytes 1769480 | tf_op jit(solution)/shard_map/ppermute | solution.py:752
  212.6 15.4 %collective-permute-start.17 = (bf16[768,384]{1,0:T(8,128)(2,1)S(1)}, bf16[768,384]{1,0:T(8,128)(2,1)S(1)}, u32[]{:S(2)}, u32[]{:S(2)}) collective-permute-start(bf16[768,384]{1,0:T(8,128)(2,1)S(1)} %add_convert_fusion.4), channel_id=1, source_target_pairs={{0,2},{2,0},{1,3},{3,1},{4,6},{6,4},{5,7},{7,5},{8,10},{10,8},{9,1... | collective-permute-start | bytes 1769480 | tf_op jit(solution)/shard_map/ppermute | solution.py:752
  233.2 19.5 %collective-permute-start.18 = (bf16[768,384]{1,0:T(8,128)(2,1)S(1)}, bf16[768,384]{1,0:T(8,128)(2,1)S(1)}, u32[]{:S(2)}, u32[]{:S(2)}) collective-permute-start(bf16[768,384]{1,0:T(8,128)(2,1)S(1)} %get-tuple-element.169.a_ref.refs_2_.refs_0_.second_ref), channel_id=1, source_target_pairs={{0,2},{2,0},{1,3},{3,1},{4,6},{6,4},{5,7},{7,5},{8,10},{10,8},{9,1... | collective-permute-start | bytes 1769480 | tf_op jit(solution)/shard_map/ppermute | solution.py:752
  235.1 46.8 %all-to-all-start.5 = ((bf16[16,304,128]{2,1,0:T(8,128)(2,1)}), bf16[16,304,128]{2,1,0:T(8,128)(2,1)}, u32[]{:S(2)}, u32[]{:S(2)}) async-start(bf16[16,304,128]{2,1,0:T(8,128)(2,1)} %shard_map.275), calls=%async_computation.5 | async-start | bytes 2490368 | tf_op jit(solution)/shard_map/all_to_all | solution.py:878
  239.4 163.5 %reduce-scatter.3.cloned.1.call-start = ((), (), s32[]{:S(2)}) async-start(), calls=%async_computation.14 | async-start | bytes 1474560 | tf_op jit(solution)/shard_map/reduce_scatter | solution.py:819
  263.4 18.5 %collective-permute-start.23 = (bf16[768,384]{1,0:T(8,128)(2,1)S(1)}, bf16[768,384]{1,0:T(8,128)(2,1)S(1)}, u32[]{:S(2)}, u32[]{:S(2)}) collective-permute-start(bf16[768,384]{1,0:T(8,128)(2,1)S(1)} %add_convert_fusion.3), channel_id=1, source_target_pairs={{0,2},{2,0},{1,3},{3,1},{4,6},{6,4},{5,7},{7,5},{8,10},{10,8},{9,1... | collective-permute-start | bytes 1769480 | tf_op jit(solution)/shard_map/ppermute | solution.py:752
  326.0 15.8 %collective-permute-start.24 = (bf16[768,384]{1,0:T(8,128)(2,1)S(1)}, bf16[768,384]{1,0:T(8,128)(2,1)S(1)}, u32[]{:S(2)}, u32[]{:S(2)}) collective-permute-start(bf16[768,384]{1,0:T(8,128)(2,1)S(1)} %get-tuple-element.197.a_ref.refs_2_.refs_0_.second_ref), channel_id=1, source_target_pairs={{0,2},{2,0},{1,3},{3,1},{4,6},{6,4},{5,7},{7,5},{8,10},{10,8},{9,1... | collective-permute-start | bytes 1769480 | tf_op jit(solution)/shard_map/ppermute | solution.py:752
  326.5 28.0 %collective-permute-start.31 = (bf16[768,768]{1,0:T(8,128)(2,1)S(1)}, bf16[768,768]{1,0:T(8,128)(2,1)S(1)}, u32[]{:S(2)}, u32[]{:S(2)}) collective-permute-start(bf16[768,768]{1,0:T(8,128)(2,1)S(1)} %copy-done.35), channel_id=1, source_target_pairs={{0,16},{16,0},{1,17},{17,1},{2,18},{18,2},{3,19},{19,3},{4,20},{20... | collective-permute-start | bytes 3538952 | tf_op jit(solution)/shard_map/ppermute | solution.py:752
  351.4 21.5 %collective-permute-start.26 = (bf16[768,384]{1,0:T(8,128)(2,1)}, bf16[768,384]{1,0:T(8,128)(2,1)}, u32[]{:S(2)}, u32[]{:S(2)}) collective-permute-start(bf16[768,384]{1,0:T(8,128)(2,1)} %get-tuple-element.204), channel_id=1, source_target_pairs={{0,1},{1,0},{2,3},{3,2},{4,5},{5,4},{6,7},{7,6},{8,9},{9,8},{10,11... | collective-permute-start | bytes 1769480 | tf_op jit(solution)/shard_map/ppermute | solution.py:752
  357.9 15.0 %collective-permute-start.29 = (bf16[768,384]{1,0:T(8,128)(2,1)}, bf16[768,384]{1,0:T(8,128)(2,1)S(1)}, u32[]{:S(2)}, u32[]{:S(2)}) collective-permute-start(bf16[768,384]{1,0:T(8,128)(2,1)} %add_convert_fusion.2), channel_id=1, source_target_pairs={{0,2},{2,0},{1,3},{3,1},{4,6},{6,4},{5,7},{7,5},{8,10},{10,8},{9,1... | collective-permute-start | bytes 1769480 | tf_op jit(solution)/shard_map/ppermute | solution.py:752
  373.0 27.4 %collective-permute-start.30 = (bf16[768,768]{1,0:T(8,128)(2,1)}, bf16[768,768]{1,0:T(8,128)(2,1)}, u32[]{:S(2)}, u32[]{:S(2)}) collective-permute-start(bf16[768,768]{1,0:T(8,128)(2,1)} %shard_map.282), channel_id=1, source_target_pairs={{0,16},{16,0},{1,17},{17,1},{2,18},{18,2},{3,19},{19,3},{4,20},{20... | collective-permute-start | bytes 3538952 | tf_op jit(solution)/shard_map/ppermute | solution.py:752
  380.2 22.8 %all-to-all-start.8 = ((bf16[8,304,128]{2,1,0:T(8,128)(2,1)}), bf16[8,304,128]{2,1,0:T(8,128)(2,1)S(1)}, u32[]{:S(2)}, u32[]{:S(2)}) async-start(bf16[8,304,128]{2,1,0:T(8,128)(2,1)} %shard_map.284), calls=%async_computation.8 | async-start | bytes 1245184 | tf_op jit(solution)/shard_map/all_to_all | solution.py:917
  403.8 14.8 %all-to-all-start.9 = ((bf16[16,48,384]{2,1,0:T(8,128)(2,1)}), bf16[16,48,384]{2,1,0:T(8,128)(2,1)S(1)}, u32[]{:S(2)}, u32[]{:S(2)}) async-start(bf16[16,48,384]{2,1,0:T(8,128)(2,1)} %bitcast.25), calls=%async_computation.10 | async-start | bytes 1179648 | tf_op jit(solution)/shard_map/all_to_all | solution.py:797
  407.4 41.3 %reduce-scatter.5.cloned.1.call-start = ((), (), s32[]{:S(2)}) async-start(), calls=%async_computation.15 | async-start | bytes 1474560 | tf_op jit(solution)/shard_map/reduce_scatter | solution.py:819
  423.6 22.7 %all-to-all-start.10 = ((bf16[16,48,384]{2,1,0:T(8,128)(2,1)}), bf16[16,48,384]{2,1,0:T(8,128)(2,1)S(1)}, u32[]{:S(2)}, u32[]{:S(2)}) async-start(bf16[16,48,384]{2,1,0:T(8,128)(2,1)} %shard_map.285), calls=%async_computation.11 | async-start | bytes 1179648 | tf_op jit(solution)/shard_map/all_to_all | solution.py:801
  427.3 91.8 %all-gather.3.cloned.1.call-start = ((), (), s32[]{:S(2)}) async-start(), calls=%async_computation.16 | async-start | bytes 2949120 | tf_op jit(solution)/shard_map/all_gather | solution.py:957
  497.0 14.1 %collective-permute-start.32 = (bf16[8,304,128]{2,1,0:T(8,128)(2,1)S(1)}, bf16[8,304,128]{2,1,0:T(8,128)(2,1)S(1)}, u32[]{:S(2)}, u32[]{:S(2)}) collective-permute-start(bf16[8,304,128]{2,1,0:T(8,128)(2,1)S(1)} %get-tuple-element.251), channel_id=1, source_target_pairs={{0,16},{16,0},{1,17},{17,1},{2,18},{18,2},{3,19},{19,3},{4,20},{20... | collective-permute-start | bytes 1867784 | tf_op jit(solution)/shard_map/ppermute | solution.py:752
  (65 other events, 350.0 us)
Sparse Core Ops, SparseCore 0:
  355.9 28.2 reduce-scatter.2
  411.1 36.5 reduce-scatter.4
  460.6 58.4 all-gather.2

commit v5 on v4

--- a/solution.py
+++ b/solution.py
@@ -673,36 +673,43 @@
     return keep, give
 
 
-def widened(gathered):
-    planes, _, rows, width = gathered.shape
-
-    def kernel(x_hbm, one_hbm, two_hbm, in_ref, out_ref, sems, sent):
-        order = [(p, k) for k in range(2) for p in range(planes)]
-        copies = [
-            pltpu.make_async_copy(x_hbm.at[p, k], in_ref.at[p, k], sems.at[p, k]) for p, k in order
-        ]
-        for copy in copies:
-            copy.start()
+def widened(flag, mine, other):
+    units, width = mine.shape
+    steps = blocks(units, 256)
+
+    def kernel(flag_ref, mine_hbm, other_hbm, one_hbm, two_hbm, in_ref, out_ref, sems, sent):
+        sources = ((mine_hbm, other_hbm), (other_hbm, mine_hbm))
+        copies = chosen(
+            flag_ref[0],
+            [
+                (tuple(src.at[a:b] for src in pair), in_ref.at[k, a:b])
+                for k, pair in enumerate(sources)
+                for a, b in steps
+            ],
+            sems,
+        )
         writes = []
-        for copy, (p, k) in zip(copies, order):
-            copy.wait()
-            out_ref[p, k] = in_ref[p, k].astype(F32)
-            target = (one_hbm, two_hbm)[k].at[p * rows : (p + 1) * rows]
-            writes.append(pltpu.make_async_copy(out_ref.at[p, k], target, sent.at[p, k]))
-            writes[-1].start()
+        for k, target in enumerate((one_hbm, two_hbm)):
+            for i, (a, b) in enumerate(steps):
+                copies[k * len(steps) + i].wait()
+                out_ref[k, a:b] = in_ref[k, a:b].astype(F32)
+                writes.append(
+                    pltpu.make_async_copy(out_ref.at[k, a:b], target.at[a:b], sent.at[k, i])
+                )
+                writes[-1].start()
         for write in writes:
             write.wait()
 
     return call(
         kernel,
-        (shape((planes * rows, width), F32),) * 2,
-        (gathered,),
-        [HBM],
+        (shape((units, width), F32),) * 2,
+        (flag, mine, other),
+        [SMEM] + [HBM] * 2,
         [
-            pltpu.VMEM(gathered.shape, BF),
-            pltpu.VMEM(gathered.shape, F32),
-            pltpu.SemaphoreType.DMA((planes, 2)),
-            pltpu.SemaphoreType.DMA((planes, 2)),
+            pltpu.VMEM((2, units, width), BF),
+            pltpu.VMEM((2, units, width), F32),
+            pltpu.SemaphoreType.DMA((2 * len(steps),)),
+            pltpu.SemaphoreType.DMA((2, len(steps))),
         ],
         out_specs=(HBM, HBM),
     )
@@ -953,9 +960,10 @@
     early, late, _ = lax.optimization_barrier((early, late, sent))
     mine, other = jnp.where(is_first, early, late), jnp.where(is_first, late, early)
     other = swapped(other, "section")
-    pair = jnp.stack(ordered(mine, other))
-    pair = lax.all_gather(pair, ("half", "rest"), axis=0, tiled=False)
-    one, two = widened(pair.reshape((-1,) + pair.shape[-3:]))
+    mine, other = (
+        lax.all_gather(shard, ("half", "rest"), axis=0, tiled=True) for shard in (mine, other)
+    )
+    one, two = widened(flags[0], mine, other)
     weight_sums = [one, two.reshape(width, units)]
 
     return (

time: 535 us -> 539 us (level)
  waiting for transfers between devices: 187 us -> 224 us
  blocking collectives: 112 us -> 75.7 us
    all_to_all x1 -> x0, blocking collectives: 36.4 us -> none  [shards(): got = lax.all_to_all(sent, PLANE, 0, 0, tiled=True)]
    all_to_all x0 -> x1, waiting for transfers between devices: none -> 23.3 us  [shards(): got = lax.all_to_all(sent, PLANE, 0, 0, tiled=True)]
    all_gather x1 -> x2, waiting for transfers between devices: 1.37 us -> 12.5 us  [shards(): lax.all_gather(shard, ('half', 'rest'), axis=0, tiled=True)]
    unnamed x90 -> x94, local copies, waits for them, and re-layouts: 17.5 us -> 18.9 us
  transfers between devices with their start and end apart: 44 -> 46, of which waited for: 30 -> 32; matrix products, arithmetic and copies ran while one was open for 3% -> 3% of each run, Pallas kernels for 16% -> 16%
where the time goes in v5:
time: 539 us; the launch traced here: 533 us
  waiting for transfers between devices  224 us (42%)
  Pallas kernels  135 us (25%)
  blocking collectives  75.7 us (14%)
  starting transfers between devices  47.9 us (9%)
  local copies, waits for them, and re-layouts  23.1 us (4%)
  between operations  16.4 us (3%)
  other arithmetic  11.3 us (2%)
    ppermute x34, waiting for transfers between devices, swapped(): lax.ppermute(array, axis, [(i, (i + by) % size) for i in range(size)])  146 us
    pallas_call x31, Pallas kernels, call(): pl.pallas_call(kernel, out_shape=outs, in_specs=specs or [VMEM] * len(arg...  125 us
    all_to_all x3, blocking collectives, fourier(): lax.all_to_all(mixed, RING, 0, 0, tiled=True).reshape(width, columns)  44.9 us
    all_to_all x2, blocking collectives, fourier(): got = lax.all_to_all(sent, RING, 0, 0, tiled=True)  30.8 us
    all_to_all x2, waiting for transfers between devices, fourier(): got = lax.all_to_all(sent, RING, 0, 0, tiled=True)  24.3 us
    all_to_all x1, waiting for transfers between devices, shards(): got = lax.all_to_all(sent, PLANE, 0, 0, tiled=True)  23.3 us
    unnamed x94, local copies, waits for them, and re-layouts  18.9 us
    ppermute x34, starting transfers between devices, swapped(): lax.ppermute(array, axis, [(i, (i + by) % size) for i in range(size)])  16.9 us
  transfers between devices with their start and end apart: 46, of which 32 were waited for; matrix products, arithmetic and copies ran while one was open for 3% of the time, Pallas kernels for 16%

profile of v5, /device:TPU:0, one launch (start us, length us, event | category | flops | bytes accessed | tf_op | source)
XLA Modules:
  0.0 533.3 jit_solution(12579027957056519546)
XLA Ops:
  11.8 6.4 %all-to-all-start = ((bf16[8,576,128]{2,1,0:T(8,128)(2,1)}), bf16[8,576,128]{2,1,0:T(8,128)(2,1)S(1)}, u32[]{:S(2)}, u32[]{:S(2)}) async-start(bf16[8,576,128]{2,1,0:T(8,128)(2,1)} %shard_map.257), calls=%async_computation | async-start | bytes 2359296 | tf_op jit(solution)/shard_map/all_to_all | solution.py:847
  22.6 24.4 %collective-permute-done.other1 = bf16[768,768]{1,0:T(8,128)(2,1)S(1)} collective-permute-done((bf16[768,768]{1,0:T(8,128)(2,1)S(1)}, bf16[768,768]{1,0:T(8,128)(2,1)S(1)}, u32[]{:S(2)}, u32[]{:S(2)}) %collective-permute-start) | collective-permute-done | bytes 1179680 | tf_op jit(solution)/shard_map/ppermute | solution.py:759
  64.0 13.8 %all-to-all-done.1.d_ref = bf16[16,48,384]{2,1,0:T(8,128)(2,1)S(1)} async-done(((bf16[16,48,384]{2,1,0:T(8,128)(2,1)}), bf16[16,48,384]{2,1,0:T(8,128)(2,1)S(1)}, u32[]{:S(2)}, u32[]{:S(2)}) %all-to-all-start.1) | async-done | bytes 589856 | tf_op jit(solution)/shard_map/all_to_all | solution.py:804
  82.0 16.1 %all_to_all.60 = bf16[16,48,384]{2,1,0:T(8,128)(2,1)S(1)} all-to-all(bf16[16,48,384]{2,1,0:T(8,128)(2,1)S(1)} %shard_map.259), channel_id=1, replica_groups=mesh['section'=2,'half'=2,'rest'=2,'side'=2,'core'=2] {'section','rest',..., dimensions={0} | all-to-all | bytes 1179648 | tf_op jit(solution)/shard_map/all_to_all | solution.py:808
  104.7 6.3 %shard_map.261 = (bf16[768,384]{1,0:T(8,128)(2,1)S(1)}, bf16[768,384]{1,0:T(8,128)(2,1)}, bf16[768,768]{1,0:T(8,128)(2,1)}, bf16[768,768]{1,0:T(8,128)(2,1)}) custom-call(s32[1]{0:T(128)} %bitcast.12.flag_ref, bf16[768,384]{1,0:T(8,128)(2,1)S(1)} %get-tuple-element.135.a_ref.refs_6_.refs_8_, bf16[768,384]{1,0:T(8,128)(2,1)} %copy-done.31, ...), custom_call_target="tpu_custom_call" | custom-call | flops 1811939328 | bytes 6291456 | tf_op jit(solution)/shard_map/pallas_call | solution.py:92
  111.8 5.8 %collective-permute-done.5.a_ref.refs_8_.refs_10_ = bf16[768,384]{1,0:T(8,128)(2,1)S(1)} collective-permute-done((bf16[768,384]{1,0:T(8,128)(2,1)S(1)}, bf16[768,384]{1,0:T(8,128)(2,1)S(1)}, u32[]{:S(2)}, u32[]{:S(2)}) %collective-permute-start.5) | collective-permute-done | bytes 589856 | tf_op jit(solution)/shard_map/ppermute | solution.py:759
  132.3 13.3 %collective-permute-done.10.refs_3_ = bf16[768,384]{1,0:T(8,128)(2,1)} collective-permute-done((bf16[768,384]{1,0:T(8,128)(2,1)}, bf16[768,384]{1,0:T(8,128)(2,1)}, u32[]{:S(2)}, u32[]{:S(2)}) %collective-permute-start.10) | collective-permute-done | bytes 589856 | tf_op jit(solution)/shard_map/ppermute | solution.py:759
  151.3 13.8 %all_to_all.61.d_ref = bf16[16,48,384]{2,1,0:T(8,128)(2,1)S(1)} all-to-all(bf16[16,48,384]{2,1,0:T(8,128)(2,1)S(1)} %bitcast.57), channel_id=1, replica_groups=mesh['section'=2,'half'=2,'rest'=2,'side'=2,'core'=2] {'section','rest',..., dimensions={0} | all-to-all | bytes 1179648 | tf_op jit(solution)/shard_map/all_to_all | solution.py:804
  169.3 14.2 %all_to_all.62 = bf16[16,48,384]{2,1,0:T(8,128)(2,1)S(1)} all-to-all(bf16[16,48,384]{2,1,0:T(8,128)(2,1)S(1)} %shard_map.265), channel_id=1, replica_groups=mesh['section'=2,'half'=2,'rest'=2,'side'=2,'core'=2] {'section','rest',..., dimensions={0} | all-to-all | bytes 1179648 | tf_op jit(solution)/shard_map/all_to_all | solution.py:808
  195.6 6.6 %collective-permute-done.12.a_ref.refs_8_.refs_10_ = bf16[768,384]{1,0:T(8,128)(2,1)S(1)} collective-permute-done((bf16[768,384]{1,0:T(8,128)(2,1)S(1)}, bf16[768,384]{1,0:T(8,128)(2,1)S(1)}, u32[]{:S(2)}, u32[]{:S(2)}) %collective-permute-start.12) | collective-permute-done | bytes 589856 | tf_op jit(solution)/shard_map/ppermute | solution.py:759
  213.5 14.7 %collective-permute-done.17.refs_3_ = bf16[768,384]{1,0:T(8,128)(2,1)S(1)} collective-permute-done((bf16[768,384]{1,0:T(8,128)(2,1)S(1)}, bf16[768,384]{1,0:T(8,128)(2,1)S(1)}, u32[]{:S(2)}, u32[]{:S(2)}) %collective-permute-start.17) | collective-permute-done | bytes 589856 | tf_op jit(solution)/shard_map/ppermute | solution.py:759
  274.7 7.4 %collective-permute-done.23.refs_2_ = bf16[768,384]{1,0:T(8,128)(2,1)S(1)} collective-permute-done((bf16[768,384]{1,0:T(8,128)(2,1)S(1)}, bf16[768,384]{1,0:T(8,128)(2,1)S(1)}, u32[]{:S(2)}, u32[]{:S(2)}) %collective-permute-start.23) | collective-permute-done | bytes 589856 | tf_op jit(solution)/shard_map/ppermute | solution.py:759
  287.0 16.9 %all_to_all.63.d_ref = bf16[16,48,384]{2,1,0:T(8,128)(2,1)S(1)} all-to-all(bf16[16,48,384]{2,1,0:T(8,128)(2,1)S(1)} %bitcast.56), channel_id=1, replica_groups=mesh['section'=2,'half'=2,'rest'=2,'side'=2,'core'=2] {'section','rest',..., dimensions={0} | all-to-all | bytes 1179648 | tf_op jit(solution)/shard_map/all_to_all | solution.py:804
  308.1 14.5 %all_to_all.64 = bf16[16,48,384]{2,1,0:T(8,128)(2,1)} all-to-all(bf16[16,48,384]{2,1,0:T(8,128)(2,1)S(1)} %shard_map.277), channel_id=1, replica_groups=mesh['section'=2,'half'=2,'rest'=2,'side'=2,'core'=2] {'section','rest',..., dimensions={0} | all-to-all | bytes 1179648 | tf_op jit(solution)/shard_map/all_to_all | solution.py:808
  329.1 6.5 %shard_map.279 = (bf16[768,384]{1,0:T(8,128)(2,1)S(1)}, bf16[768,384]{1,0:T(8,128)(2,1)}, bf16[768,768]{1,0:T(8,128)(2,1)}, f32[8,768]{1,0:T(8,128)S(1)}) custom-call(s32[1]{0:T(128)} %bitcast.12.flag_ref, bf16[768,384]{1,0:T(8,128)(2,1)S(1)} %get-tuple-element.197.a_ref.refs_2_.refs_0_.second_ref, bf16[768,384]{1,0:T(8,128)(2,1)} %copy-done.2, ...), custom_call_target="tpu_custom_call" | custom-call | flops 1811939328 | bytes 6291456 | tf_op jit(solution)/shard_map/pallas_call | solution.py:92
  335.7 6.4 %collective-permute-done.24.a_ref.refs_4_.refs_2_ = bf16[768,384]{1,0:T(8,128)(2,1)S(1)} collective-permute-done((bf16[768,384]{1,0:T(8,128)(2,1)S(1)}, bf16[768,384]{1,0:T(8,128)(2,1)S(1)}, u32[]{:S(2)}, u32[]{:S(2)}) %collective-permute-start.24) | collective-permute-done | bytes 589856 | tf_op jit(solution)/shard_map/ppermute | solution.py:759
  344.9 6.6 %shard_map.280 = (bf16[768,384]{1,0:T(8,128)(2,1)S(1)}, bf16[768,384]{1,0:T(8,128)(2,1)}, bf16[768,768]{1,0:T(8,128)(2,1)}, f32[8,768]{1,0:T(8,128)S(1)}) custom-call(s32[1]{0:T(128)} %bitcast.12.flag_ref, bf16[768,384]{1,0:T(8,128)(2,1)S(1)} %collective-permute-done.24.a_ref.refs_4_.refs_2_, bf16[768,384]{1,0:T(8,128)(2,1)} %copy-done.25, ...), custom_call_target="tpu_custom_call" | custom-call | flops 1811939328 | bytes 6291456 | tf_op jit(solution)/shard_map/pallas_call | solution.py:92
  384.4 16.2 %collective-permute-done.30 = bf16[768,768]{1,0:T(8,128)(2,1)} collective-permute-done((bf16[768,768]{1,0:T(8,128)(2,1)}, bf16[768,768]{1,0:T(8,128)(2,1)}, u32[]{:S(2)}, u32[]{:S(2)}) %collective-permute-start.30) | collective-permute-done | bytes 1179680 | tf_op jit(solution)/shard_map/ppermute | solution.py:759
  408.3 10.5 %all-to-all-done.9.d_ref = bf16[16,48,384]{2,1,0:T(8,128)(2,1)S(1)} async-done(((bf16[16,48,384]{2,1,0:T(8,128)(2,1)}), bf16[16,48,384]{2,1,0:T(8,128)(2,1)S(1)}, u32[]{:S(2)}, u32[]{:S(2)}) %all-to-all-start.9) | async-done | bytes 589856 | tf_op jit(solution)/shard_map/all_to_all | solution.py:804
  431.2 15.4 %all-to-all-done.10 = bf16[16,48,384]{2,1,0:T(8,128)(2,1)S(1)} async-done(((bf16[16,48,384]{2,1,0:T(8,128)(2,1)}), bf16[16,48,384]{2,1,0:T(8,128)(2,1)S(1)}, u32[]{:S(2)}, u32[]{:S(2)}) %all-to-all-start.10) | async-done | bytes 589856 | tf_op jit(solution)/shard_map/all_to_all | solution.py:808
  455.7 8.8 %collective-permute-done.33 = bf16[192,768]{1,0:T(8,128)(2,1)S(1)} collective-permute-done((bf16[192,768]{1,0:T(8,128)(2,1)S(1)}, bf16[192,768]{1,0:T(8,128)(2,1)S(1)}, u32[]{:S(2)}, u32[]{:S(2)}) %collective-permute-start.33) | collective-permute-done | bytes 294944 | tf_op jit(solution)/shard_map/ppermute | solution.py:759
  465.2 23.3 %all-to-all-done.11 = bf16[8,304,128]{2,1,0:T(8,128)(2,1)S(1)} async-done(((bf16[8,304,128]{2,1,0:T(8,128)(2,1)}), bf16[8,304,128]{2,1,0:T(8,128)(2,1)S(1)}, u32[]{:S(2)}, u32[]{:S(2)}) %all-to-all-start.11) | async-done | bytes 622624 | tf_op jit(solution)/shard_map/all_to_all | solution.py:943
  488.6 13.9 %collective-permute-done.32 = bf16[8,304,128]{2,1,0:T(8,128)(2,1)S(1)} collective-permute-done((bf16[8,304,128]{2,1,0:T(8,128)(2,1)S(1)}, bf16[8,304,128]{2,1,0:T(8,128)(2,1)S(1)}, u32[]{:S(2)}, u32[]{:S(2)}) %collective-permute-start.32) | collective-permute-done | bytes 622624 | tf_op jit(solution)/shard_map/ppermute | solution.py:759
  508.9 12.5 %all-gather.5.cloned.1.call-done.other_hbm = bf16[768,768]{1,0:T(8,128)(2,1)} async-done(((bf16[192,768]{1,0:T(8,128)(2,1)}), bf16[768,768]{1,0:T(8,128)(2,1)}) %all-gather.5.cloned.1.call-update) | async-done | bytes 1179664 | tf_op jit(solution)/shard_map/all_gather | solution.py:964
  (271 shorter events, 222.4 us)
Async XLA Ops:
  11.8 35.8 %all-to-all-start = ((bf16[8,576,128]{2,1,0:T(8,128)(2,1)}), bf16[8,576,128]{2,1,0:T(8,128)(2,1)S(1)}, u32[]{:S(2)}, u32[]{:S(2)}) async-start(bf16[8,576,128]{2,1,0:T(8,128)(2,1)} %shard_map.257), calls=%async_computation | async-start | bytes 2359296 | tf_op jit(solution)/shard_map/all_to_all | solution.py:847
  18.2 28.8 %collective-permute-start = (bf16[768,768]{1,0:T(8,128)(2,1)S(1)}, bf16[768,768]{1,0:T(8,128)(2,1)S(1)}, u32[]{:S(2)}, u32[]{:S(2)}) collective-permute-start(bf16[768,768]{1,0:T(8,128)(2,1)S(1)} %bitcast.66), channel_id=1, source_target_pairs={{0,16},{16,0},{1,17},{17,1},{2,18},{18,2},{3,19},{19,3},{4,20},{20... | collective-permute-start | bytes 3538952 | tf_op jit(solution)/shard_map/ppermute | solution.py:759
  20.6 37.0 %collective-permute-start.2 = (f32[1728]{0:T(1024)S(1)}, f32[1728]{0:T(1024)S(1)}, u32[]{:S(2)}, u32[]{:S(2)}) collective-permute-start(f32[1728]{0:T(1024)S(1)} %concatenate.12), channel_id=1, source_target_pairs={{0,16},{16,0},{1,17},{17,1},{2,18},{18,2},{3,19},{19,3},{4,20},{20... | collective-permute-start | bytes 20744 | tf_op jit(solution)/shard_map/ppermute | solution.py:759
  21.1 60.9 %collective-permute-start.1 = (bf16[768,768]{1,0:T(8,128)(2,1)}, bf16[768,768]{1,0:T(8,128)(2,1)}, u32[]{:S(2)}, u32[]{:S(2)}) collective-permute-start(bf16[768,768]{1,0:T(8,128)(2,1)} %bitcast.3.own2), channel_id=1, source_target_pairs={{0,16},{16,0},{1,17},{17,1},{2,18},{18,2},{3,19},{19,3},{4,20},{20... | collective-permute-start | bytes 3538952 | tf_op jit(solution)/shard_map/ppermute | solution.py:759
  52.8 25.0 %all-to-all-start.1 = ((bf16[16,48,384]{2,1,0:T(8,128)(2,1)}), bf16[16,48,384]{2,1,0:T(8,128)(2,1)S(1)}, u32[]{:S(2)}, u32[]{:S(2)}) async-start(bf16[16,48,384]{2,1,0:T(8,128)(2,1)} %bitcast.2), calls=%async_computation.1 | async-start | bytes 1179648 | tf_op jit(solution)/shard_map/all_to_all | solution.py:804
  101.9 15.7 %collective-permute-start.5 = (bf16[768,384]{1,0:T(8,128)(2,1)S(1)}, bf16[768,384]{1,0:T(8,128)(2,1)S(1)}, u32[]{:S(2)}, u32[]{:S(2)}) collective-permute-start(bf16[768,384]{1,0:T(8,128)(2,1)S(1)} %get-tuple-element.135.a_ref.refs_6_.refs_8_), channel_id=1, source_target_pairs={{0,2},{2,0},{1,3},{3,1},{4,6},{6,4},{5,7},{7,5},{8,10},{10,8},{9,1... | collective-permute-start | bytes 1769480 | tf_op jit(solution)/shard_map/ppermute | solution.py:759
  129.6 16.0 %collective-permute-start.10 = (bf16[768,384]{1,0:T(8,128)(2,1)}, bf16[768,384]{1,0:T(8,128)(2,1)}, u32[]{:S(2)}, u32[]{:S(2)}) collective-permute-start(bf16[768,384]{1,0:T(8,128)(2,1)} %add_convert_fusion.5), channel_id=1, source_target_pairs={{0,2},{2,0},{1,3},{3,1},{4,6},{6,4},{5,7},{7,5},{8,10},{10,8},{9,1... | collective-permute-start | bytes 1769480 | tf_op jit(solution)/shard_map/ppermute | solution.py:759
  186.5 15.7 %collective-permute-start.12 = (bf16[768,384]{1,0:T(8,128)(2,1)S(1)}, bf16[768,384]{1,0:T(8,128)(2,1)S(1)}, u32[]{:S(2)}, u32[]{:S(2)}) collective-permute-start(bf16[768,384]{1,0:T(8,128)(2,1)S(1)} %get-tuple-element.157.a_ref.refs_6_.refs_8_), channel_id=1, source_target_pairs={{0,2},{2,0},{1,3},{3,1},{4,6},{6,4},{5,7},{7,5},{8,10},{10,8},{9,1... | collective-permute-start | bytes 1769480 | tf_op jit(solution)/shard_map/ppermute | solution.py:759
  212.8 15.4 %collective-permute-start.17 = (bf16[768,384]{1,0:T(8,128)(2,1)S(1)}, bf16[768,384]{1,0:T(8,128)(2,1)S(1)}, u32[]{:S(2)}, u32[]{:S(2)}) collective-permute-start(bf16[768,384]{1,0:T(8,128)(2,1)S(1)} %add_convert_fusion.4), channel_id=1, source_target_pairs={{0,2},{2,0},{1,3},{3,1},{4,6},{6,4},{5,7},{7,5},{8,10},{10,8},{9,1... | collective-permute-start | bytes 1769480 | tf_op jit(solution)/shard_map/ppermute | solution.py:759
  233.3 19.5 %collective-permute-start.18 = (bf16[768,384]{1,0:T(8,128)(2,1)S(1)}, bf16[768,384]{1,0:T(8,128)(2,1)S(1)}, u32[]{:S(2)}, u32[]{:S(2)}) collective-permute-start(bf16[768,384]{1,0:T(8,128)(2,1)S(1)} %get-tuple-element.169.a_ref.refs_2_.refs_0_.second_ref), channel_id=1, source_target_pairs={{0,2},{2,0},{1,3},{3,1},{4,6},{6,4},{5,7},{7,5},{8,10},{10,8},{9,1... | collective-permute-start | bytes 1769480 | tf_op jit(solution)/shard_map/ppermute | solution.py:759
  235.2 46.8 %all-to-all-start.5 = ((bf16[16,304,128]{2,1,0:T(8,128)(2,1)}), bf16[16,304,128]{2,1,0:T(8,128)(2,1)}, u32[]{:S(2)}, u32[]{:S(2)}) async-start(bf16[16,304,128]{2,1,0:T(8,128)(2,1)} %shard_map.275), calls=%async_computation.5 | async-start | bytes 2490368 | tf_op jit(solution)/shard_map/all_to_all | solution.py:885
  239.6 163.6 %reduce-scatter.3.cloned.1.call-start = ((), (), s32[]{:S(2)}) async-start(), calls=%async_computation.14 | async-start | bytes 1474560 | tf_op jit(solution)/shard_map/reduce_scatter | solution.py:826
  263.6 18.4 %collective-permute-start.23 = (bf16[768,384]{1,0:T(8,128)(2,1)S(1)}, bf16[768,384]{1,0:T(8,128)(2,1)S(1)}, u32[]{:S(2)}, u32[]{:S(2)}) collective-permute-start(bf16[768,384]{1,0:T(8,128)(2,1)S(1)} %add_convert_fusion.3), channel_id=1, source_target_pairs={{0,2},{2,0},{1,3},{3,1},{4,6},{6,4},{5,7},{7,5},{8,10},{10,8},{9,1... | collective-permute-start | bytes 1769480 | tf_op jit(solution)/shard_map/ppermute | solution.py:759
  326.3 15.8 %collective-permute-start.24 = (bf16[768,384]{1,0:T(8,128)(2,1)S(1)}, bf16[768,384]{1,0:T(8,128)(2,1)S(1)}, u32[]{:S(2)}, u32[]{:S(2)}) collective-permute-start(bf16[768,384]{1,0:T(8,128)(2,1)S(1)} %get-tuple-element.197.a_ref.refs_2_.refs_0_.second_ref), channel_id=1, source_target_pairs={{0,2},{2,0},{1,3},{3,1},{4,6},{6,4},{5,7},{7,5},{8,10},{10,8},{9,1... | collective-permute-start | bytes 1769480 | tf_op jit(solution)/shard_map/ppermute | solution.py:759
  326.7 28.0 %collective-permute-start.31 = (bf16[768,768]{1,0:T(8,128)(2,1)S(1)}, bf16[768,768]{1,0:T(8,128)(2,1)S(1)}, u32[]{:S(2)}, u32[]{:S(2)}) collective-permute-start(bf16[768,768]{1,0:T(8,128)(2,1)S(1)} %copy-done.35), channel_id=1, source_target_pairs={{0,16},{16,0},{1,17},{17,1},{2,18},{18,2},{3,19},{19,3},{4,20},{20... | collective-permute-start | bytes 3538952 | tf_op jit(solution)/shard_map/ppermute | solution.py:759
  351.7 21.5 %collective-permute-start.26 = (bf16[768,384]{1,0:T(8,128)(2,1)}, bf16[768,384]{1,0:T(8,128)(2,1)}, u32[]{:S(2)}, u32[]{:S(2)}) collective-permute-start(bf16[768,384]{1,0:T(8,128)(2,1)} %get-tuple-element.204), channel_id=1, source_target_pairs={{0,1},{1,0},{2,3},{3,2},{4,5},{5,4},{6,7},{7,6},{8,9},{9,8},{10,11... | collective-permute-start | bytes 1769480 | tf_op jit(solution)/shard_map/ppermute | solution.py:759
  358.2 15.0 %collective-permute-start.29 = (bf16[768,384]{1,0:T(8,128)(2,1)}, bf16[768,384]{1,0:T(8,128)(2,1)S(1)}, u32[]{:S(2)}, u32[]{:S(2)}) collective-permute-start(bf16[768,384]{1,0:T(8,128)(2,1)} %add_convert_fusion.2), channel_id=1, source_target_pairs={{0,2},{2,0},{1,3},{3,1},{4,6},{6,4},{5,7},{7,5},{8,10},{10,8},{9,1... | collective-permute-start | bytes 1769480 | tf_op jit(solution)/shard_map/ppermute | solution.py:759
  373.2 27.4 %collective-permute-start.30 = (bf16[768,768]{1,0:T(8,128)(2,1)}, bf16[768,768]{1,0:T(8,128)(2,1)}, u32[]{:S(2)}, u32[]{:S(2)}) collective-permute-start(bf16[768,768]{1,0:T(8,128)(2,1)} %shard_map.282), channel_id=1, source_target_pairs={{0,16},{16,0},{1,17},{17,1},{2,18},{18,2},{3,19},{19,3},{4,20},{20... | collective-permute-start | bytes 3538952 | tf_op jit(solution)/shard_map/ppermute | solution.py:759
  380.4 22.7 %all-to-all-start.8 = ((bf16[8,304,128]{2,1,0:T(8,128)(2,1)}), bf16[8,304,128]{2,1,0:T(8,128)(2,1)S(1)}, u32[]{:S(2)}, u32[]{:S(2)}) async-start(bf16[8,304,128]{2,1,0:T(8,128)(2,1)} %shard_map.284), calls=%async_computation.8 | async-start | bytes 1245184 | tf_op jit(solution)/shard_map/all_to_all | solution.py:924
  407.6 42.1 %reduce-scatter.5.cloned.1.call-start = ((), (), s32[]{:S(2)}) async-start(), calls=%async_computation.15 | async-start | bytes 1474560 | tf_op jit(solution)/shard_map/reduce_scatter | solution.py:826
  423.8 22.7 %all-to-all-start.10 = ((bf16[16,48,384]{2,1,0:T(8,128)(2,1)}), bf16[16,48,384]{2,1,0:T(8,128)(2,1)S(1)}, u32[]{:S(2)}, u32[]{:S(2)}) async-start(bf16[16,48,384]{2,1,0:T(8,128)(2,1)} %shard_map.285), calls=%async_computation.11 | async-start | bytes 1179648 | tf_op jit(solution)/shard_map/all_to_all | solution.py:808
  427.5 81.4 %all-gather.3.cloned.1.call-start = ((), (), s32[]{:S(2)}) async-start(), calls=%async_computation.16 | async-start | bytes 1474560 | tf_op jit(solution)/shard_map/all_gather | solution.py:964
  451.4 37.0 %all-to-all-start.11 = ((bf16[8,304,128]{2,1,0:T(8,128)(2,1)}), bf16[8,304,128]{2,1,0:T(8,128)(2,1)S(1)}, u32[]{:S(2)}, u32[]{:S(2)}) async-start(bf16[8,304,128]{2,1,0:T(8,128)(2,1)} %shard_map.288), calls=%async_computation.12 | async-start | bytes 1245184 | tf_op jit(solution)/shard_map/all_to_all | solution.py:943
  455.1 66.4 %all-gather.5.cloned.1.call-start = ((), (), s32[]{:S(2)}) async-start(), calls=%async_computation.17 | async-start | bytes 1474560 | tf_op jit(solution)/shard_map/all_gather | solution.py:964
  (69 other events, 381.2 us)
Sparse Core Ops, SparseCore 0:
  356.2 28.2 reduce-scatter.2
  411.3 36.5 reduce-scatter.4
  451.5 40.2 all-gather.2
  493.3 28.1 all-gather.4

commit v6 on v4

--- a/solution.py
+++ b/solution.py
@@ -838,14 +838,15 @@
 
     got = send_pencils((inputs, cotangent), section, sections, halves, mps, sorting)
     got = lax.all_to_all(got, PLANE, 0, 0, tiled=True)
-    got, other_one = lax.optimization_barrier((got, other_one))
     low, sent = take_pencils(got, 0, 2, halves, mps, count, packed)
     up, _ = lax.optimization_barrier((got, sent))
     flags = [is_first.astype(jnp.int32).reshape(1), (1 - is_first.astype(jnp.int32)).reshape(1)]
     saved, outs, hits = [], [], jnp.zeros((), F32)
     for layer in range(2):
         if layer == 0:
-            mixed, other_two, table, biases = fourier(sent, other_two, table, biases)
+            mixed, other_one, other_two, table, biases = fourier(
+                sent, other_one, other_two, table, biases
+            )
         else:
             mixed = fourier(sent)
         unit1, inv1, normed = first_norm(mixed, low, unpack, factor, table, layer)

time: 535 us -> 535 us (level)
    all_to_all x1, waiting for transfers between devices: 0.56 us -> 25.7 us  [shards(): got = lax.all_to_all(got, PLANE, 0, 0, tiled=True)]
    ppermute x34, waiting for transfers between devices: 145 us -> 120 us  [swapped(): lax.ppermute(array, axis, [(i, (i + by) % size) for i in range(size)])]
    unnamed x90 -> x98, local copies, waits for them, and re-layouts: 17.5 us -> 16.8 us
  transfers between devices with their start and end apart: 44 -> 44, of which waited for: 30 -> 29; matrix products, arithmetic and copies ran while one was open for 3% -> 2% of each run, Pallas kernels for 16% -> 16%
where the time goes in v6:
time: 535 us; the launch traced here: 529 us
  waiting for transfers between devices  190 us (36%)
  Pallas kernels  135 us (25%)
  blocking collectives  111 us (21%)
  starting transfers between devices  45 us (8%)
  local copies, waits for them, and re-layouts  20.3 us (4%)
  between operations  16.4 us (3%)
  other arithmetic  11.7 us (2%)
    pallas_call x31, Pallas kernels, call(): pl.pallas_call(kernel, out_shape=outs, in_specs=specs or [VMEM] * len(arg...  125 us
    ppermute x34, waiting for transfers between devices, swapped(): lax.ppermute(array, axis, [(i, (i + by) % size) for i in range(size)])  120 us
    all_to_all x3, blocking collectives, fourier(): lax.all_to_all(mixed, RING, 0, 0, tiled=True).reshape(width, columns)  43.7 us
    all_to_all x1, blocking collectives, shards(): got = lax.all_to_all(sent, PLANE, 0, 0, tiled=True)  36.4 us
    all_to_all x2, blocking collectives, fourier(): got = lax.all_to_all(sent, RING, 0, 0, tiled=True)  31.1 us
    all_to_all x2, waiting for transfers between devices, fourier(): got = lax.all_to_all(sent, RING, 0, 0, tiled=True)  26.8 us
    all_to_all x1, waiting for transfers between devices, shards(): got = lax.all_to_all(got, PLANE, 0, 0, tiled=True)  25.7 us
    ppermute x34, starting transfers between devices, swapped(): lax.ppermute(array, axis, [(i, (i + by) % size) for i in range(size)])  17.9 us
  transfers between devices with their start and end apart: 44, of which 29 were waited for; matrix products, arithmetic and copies ran while one was open for 2% of the time, Pallas kernels for 16%

profile of v6, /device:TPU:0, one launch (start us, length us, event | category | flops | bytes accessed | tf_op | source)
XLA Modules:
  0.0 529.2 jit_solution(14802472867729119519)
XLA Ops:
  11.8 6.4 %all-to-all-start = ((bf16[8,576,128]{2,1,0:T(8,128)(2,1)}), bf16[8,576,128]{2,1,0:T(8,128)(2,1)S(1)}, u32[]{:S(2)}, u32[]{:S(2)}) async-start(bf16[8,576,128]{2,1,0:T(8,128)(2,1)} %shard_map.257), calls=%async_computation | async-start | bytes 2359296 | tf_op jit(solution)/shard_map/all_to_all | solution.py:840
  21.9 25.7 %all-to-all-done.refs_0_ = bf16[8,576,128]{2,1,0:T(8,128)(2,1)S(1)} async-done(((bf16[8,576,128]{2,1,0:T(8,128)(2,1)}), bf16[8,576,128]{2,1,0:T(8,128)(2,1)S(1)}, u32[]{:S(2)}, u32[]{:S(2)}) %all-to-all-start) | async-done | bytes 1179680 | tf_op jit(solution)/shard_map/all_to_all | solution.py:840
  63.0 16.4 %all-to-all-done.1.d_ref = bf16[16,48,384]{2,1,0:T(8,128)(2,1)S(1)} async-done(((bf16[16,48,384]{2,1,0:T(8,128)(2,1)}), bf16[16,48,384]{2,1,0:T(8,128)(2,1)S(1)}, u32[]{:S(2)}, u32[]{:S(2)}) %all-to-all-start.1) | async-done | bytes 589856 | tf_op jit(solution)/shard_map/all_to_all | solution.py:797
  83.6 15.0 %all_to_all.60 = bf16[16,48,384]{2,1,0:T(8,128)(2,1)S(1)} all-to-all(bf16[16,48,384]{2,1,0:T(8,128)(2,1)S(1)} %shard_map.259), channel_id=1, replica_groups=mesh['section'=2,'half'=2,'rest'=2,'side'=2,'core'=2] {'section','rest',..., dimensions={0} | all-to-all | bytes 1179648 | tf_op jit(solution)/shard_map/all_to_all | solution.py:801
  105.2 6.3 %shard_map.261 = (bf16[768,384]{1,0:T(8,128)(2,1)S(1)}, bf16[768,384]{1,0:T(8,128)(2,1)}, bf16[768,768]{1,0:T(8,128)(2,1)}, bf16[768,768]{1,0:T(8,128)(2,1)}) custom-call(s32[1]{0:T(128)} %bitcast.12.flag_ref, bf16[768,384]{1,0:T(8,128)(2,1)S(1)} %get-tuple-element.133.a_ref.refs_6_.refs_8_, bf16[768,384]{1,0:T(8,128)(2,1)} %copy-done.30, ...), custom_call_target="tpu_custom_call" | custom-call | flops 1811939328 | bytes 6291456 | tf_op jit(solution)/shard_map/pallas_call | solution.py:92
  112.3 5.8 %collective-permute-done.5.a_ref.refs_8_.refs_10_ = bf16[768,384]{1,0:T(8,128)(2,1)S(1)} collective-permute-done((bf16[768,384]{1,0:T(8,128)(2,1)S(1)}, bf16[768,384]{1,0:T(8,128)(2,1)S(1)}, u32[]{:S(2)}, u32[]{:S(2)}) %collective-permute-start.5) | collective-permute-done | bytes 589856 | tf_op jit(solution)/shard_map/ppermute | solution.py:752
  132.8 13.3 %collective-permute-done.10.refs_3_ = bf16[768,384]{1,0:T(8,128)(2,1)} collective-permute-done((bf16[768,384]{1,0:T(8,128)(2,1)}, bf16[768,384]{1,0:T(8,128)(2,1)}, u32[]{:S(2)}, u32[]{:S(2)}) %collective-permute-start.10) | collective-permute-done | bytes 589856 | tf_op jit(solution)/shard_map/ppermute | solution.py:752
  151.8 13.8 %all_to_all.61.d_ref = bf16[16,48,384]{2,1,0:T(8,128)(2,1)S(1)} all-to-all(bf16[16,48,384]{2,1,0:T(8,128)(2,1)S(1)} %bitcast.62), channel_id=1, replica_groups=mesh['section'=2,'half'=2,'rest'=2,'side'=2,'core'=2] {'section','rest',..., dimensions={0} | all-to-all | bytes 1179648 | tf_op jit(solution)/shard_map/all_to_all | solution.py:797
  169.8 14.2 %all_to_all.62 = bf16[16,48,384]{2,1,0:T(8,128)(2,1)S(1)} all-to-all(bf16[16,48,384]{2,1,0:T(8,128)(2,1)S(1)} %shard_map.265), channel_id=1, replica_groups=mesh['section'=2,'half'=2,'rest'=2,'side'=2,'core'=2] {'section','rest',..., dimensions={0} | all-to-all | bytes 1179648 | tf_op jit(solution)/shard_map/all_to_all | solution.py:801
  196.1 6.7 %collective-permute-done.12.a_ref.refs_8_.refs_10_ = bf16[768,384]{1,0:T(8,128)(2,1)S(1)} collective-permute-done((bf16[768,384]{1,0:T(8,128)(2,1)S(1)}, bf16[768,384]{1,0:T(8,128)(2,1)S(1)}, u32[]{:S(2)}, u32[]{:S(2)}) %collective-permute-start.12) | collective-permute-done | bytes 589856 | tf_op jit(solution)/shard_map/ppermute | solution.py:752
  213.9 14.8 %collective-permute-done.17.refs_3_ = bf16[768,384]{1,0:T(8,128)(2,1)S(1)} collective-permute-done((bf16[768,384]{1,0:T(8,128)(2,1)S(1)}, bf16[768,384]{1,0:T(8,128)(2,1)S(1)}, u32[]{:S(2)}, u32[]{:S(2)}) %collective-permute-start.17) | collective-permute-done | bytes 589856 | tf_op jit(solution)/shard_map/ppermute | solution.py:752
  247.3 6.1 %collective-permute-done.18.a_ref.refs_4_.refs_2_ = bf16[768,384]{1,0:T(8,128)(2,1)S(1)} collective-permute-done((bf16[768,384]{1,0:T(8,128)(2,1)S(1)}, bf16[768,384]{1,0:T(8,128)(2,1)S(1)}, u32[]{:S(2)}, u32[]{:S(2)}) %collective-permute-start.18) | collective-permute-done | bytes 589856 | tf_op jit(solution)/shard_map/ppermute | solution.py:752
  276.1 6.2 %collective-permute-done.23.refs_2_ = bf16[768,384]{1,0:T(8,128)(2,1)} collective-permute-done((bf16[768,384]{1,0:T(8,128)(2,1)S(1)}, bf16[768,384]{1,0:T(8,128)(2,1)}, u32[]{:S(2)}, u32[]{:S(2)}) %collective-permute-start.23) | collective-permute-done | bytes 589856 | tf_op jit(solution)/shard_map/ppermute | solution.py:752
  286.9 17.3 %all_to_all.63.d_ref = bf16[16,48,384]{2,1,0:T(8,128)(2,1)S(1)} all-to-all(bf16[16,48,384]{2,1,0:T(8,128)(2,1)S(1)} %bitcast.61), channel_id=1, replica_groups=mesh['section'=2,'half'=2,'rest'=2,'side'=2,'core'=2] {'section','rest',..., dimensions={0} | all-to-all | bytes 1179648 | tf_op jit(solution)/shard_map/all_to_all | solution.py:797
  308.3 14.5 %all_to_all.64 = bf16[16,48,384]{2,1,0:T(8,128)(2,1)} all-to-all(bf16[16,48,384]{2,1,0:T(8,128)(2,1)S(1)} %shard_map.277), channel_id=1, replica_groups=mesh['section'=2,'half'=2,'rest'=2,'side'=2,'core'=2] {'section','rest',..., dimensions={0} | all-to-all | bytes 1179648 | tf_op jit(solution)/shard_map/all_to_all | solution.py:801
  329.4 6.6 %shard_map.279 = (bf16[768,384]{1,0:T(8,128)(2,1)S(1)}, bf16[768,384]{1,0:T(8,128)(2,1)}, bf16[768,768]{1,0:T(8,128)(2,1)}, f32[8,768]{1,0:T(8,128)S(1)}) custom-call(s32[1]{0:T(128)} %bitcast.12.flag_ref, bf16[768,384]{1,0:T(8,128)(2,1)S(1)} %get-tuple-element.195.a_ref.refs_2_.refs_0_.second_ref, bf16[768,384]{1,0:T(8,128)(2,1)} %copy-done.2, ...), custom_call_target="tpu_custom_call" | custom-call | flops 1811939328 | bytes 6291456 | tf_op jit(solution)/shard_map/pallas_call | solution.py:92
  335.9 6.4 %collective-permute-done.24.a_ref.refs_4_.refs_2_ = bf16[768,384]{1,0:T(8,128)(2,1)S(1)} collective-permute-done((bf16[768,384]{1,0:T(8,128)(2,1)S(1)}, bf16[768,384]{1,0:T(8,128)(2,1)S(1)}, u32[]{:S(2)}, u32[]{:S(2)}) %collective-permute-start.24) | collective-permute-done | bytes 589856 | tf_op jit(solution)/shard_map/ppermute | solution.py:752
  345.2 6.6 %shard_map.280 = (bf16[768,384]{1,0:T(8,128)(2,1)S(1)}, bf16[768,384]{1,0:T(8,128)(2,1)}, bf16[768,768]{1,0:T(8,128)(2,1)}, f32[8,768]{1,0:T(8,128)S(1)}) custom-call(s32[1]{0:T(128)} %bitcast.12.flag_ref, bf16[768,384]{1,0:T(8,128)(2,1)S(1)} %collective-permute-done.24.a_ref.refs_4_.refs_2_, bf16[768,384]{1,0:T(8,128)(2,1)} %copy-done.24, ...), custom_call_target="tpu_custom_call" | custom-call | flops 1811939328 | bytes 6291456 | tf_op jit(solution)/shard_map/pallas_call | solution.py:92
  384.7 16.2 %collective-permute-done.30 = bf16[768,768]{1,0:T(8,128)(2,1)} collective-permute-done((bf16[768,768]{1,0:T(8,128)(2,1)}, bf16[768,768]{1,0:T(8,128)(2,1)}, u32[]{:S(2)}, u32[]{:S(2)}) %collective-permute-start.30) | collective-permute-done | bytes 1179680 | tf_op jit(solution)/shard_map/ppermute | solution.py:752
  407.9 10.4 %all-to-all-done.9.d_ref = bf16[16,48,384]{2,1,0:T(8,128)(2,1)S(1)} async-done(((bf16[16,48,384]{2,1,0:T(8,128)(2,1)}), bf16[16,48,384]{2,1,0:T(8,128)(2,1)S(1)}, u32[]{:S(2)}, u32[]{:S(2)}) %all-to-all-start.9) | async-done | bytes 589856 | tf_op jit(solution)/shard_map/all_to_all | solution.py:797
  430.7 15.4 %all-to-all-done.10 = bf16[16,48,384]{2,1,0:T(8,128)(2,1)S(1)} async-done(((bf16[16,48,384]{2,1,0:T(8,128)(2,1)}), bf16[16,48,384]{2,1,0:T(8,128)(2,1)S(1)}, u32[]{:S(2)}, u32[]{:S(2)}) %all-to-all-start.10) | async-done | bytes 589856 | tf_op jit(solution)/shard_map/all_to_all | solution.py:801
  450.6 7.7 %collective-permute-done.33 = bf16[192,768]{1,0:T(8,128)(2,1)S(1)} collective-permute-done((bf16[192,768]{1,0:T(8,128)(2,1)S(1)}, bf16[192,768]{1,0:T(8,128)(2,1)S(1)}, u32[]{:S(2)}, u32[]{:S(2)}) %collective-permute-start.33) | collective-permute-done | bytes 294944 | tf_op jit(solution)/shard_map/ppermute | solution.py:752
  460.2 36.4 %all_to_all.65 = bf16[8,304,128]{2,1,0:T(8,128)(2,1)S(1)} all-to-all(bf16[8,304,128]{2,1,0:T(8,128)(2,1)S(1)} %shard_map.288), channel_id=1, replica_groups=mesh['section'=2,'half'=2,'rest'=2,'side'=2,'core'=2] {'half','side','co..., dimensions={0} | all-to-all | bytes 1245184 | tf_op jit(solution)/shard_map/all_to_all | solution.py:937
  496.8 14.0 %collective-permute-done.32 = bf16[8,304,128]{2,1,0:T(8,128)(2,1)S(1)} collective-permute-done((bf16[8,304,128]{2,1,0:T(8,128)(2,1)S(1)}, bf16[8,304,128]{2,1,0:T(8,128)(2,1)S(1)}, u32[]{:S(2)}, u32[]{:S(2)}) %collective-permute-start.32) | collective-permute-done | bytes 622624 | tf_op jit(solution)/shard_map/ppermute | solution.py:752
  (273 shorter events, 210.6 us)
Async XLA Ops:
  11.8 35.8 %all-to-all-start = ((bf16[8,576,128]{2,1,0:T(8,128)(2,1)}), bf16[8,576,128]{2,1,0:T(8,128)(2,1)S(1)}, u32[]{:S(2)}, u32[]{:S(2)}) async-start(bf16[8,576,128]{2,1,0:T(8,128)(2,1)} %shard_map.257), calls=%async_computation | async-start | bytes 2359296 | tf_op jit(solution)/shard_map/all_to_all | solution.py:840
  18.4 38.2 %collective-permute-start.2 = (f32[1728]{0:T(1024)S(1)}, f32[1728]{0:T(1024)S(1)}, u32[]{:S(2)}, u32[]{:S(2)}) collective-permute-start(f32[1728]{0:T(1024)S(1)} %concatenate.12), channel_id=1, source_target_pairs={{0,16},{16,0},{1,17},{17,1},{2,18},{18,2},{3,19},{19,3},{4,20},{20... | collective-permute-start | bytes 20744 | tf_op jit(solution)/shard_map/ppermute | solution.py:752
  19.9 63.7 %collective-permute-start = (bf16[768,768]{1,0:T(8,128)(2,1)S(1)}, bf16[768,768]{1,0:T(8,128)(2,1)}, u32[]{:S(2)}, u32[]{:S(2)}) collective-permute-start(bf16[768,768]{1,0:T(8,128)(2,1)S(1)} %bitcast.71), channel_id=1, source_target_pairs={{0,16},{16,0},{1,17},{17,1},{2,18},{18,2},{3,19},{19,3},{4,20},{20... | collective-permute-start | bytes 3538952 | tf_op jit(solution)/shard_map/ppermute | solution.py:752
  20.4 63.2 %collective-permute-start.1 = (bf16[768,768]{1,0:T(8,128)(2,1)}, bf16[768,768]{1,0:T(8,128)(2,1)}, u32[]{:S(2)}, u32[]{:S(2)}) collective-permute-start(bf16[768,768]{1,0:T(8,128)(2,1)} %bitcast.72), channel_id=1, source_target_pairs={{0,16},{16,0},{1,17},{17,1},{2,18},{18,2},{3,19},{19,3},{4,20},{20... | collective-permute-start | bytes 3538952 | tf_op jit(solution)/shard_map/ppermute | solution.py:752
  52.8 26.6 %all-to-all-start.1 = ((bf16[16,48,384]{2,1,0:T(8,128)(2,1)}), bf16[16,48,384]{2,1,0:T(8,128)(2,1)S(1)}, u32[]{:S(2)}, u32[]{:S(2)}) async-start(bf16[16,48,384]{2,1,0:T(8,128)(2,1)} %bitcast.1), calls=%async_computation.1 | async-start | bytes 1179648 | tf_op jit(solution)/shard_map/all_to_all | solution.py:797
  102.3 15.7 %collective-permute-start.5 = (bf16[768,384]{1,0:T(8,128)(2,1)S(1)}, bf16[768,384]{1,0:T(8,128)(2,1)S(1)}, u32[]{:S(2)}, u32[]{:S(2)}) collective-permute-start(bf16[768,384]{1,0:T(8,128)(2,1)S(1)} %get-tuple-element.133.a_ref.refs_6_.refs_8_), channel_id=1, source_target_pairs={{0,2},{2,0},{1,3},{3,1},{4,6},{6,4},{5,7},{7,5},{8,10},{10,8},{9,1... | collective-permute-start | bytes 1769480 | tf_op jit(solution)/shard_map/ppermute | solution.py:752
  130.0 16.0 %collective-permute-start.10 = (bf16[768,384]{1,0:T(8,128)(2,1)}, bf16[768,384]{1,0:T(8,128)(2,1)}, u32[]{:S(2)}, u32[]{:S(2)}) collective-permute-start(bf16[768,384]{1,0:T(8,128)(2,1)} %add_convert_fusion.5), channel_id=1, source_target_pairs={{0,2},{2,0},{1,3},{3,1},{4,6},{6,4},{5,7},{7,5},{8,10},{10,8},{9,1... | collective-permute-start | bytes 1769480 | tf_op jit(solution)/shard_map/ppermute | solution.py:752
  187.0 15.7 %collective-permute-start.12 = (bf16[768,384]{1,0:T(8,128)(2,1)S(1)}, bf16[768,384]{1,0:T(8,128)(2,1)S(1)}, u32[]{:S(2)}, u32[]{:S(2)}) collective-permute-start(bf16[768,384]{1,0:T(8,128)(2,1)S(1)} %get-tuple-element.155.a_ref.refs_6_.refs_8_), channel_id=1, source_target_pairs={{0,2},{2,0},{1,3},{3,1},{4,6},{6,4},{5,7},{7,5},{8,10},{10,8},{9,1... | collective-permute-start | bytes 1769480 | tf_op jit(solution)/shard_map/ppermute | solution.py:752
  213.3 15.4 %collective-permute-start.17 = (bf16[768,384]{1,0:T(8,128)(2,1)S(1)}, bf16[768,384]{1,0:T(8,128)(2,1)S(1)}, u32[]{:S(2)}, u32[]{:S(2)}) collective-permute-start(bf16[768,384]{1,0:T(8,128)(2,1)S(1)} %add_convert_fusion.4), channel_id=1, source_target_pairs={{0,2},{2,0},{1,3},{3,1},{4,6},{6,4},{5,7},{7,5},{8,10},{10,8},{9,1... | collective-permute-start | bytes 1769480 | tf_op jit(solution)/shard_map/ppermute | solution.py:752
  233.9 19.5 %collective-permute-start.18 = (bf16[768,384]{1,0:T(8,128)(2,1)S(1)}, bf16[768,384]{1,0:T(8,128)(2,1)S(1)}, u32[]{:S(2)}, u32[]{:S(2)}) collective-permute-start(bf16[768,384]{1,0:T(8,128)(2,1)S(1)} %get-tuple-element.167.a_ref.refs_2_.refs_0_.second_ref), channel_id=1, source_target_pairs={{0,2},{2,0},{1,3},{3,1},{4,6},{6,4},{5,7},{7,5},{8,10},{10,8},{9,1... | collective-permute-start | bytes 1769480 | tf_op jit(solution)/shard_map/ppermute | solution.py:752
  235.8 46.6 %all-to-all-start.5 = ((bf16[16,304,128]{2,1,0:T(8,128)(2,1)}), bf16[16,304,128]{2,1,0:T(8,128)(2,1)S(1)}, u32[]{:S(2)}, u32[]{:S(2)}) async-start(bf16[16,304,128]{2,1,0:T(8,128)(2,1)} %shard_map.275), calls=%async_computation.5 | async-start | bytes 2490368 | tf_op jit(solution)/shard_map/all_to_all | solution.py:879
  239.7 163.8 %reduce-scatter.3.cloned.1.call-start = ((), (), s32[]{:S(2)}) async-start(), calls=%async_computation.14 | async-start | bytes 1474560 | tf_op jit(solution)/shard_map/reduce_scatter | solution.py:819
  264.2 18.2 %collective-permute-start.23 = (bf16[768,384]{1,0:T(8,128)(2,1)S(1)}, bf16[768,384]{1,0:T(8,128)(2,1)}, u32[]{:S(2)}, u32[]{:S(2)}) collective-permute-start(bf16[768,384]{1,0:T(8,128)(2,1)S(1)} %add_convert_fusion.3), channel_id=1, source_target_pairs={{0,2},{2,0},{1,3},{3,1},{4,6},{6,4},{5,7},{7,5},{8,10},{10,8},{9,1... | collective-permute-start | bytes 1769480 | tf_op jit(solution)/shard_map/ppermute | solution.py:752
  326.5 15.8 %collective-permute-start.24 = (bf16[768,384]{1,0:T(8,128)(2,1)S(1)}, bf16[768,384]{1,0:T(8,128)(2,1)S(1)}, u32[]{:S(2)}, u32[]{:S(2)}) collective-permute-start(bf16[768,384]{1,0:T(8,128)(2,1)S(1)} %get-tuple-element.195.a_ref.refs_2_.refs_0_.second_ref), channel_id=1, source_target_pairs={{0,2},{2,0},{1,3},{3,1},{4,6},{6,4},{5,7},{7,5},{8,10},{10,8},{9,1... | collective-permute-start | bytes 1769480 | tf_op jit(solution)/shard_map/ppermute | solution.py:752
  327.0 28.0 %collective-permute-start.31 = (bf16[768,768]{1,0:T(8,128)(2,1)S(1)}, bf16[768,768]{1,0:T(8,128)(2,1)S(1)}, u32[]{:S(2)}, u32[]{:S(2)}) collective-permute-start(bf16[768,768]{1,0:T(8,128)(2,1)S(1)} %copy-done.35), channel_id=1, source_target_pairs={{0,16},{16,0},{1,17},{17,1},{2,18},{18,2},{3,19},{19,3},{4,20},{20... | collective-permute-start | bytes 3538952 | tf_op jit(solution)/shard_map/ppermute | solution.py:752
  352.0 21.4 %collective-permute-start.26 = (bf16[768,384]{1,0:T(8,128)(2,1)}, bf16[768,384]{1,0:T(8,128)(2,1)}, u32[]{:S(2)}, u32[]{:S(2)}) collective-permute-start(bf16[768,384]{1,0:T(8,128)(2,1)} %get-tuple-element.202), channel_id=1, source_target_pairs={{0,1},{1,0},{2,3},{3,2},{4,5},{5,4},{6,7},{7,6},{8,9},{9,8},{10,11... | collective-permute-start | bytes 1769480 | tf_op jit(solution)/shard_map/ppermute | solution.py:752
  358.4 15.1 %collective-permute-start.29 = (bf16[768,384]{1,0:T(8,128)(2,1)}, bf16[768,384]{1,0:T(8,128)(2,1)S(1)}, u32[]{:S(2)}, u32[]{:S(2)}) collective-permute-start(bf16[768,384]{1,0:T(8,128)(2,1)} %add_convert_fusion.2), channel_id=1, source_target_pairs={{0,2},{2,0},{1,3},{3,1},{4,6},{6,4},{5,7},{7,5},{8,10},{10,8},{9,1... | collective-permute-start | bytes 1769480 | tf_op jit(solution)/shard_map/ppermute | solution.py:752
  373.5 27.4 %collective-permute-start.30 = (bf16[768,768]{1,0:T(8,128)(2,1)}, bf16[768,768]{1,0:T(8,128)(2,1)}, u32[]{:S(2)}, u32[]{:S(2)}) collective-permute-start(bf16[768,768]{1,0:T(8,128)(2,1)} %shard_map.282), channel_id=1, source_target_pairs={{0,16},{16,0},{1,17},{17,1},{2,18},{18,2},{3,19},{19,3},{4,20},{20... | collective-permute-start | bytes 3538952 | tf_op jit(solution)/shard_map/ppermute | solution.py:752
  380.8 22.7 %all-to-all-start.8 = ((bf16[8,304,128]{2,1,0:T(8,128)(2,1)}), bf16[8,304,128]{2,1,0:T(8,128)(2,1)S(1)}, u32[]{:S(2)}, u32[]{:S(2)}) async-start(bf16[8,304,128]{2,1,0:T(8,128)(2,1)} %shard_map.284), calls=%async_computation.8 | async-start | bytes 1245184 | tf_op jit(solution)/shard_map/all_to_all | solution.py:918
  403.5 14.8 %all-to-all-start.9 = ((bf16[16,48,384]{2,1,0:T(8,128)(2,1)}), bf16[16,48,384]{2,1,0:T(8,128)(2,1)S(1)}, u32[]{:S(2)}, u32[]{:S(2)}) async-start(bf16[16,48,384]{2,1,0:T(8,128)(2,1)} %bitcast.25), calls=%async_computation.10 | async-start | bytes 1179648 | tf_op jit(solution)/shard_map/all_to_all | solution.py:797
  407.1 41.3 %reduce-scatter.5.cloned.1.call-start = ((), (), s32[]{:S(2)}) async-start(), calls=%async_computation.15 | async-start | bytes 1474560 | tf_op jit(solution)/shard_map/reduce_scatter | solution.py:819
  423.3 22.7 %all-to-all-start.10 = ((bf16[16,48,384]{2,1,0:T(8,128)(2,1)}), bf16[16,48,384]{2,1,0:T(8,128)(2,1)S(1)}, u32[]{:S(2)}, u32[]{:S(2)}) async-start(bf16[16,48,384]{2,1,0:T(8,128)(2,1)} %shard_map.285), calls=%async_computation.11 | async-start | bytes 1179648 | tf_op jit(solution)/shard_map/all_to_all | solution.py:801
  427.0 91.8 %all-gather.3.cloned.1.call-start = ((), (), s32[]{:S(2)}) async-start(), calls=%async_computation.16 | async-start | bytes 2949120 | tf_op jit(solution)/shard_map/all_gather | solution.py:958
  496.7 14.1 %collective-permute-start.32 = (bf16[8,304,128]{2,1,0:T(8,128)(2,1)S(1)}, bf16[8,304,128]{2,1,0:T(8,128)(2,1)S(1)}, u32[]{:S(2)}, u32[]{:S(2)}) collective-permute-start(bf16[8,304,128]{2,1,0:T(8,128)(2,1)S(1)} %get-tuple-element.249), channel_id=1, source_target_pairs={{0,16},{16,0},{1,17},{17,1},{2,18},{18,2},{3,19},{19,3},{4,20},{20... | collective-permute-start | bytes 1867784 | tf_op jit(solution)/shard_map/ppermute | solution.py:752
  (69 other events, 376.4 us)
Sparse Core Ops, SparseCore 0:
  356.4 28.2 reduce-scatter.2
  410.8 36.5 reduce-scatter.4
  460.3 58.4 all-gather.2
